TPU v7x, 32 devices: a whole 2x2x4 slice. The times are simulated.
32 devices in a mesh: dp: 4 (over y, x), expert: 8 (over z, core).
Axes of the slice: x: 2, y: 2, z: 4, core: 2. Of those that a mesh axis runs over, the one named last changes fastest.
Arguments:
- layer_input: bfloat16 [4096, 640], P(('dp', 'expert')), may hold values from -6 to 6
- output_grad: bfloat16 [4096, 640], P(('dp', 'expert')), may hold values from -6 to 6
- gate_weights: float32 [4096, 2], P(('dp', 'expert')), may hold values from 0.1 to 1
- expert_ids: int32 [4096, 2], P(('dp', 'expert')), may hold values from 0 to 7, as said below
- slot_positions: int32 [4096, 2], P(('dp', 'expert')), may hold values from 0 to 23, as said below
- keep_mask: int32 [4096, 2], P(('dp', 'expert')), may hold values from 0 to 1, as said below
- weight_in: bfloat16 [8, 640, 5120], P('expert', None, 'dp'), may hold values from -0.25 to 0.25
- weight_out: bfloat16 [8, 5120, 640], P('expert', 'dp'), may hold values from -0.078125 to 0.078125
Outputs:
- input_grad: bfloat16 [4096, 640], P(('dp', 'expert'))
- weight_in_grad: bfloat16 [8, 640, 5120], P('expert', None, 'dp')
- weight_out_grad: bfloat16 [8, 5120, 640], P('expert', 'dp')
Inputs may be any that keep to these rules, and one draw needn't show every extreme that they name: `expert_ids`: a token's two experts differ. `slot_positions`: within the tokens of one device, taken in order with a token's first choice before its second, the choices naming one expert take positions 0, 1, 2 and so on; a choice at position 24 or beyond is dropped and has slot 0; kept choices of one device and expert have distinct slots. `keep_mask`: 1 exactly where the choice's position is below 24.
All inputs are finite; a program needn't handle non-finite values.
Results may differ from a plain program's by a relative error of at most 0.015.
Values may be sent and summed in bfloat16 or wider, within the bound.
No kernel may reach another device: no remote copies, remote signals or barrier semaphores. Data moves between devices by JAX's collectives and lax.ppermute only.
A program may use at most 64 MiB of HBM per device.

v0:
```python
import jax
import jax.numpy as jnp
from jax import lax
from jax.sharding import PartitionSpec as P

root_coef = 0.7978845608028654
cube_coef = 0.044715


def gelu_value(preact):
    inner_arg = root_coef * (preact + cube_coef * preact * preact * preact)
    return 0.5 * preact * (1.0 + jnp.tanh(inner_arg))


def gelu_slope(preact):
    inner_arg = root_coef * (preact + cube_coef * preact * preact * preact)
    tanh_value = jnp.tanh(inner_arg)
    return 0.5 * (1.0 + tanh_value) + 0.5 * preact * (1.0 - tanh_value * tanh_value) * root_coef * (
        1.0 + 3.0 * cube_coef * preact * preact
    )


def expert_grads(pieces, weight_in, weight_out, local_experts):
    piece_in, piece_cot = pieces
    groups, owners, merged_slots, feature_width = piece_in.shape
    slot_cap = merged_slots // local_experts
    rows_in = piece_in.reshape(groups, owners, local_experts, slot_cap, feature_width)
    rows_cot = piece_cot.reshape(groups, owners, local_experts, slot_cap, feature_width)
    preact = jnp.einsum("gjlcd,ldf->gjlcf", rows_in, weight_in, preferred_element_type=jnp.float32)
    hidden = gelu_value(preact).astype(jnp.bfloat16)
    backprop = jnp.einsum(
        "gjlcd,lfd->gjlcf", rows_cot, weight_out, preferred_element_type=jnp.float32
    )
    grad_pre = (gelu_slope(preact) * backprop).astype(jnp.bfloat16)
    total_in = jnp.einsum("gjlcd,gjlcf->ldf", rows_in, grad_pre, preferred_element_type=jnp.float32)
    total_out = jnp.einsum("gjlcf,gjlcd->lfd", hidden, rows_cot, preferred_element_type=jnp.float32)
    return (total_in, total_out, grad_pre)


def body(
    layer_input,
    output_grad,
    gate_weights,
    expert_ids,
    slot_positions,
    keep_mask,
    weight_in,
    weight_out,
):
    token_count, feature_width = layer_input.shape
    owner_count = lax.axis_size("expert")
    local_experts = weight_in.shape[0]
    expert_total = local_experts * owner_count
    slot_cap = 3 * token_count // (2 * expert_total)
    bucket_total = expert_total * slot_cap
    target = (expert_ids * slot_cap + slot_positions).reshape(-1)
    kept_rows = keep_mask.reshape(-1) > 0
    columns = lax.broadcasted_iota(jnp.int32, (2 * token_count, bucket_total), 1)
    selector = ((columns == target[:, None]) & kept_rows[:, None]).astype(jnp.bfloat16)
    repeated_input = jnp.repeat(layer_input, 2, axis=0)
    scaled = (
        gate_weights.reshape(-1, 1) * jnp.repeat(output_grad, 2, axis=0).astype(jnp.float32)
    ).astype(jnp.bfloat16)
    send_input = jnp.einsum(
        "rb,rd->bd", selector, repeated_input, preferred_element_type=jnp.float32
    ).astype(jnp.bfloat16)
    send_cotan = jnp.einsum(
        "rb,rd->bd", selector, scaled, preferred_element_type=jnp.float32
    ).astype(jnp.bfloat16)
    send_input = send_input.reshape(owner_count, local_experts * slot_cap, feature_width)
    send_cotan = send_cotan.reshape(owner_count, local_experts * slot_cap, feature_width)
    arrived_input, arrived_cotan = (
        lax.all_to_all(send_input, "expert", split_axis=0, concat_axis=0, tiled=True),
        lax.all_to_all(send_cotan, "expert", split_axis=0, concat_axis=0, tiled=True),
    )
    total_in, total_out, grad_all = expert_grads(
        (
            lax.all_gather(arrived_input[None], "dp", axis=0, tiled=True),
            lax.all_gather(arrived_cotan[None], "dp", axis=0, tiled=True),
        ),
        weight_in,
        weight_out,
        local_experts,
    )
    partial_value = jnp.einsum(
        "gjlcf,ldf->gjlcd", grad_all, weight_in, preferred_element_type=jnp.float32
    ).astype(jnp.bfloat16)
    moved = lax.all_to_all(
        lax.all_to_all(partial_value, "dp", split_axis=0, concat_axis=0, tiled=True),
        "expert",
        split_axis=1,
        concat_axis=1,
        tiled=True,
    )
    back_rows = (
        jnp.sum(moved.astype(jnp.float32), axis=0)
        .astype(jnp.bfloat16)
        .reshape(bucket_total, feature_width)
    )
    picked = jnp.einsum(
        "rb,bd->rd", selector, back_rows, preferred_element_type=jnp.float32
    ).reshape(token_count, 2, feature_width)
    input_grad = jnp.sum(picked, axis=1).astype(jnp.bfloat16)
    return (input_grad, total_in.astype(jnp.bfloat16), total_out.astype(jnp.bfloat16))


def solution(mesh):
    in_specs = (
        P(("dp", "expert"), None),
        P(("dp", "expert"), None),
        P(("dp", "expert"), None),
        P(("dp", "expert"), None),
        P(("dp", "expert"), None),
        P(("dp", "expert"), None),
        P("expert", None, "dp"),
        P("expert", "dp", None),
    )
    out_specs = (P(("dp", "expert"), None), P("expert", None, "dp"), P("expert", "dp", None))
    return jax.shard_map(body, mesh=mesh, in_specs=in_specs, out_specs=out_specs, check_vma=False)
```

profile of v0, /device:TPU:0, one launch (start us, length us, event | category | flops | bytes accessed | tf_op | source)
XLA Modules:
  0.0 107.8 jit_solution(3134780922986654777)
XLA Ops:
  0.6 0.0 copy-start
  0.6 0.8 broadcast_compare_fusion
  1.5 0.1 copy.15
  1.6 0.1 gt.16
  1.7 0.7 multiply_add_fusion.1
  2.4 0.1 copy.14
  2.6 0.1 eq.30
  2.7 1.1 %broadcast_in_dim.13 = bf16[128,2,640]{2,1,0:T(2,128)(2,1)S(1)} broadcast(bf16[128,640]{1,0:T(8,128)(2,1)} %param.8), dimensions={0,2} | broadcast | bytes 491520 | tf_op jit(solution)/shard_map/broadcast_in_dim | solution.py:60
  3.8 0.1 reshape.95
  3.9 1.1 %convolution_convert_fusion.1 = bf16[192,640]{1,0:T(8,128)(2,1)} fusion(bf16[256,640]{1,0:T(8,128)(2,1)S(1)} %reshape.95, s32[256]{0:T(256)S(1)} %eq.30, pred[256]{0:T(512)(128)(4,1)S(1)} %gt.16), kind=kOutput, calls=%fused_computation.31 | convolution fusion | flops 63135744 | bytes 574720 | tf_op jit(solution)/shard_map/rb,rd->bd/dot_general | solution.py:64
  5.0 6.3 %all-to-all-start = ((bf16[8,24,640]{2,1,0:T(8,128)(2,1)}), bf16[8,24,640]{2,1,0:T(8,128)(2,1)S(1)}, u32[]{:S(2)}, u32[]{:S(2)}) async-start(bf16[8,24,640]{2,1,0:T(8,128)(2,1)} %bitcast.1), calls=%async_computation | async-start | bytes 491520 | tf_op jit(solution)/shard_map/all_to_all | solution.py:73
  11.3 0.8 copy.16
  12.1 0.1 mul.81
  12.3 1.1 %broadcast_in_dim.15 = f32[128,2,640]{2,1,0:T(2,128)S(1)} broadcast(bf16[128,640]{1,0:T(8,128)(2,1)} %param.9), dimensions={0,2} | broadcast | bytes 819200 | tf_op jit(solution)/shard_map/broadcast_in_dim | solution.py:62
  13.4 0.5 convert_element_type.54
  13.8 1.1 %convolution_convert_fusion = bf16[192,640]{1,0:T(8,128)(2,1)} fusion(f32[256,640]{1,0:T(8,128)S(1)} %convert_element_type.54, f32[256]{0:T(256)S(1)} %mul.81, s32[256]{0:T(256)S(1)} %eq.30, pred[256]{0:T(512)(128)(4,1)S(1)} %gt.16), kind=kOutput, calls=%fused_computation.30 | convolution fusion | flops 63463424 | bytes 903424 | tf_op jit(solution)/shard_map/rb,rd->bd/dot_general | solution.py:67
  14.9 5.8 %all-to-all-done = bf16[8,24,640]{2,1,0:T(8,128)(2,1)S(1)} async-done(((bf16[8,24,640]{2,1,0:T(8,128)(2,1)}), bf16[8,24,640]{2,1,0:T(8,128)(2,1)S(1)}, u32[]{:S(2)}, u32[]{:S(2)}) %all-to-all-start) | async-done | bytes 245792 | tf_op jit(solution)/shard_map/all_to_all | solution.py:73
  20.7 3.4 %all-to-all-start.1 = ((bf16[8,24,640]{2,1,0:T(8,128)(2,1)}), bf16[8,24,640]{2,1,0:T(8,128)(2,1)S(1)}, u32[]{:S(2)}, u32[]{:S(2)}) async-start(bf16[8,24,640]{2,1,0:T(8,128)(2,1)} %bitcast.11), calls=%async_computation.1 | async-start | bytes 491520 | tf_op jit(solution)/shard_map/all_to_all | solution.py:74
  24.1 14.1 %all-gather = bf16[32,24,640]{2,1,0:T(8,128)(2,1)S(1)} all-gather(bf16[8,24,640]{2,1,0:T(8,128)(2,1)S(1)} %all-to-all-done), channel_id=2, replica_groups=mesh['dp'=4,'expert'=8] {'dp'}, dimensions={0}, use_global_device_ids=true | all-gather | bytes 1228800 | tf_op jit(solution)/shard_map/all_gather | solution.py:78
  38.3 0.0 copy-start.1
  38.3 0.9 copy-done.1
  39.2 0.0 copy-done
  39.2 3.6 %fusion.19 = f32[4,8,24,1280]{3,2,1,0:T(8,128)} fusion(bf16[4,8,24,640]{3,2,1,0:T(8,128)(2,1)S(1)} %bitcast.104, bf16[1,640,1280]{2,1,0:T(8,128)(2,1)S(1)} %copy-done), kind=kOutput, calls=%fused_computation.25 | convolution fusion | flops 1258291200 | bytes 6553600 | tf_op jit(solution)/shard_map/gjlcd,ldf->gjlcf/dot_general | solution.py:29
  42.8 0.0 all-to-all-done.1
  42.8 12.7 %all-gather.1 = bf16[32,24,640]{2,1,0:T(8,128)(2,1)S(1)} all-gather(bf16[8,24,640]{2,1,0:T(8,128)(2,1)S(1)} %all-to-all-done.1), channel_id=3, replica_groups=mesh['dp'=4,'expert'=8] {'dp'}, dimensions={0}, use_global_device_ids=true | all-gather | bytes 1228800 | tf_op jit(solution)/shard_map/all_gather | solution.py:79
  55.5 0.0 copy-start.2
  55.5 5.5 %fusion.9 = bf16[4,8,24,1280]{3,2,1,0:T(8,128)(2,1)S(1)} fusion(bf16[4,8,24,640]{3,2,1,0:T(8,128)(2,1)S(1)} %bitcast.106, f32[4,8,24,1280]{3,2,1,0:T(8,128)} %fusion.19, bf16[1,1280,640]{2,1,0:T(8,128)(2,1)} %param.15), kind=kOutput, calls=%fused_computation.15 | convolution fusion | flops 1276968960 | bytes 8519680 | tf_op jit(solution)/shard_map/gjlcd,lfd->gjlcf/dot_general | solution.py:31
  61.1 0.0 copy-done.2
  61.1 0.0 copy-start.5
  61.1 1.8 %fusion.24 = bf16[4,8,1,24,640]{4,3,1,2,0:T(8,128)(2,1)S(1)} fusion(bf16[4,8,24,1280]{3,2,1,0:T(8,128)(2,1)S(1)} %fusion.9, bf16[1,640,1280]{2,1,0:T(8,128)(2,1)S(1)} %copy-done), kind=kOutput, calls=%fused_computation.28 | convolution fusion | flops 1258782720 | bytes 4587520 | tf_op jit(solution)/shard_map/gjlcf,ldf->gjlcd/dot_general | solution.py:85
  62.9 0.0 copy-done.5
  62.9 13.1 %all_to_all.20 = bf16[4,8,1,24,640]{4,3,1,2,0:T(8,128)(2,1)S(1)} all-to-all(bf16[4,8,1,24,640]{4,3,1,2,0:T(8,128)(2,1)S(1)} %fusion.24), channel_id=1, replica_groups=mesh['dp'=4,'expert'=8] {'dp'}, dimensions={0} | all-to-all | bytes 1966080 | tf_op jit(solution)/shard_map/all_to_all | solution.py:89
  76.0 1.1 copy.18
  77.0 4.4 %all-to-all-start.3 = ((bf16[4,8,1,24,640]{4,3,0,2,1:T(8,128)(2,1)}), bf16[4,8,1,24,640]{4,3,0,2,1:T(8,128)(2,1)S(1)}, u32[]{:S(2)}, u32[]{:S(2)}) async-start(bf16[4,8,1,24,640]{4,3,0,2,1:T(8,128)(2,1)} %copy.18), calls=%async_computation.3 | async-start | bytes 1966080 | tf_op jit(solution)/shard_map/all_to_all | solution.py:88
  81.4 0.0 copy-start.3
  81.5 0.0 copy-start.4
  81.5 4.6 %fusion.11 = bf16[1,640,1280]{2,1,0:T(8,128)(2,1)} fusion(bf16[4,8,24,640]{3,2,1,0:T(8,128)(2,1)} %bitcast.105, bf16[4,8,24,1280]{3,2,1,0:T(8,128)(2,1)} %copy-done.5), kind=kOutput, calls=%fused_computation.17 | convolution fusion | flops 1259110400 | bytes 4587520 | tf_op jit(solution)/shard_map/gjlcd,gjlcf->ldf/dot_general | solution.py:35
  86.1 0.0 copy-done.3
  86.1 0.0 copy-done.4
  86.1 3.4 %fusion.10 = bf16[1,1280,640]{2,1,0:T(8,128)(2,1)} fusion(bf16[4,8,24,640]{3,2,1,0:T(8,128)(2,1)S(1)} %bitcast.107, f32[4,8,24,1280]{3,2,1,0:T(8,128)S(1)} %copy-done.4), kind=kOutput, calls=%fused_computation.16 | convolution fusion | flops 1267957760 | bytes 6553600 | tf_op jit(solution)/shard_map/gjlcf,gjlcd->lfd/dot_general | solution.py:36
  89.5 17.2 %all-to-all-done.3 = bf16[4,8,1,24,640]{4,3,0,2,1:T(8,128)(2,1)S(1)} async-done(((bf16[4,8,1,24,640]{4,3,0,2,1:T(8,128)(2,1)}), bf16[4,8,1,24,640]{4,3,0,2,1:T(8,128)(2,1)S(1)}, u32[]{:S(2)}, u32[]{:S(2)}) %all-to-all-start.3) | async-done | bytes 983072 | tf_op jit(solution)/shard_map/all_to_all | solution.py:88
  106.6 0.2 reduce_sum.21
  106.8 1.0 convolution_reduce_fusion
Async XLA Ops:
  0.6 38.6 %copy-start = (bf16[1,640,1280]{2,1,0:T(8,128)(2,1)S(1)}, bf16[1,640,1280]{2,1,0:T(8,128)(2,1)}, u32[]{:S(2)}) copy-start(bf16[1,640,1280]{2,1,0:T(8,128)(2,1)} %param.14) | copy-start | bytes 4915204
  5.0 15.7 %all-to-all-start = ((bf16[8,24,640]{2,1,0:T(8,128)(2,1)}), bf16[8,24,640]{2,1,0:T(8,128)(2,1)S(1)}, u32[]{:S(2)}, u32[]{:S(2)}) async-start(bf16[8,24,640]{2,1,0:T(8,128)(2,1)} %bitcast.1), calls=%async_computation | async-start | bytes 491520 | tf_op jit(solution)/shard_map/all_to_all | solution.py:73
  20.7 22.1 %all-to-all-start.1 = ((bf16[8,24,640]{2,1,0:T(8,128)(2,1)}), bf16[8,24,640]{2,1,0:T(8,128)(2,1)S(1)}, u32[]{:S(2)}, u32[]{:S(2)}) async-start(bf16[8,24,640]{2,1,0:T(8,128)(2,1)} %bitcast.11), calls=%async_computation.1 | async-start | bytes 491520 | tf_op jit(solution)/shard_map/all_to_all | solution.py:74
  38.3 0.9 copy-start.1
  55.5 5.5 %copy-start.2 = (bf16[32,24,640]{2,1,0:T(8,128)(2,1)}, bf16[32,24,640]{2,1,0:T(8,128)(2,1)S(1)}, u32[]{:S(2)}) copy-start(bf16[32,24,640]{2,1,0:T(8,128)(2,1)S(1)} %all-gather.1) | copy-start | bytes 2949124
  61.1 1.8 %copy-start.5 = (bf16[4,8,24,1280]{3,2,1,0:T(8,128)(2,1)}, bf16[4,8,24,1280]{3,2,1,0:T(8,128)(2,1)S(1)}, u32[]{:S(2)}) copy-start(bf16[4,8,24,1280]{3,2,1,0:T(8,128)(2,1)S(1)} %fusion.9) | copy-start | bytes 5898244
  77.0 29.6 %all-to-all-start.3 = ((bf16[4,8,1,24,640]{4,3,0,2,1:T(8,128)(2,1)}), bf16[4,8,1,24,640]{4,3,0,2,1:T(8,128)(2,1)S(1)}, u32[]{:S(2)}, u32[]{:S(2)}) async-start(bf16[4,8,1,24,640]{4,3,0,2,1:T(8,128)(2,1)} %copy.18), calls=%async_computation.3 | async-start | bytes 1966080 | tf_op jit(solution)/shard_map/all_to_all | solution.py:88
  81.4 4.6 %copy-start.3 = (bf16[32,24,640]{2,1,0:T(8,128)(2,1)S(1)}, bf16[32,24,640]{2,1,0:T(8,128)(2,1)}, u32[]{:S(2)}) copy-start(bf16[32,24,640]{2,1,0:T(8,128)(2,1)} %copy-done.2) | copy-start | bytes 2949124
  81.5 4.6 %copy-start.4 = (f32[4,8,24,1280]{3,2,1,0:T(8,128)S(1)}, f32[4,8,24,1280]{3,2,1,0:T(8,128)}, u32[]{:S(2)}) copy-start(f32[4,8,24,1280]{3,2,1,0:T(8,128)} %fusion.19) | copy-start | bytes 11796484
where the time goes:
time: 108 us
  blocking collectives  39.9 us (37%)
  waiting for transfers between devices  23 us (21%)
  matrix products  22.1 us (20%)
  starting transfers between devices  14.2 us (13%)
  local copies, waits for them, and re-layouts  6.25 us (6%)
  other arithmetic  1.69 us (2%)
    all_to_all x1, waiting for transfers between devices, body(): lax.all_to_all(lax.all_to_all(partial_value, 'dp', split_axis=0, concat_a...  17.2 us
    all_gather x1, blocking collectives, body(): lax.all_gather(arrived_input[None], 'dp', axis=0, tiled=True)  14.1 us
    all_to_all x1, blocking collectives, body(): lax.all_to_all(partial_value, 'dp', split_axis=0, concat_axis=0, tiled=True)  13.1 us
    all_gather x1, blocking collectives, body(): lax.all_gather(arrived_cotan[None], 'dp', axis=0, tiled=True)  12.7 us
    all_to_all x1, starting transfers between devices, body(): lax.all_to_all(send_input, 'expert', split_axis=0, concat_axis=0, tiled=T...  6.33 us
    all_to_all x1, waiting for transfers between devices, body(): lax.all_to_all(send_input, 'expert', split_axis=0, concat_axis=0, tiled=T...  5.81 us
    dot_general x1, matrix products, expert_grads(): jnp.einsum('gjlcd,lfd->gjlcf', rows_cot, weight_out, preferred_element_ty...  5.52 us
    dot_general x1, matrix products, expert_grads(): jnp.einsum('gjlcd,gjlcf->ldf', rows_in, grad_pre, preferred_element_type=...  4.63 us
  transfers between devices with their start and end apart: 3, of which 2 were waited for; matrix products, arithmetic and copies ran while one was open for 14% of the time, Pallas kernels for 0%

commit v1 on v0

v1 whole, which is shorter than its diff:
```python
import functools

import jax
import jax.numpy as jnp
from jax import lax
from jax.experimental import pallas as pl
from jax.experimental.pallas import tpu as pltpu
from jax.sharding import PartitionSpec as P

root_coef = 0.7978845608028654
cube_coef = 0.044715
vmem_whole = pl.BlockSpec(memory_space=pltpu.VMEM)
f32 = jnp.float32
bf16 = jnp.bfloat16


def vmem_out(shape, dtype=bf16):
    return pltpu.VMEM(shape, dtype)


def params(mib):
    return pltpu.CompilerParams(vmem_limit_bytes=mib * 1024 * 1024)


def cost(flops, moved, trans=0):
    return pl.CostEstimate(flops=flops, bytes_accessed=moved, transcendentals=trans)


def selector_columns(ids, slots, keep, me, slot_cap, half):
    relative = ids ^ me
    column = (relative & 1) * half + (relative >> 1) * slot_cap + slots
    return jnp.where(keep > 0, column, -1)


def dispatch_kernel(slot_cap, tokens_ref, grads_ref, gate_ref, ids_ref, slots_ref, keep_ref, own_ref, other_ref):
    half = own_ref.shape[0]
    token_count, width = tokens_ref.shape
    me = lax.axis_index("expert")
    column = selector_columns(ids_ref[...], slots_ref[...], keep_ref[...], me, slot_cap, half)
    gate = gate_ref[...]
    for base, out_ref in ((half, other_ref), (0, own_ref)):
        rows = lax.broadcasted_iota(jnp.int32, (half, token_count), 0) + base
        first, second = rows == column[0:1], rows == column[1:2]
        picked = (first | second).astype(f32).astype(bf16)
        scale = jnp.sum(
            jnp.where(first, gate[0:1], 0.0) + jnp.where(second, gate[1:2], 0.0), axis=1, keepdims=True
        )
        out_ref[:, :width] = jnp.dot(picked, tokens_ref[...], preferred_element_type=f32).astype(bf16)
        row_grad = jnp.dot(picked, grads_ref[...], preferred_element_type=f32)
        out_ref[:, width:] = (scale * row_grad).astype(bf16)


def combine_kernel(slot_cap, own_ref, other_ref, ids_ref, slots_ref, keep_ref, out_ref):
    half = own_ref.shape[0]
    token_count = out_ref.shape[0]
    me = lax.axis_index("expert")
    column = selector_columns(ids_ref[...], slots_ref[...], keep_ref[...], me, slot_cap, half)
    total = jnp.zeros(out_ref.shape, f32)
    for base, rows_ref in ((0, own_ref), (half, other_ref)):
        rows = lax.broadcasted_iota(jnp.int32, (half, token_count), 0) + base
        picked = ((rows == column[0:1]) | (rows == column[1:2])).astype(f32).astype(bf16)
        total += lax.dot_general(picked, rows_ref[...], (((0,), (0,)), ((), ())), preferred_element_type=f32)
    out_ref[...] = total.astype(bf16)


def chunk_kernel(n_pieces, tile, *refs):
    pieces = refs[:n_pieces]
    win_ref, wout_ref = refs[n_pieces : n_pieces + 2]
    parts = refs[n_pieces + 2 : 2 * n_pieces + 2]
    rows_ref, hidden_ref, pre_ref, acc_ref = refs[2 * n_pieces + 2 :]
    width = win_ref.shape[0]
    hidden_total = win_ref.shape[1]
    start = 0
    spans = []
    for ref in pieces:
        count = ref.shape[0]
        rows_ref[start : start + count, :] = ref[...]
        spans.append((start, start + count))
        start += count
    for base in range(0, hidden_total, tile):
        cols = slice(base, base + tile)
        preact = jnp.dot(rows_ref[:, :width], win_ref[:, cols], preferred_element_type=f32)
        backprop = lax.dot_general(
            rows_ref[:, width:], wout_ref[cols, :], (((1,), (1,)), ((), ())), preferred_element_type=f32
        )
        square = preact * preact
        tanh_value = jnp.tanh(root_coef * (preact + cube_coef * preact * square))
        one_plus = 0.5 * (1.0 + tanh_value)
        hidden_ref[:, cols] = (preact * one_plus).astype(bf16)
        slope = one_plus + 0.5 * preact * (1.0 - tanh_value * tanh_value) * (
            root_coef + (3.0 * cube_coef * root_coef) * square
        )
        grad_pre = (slope * backprop).astype(bf16)
        pre_ref[:, cols] = grad_pre
        term = lax.dot_general(
            grad_pre, win_ref[:, cols], (((1,), (1,)), ((), ())), preferred_element_type=f32
        )
        if base == 0:
            acc_ref[...] = term
        else:
            acc_ref[...] += term
    for (low, high), ref in zip(spans, parts, strict=True):
        ref[...] = acc_ref[low:high, :].astype(bf16)


def weight_in_kernel(count, width, *refs):
    total = None
    for rows_ref, pre_ref in zip(refs[:count], refs[count : 2 * count], strict=True):
        term = lax.dot_general(
            rows_ref[:, :width], pre_ref[...], (((0,), (0,)), ((), ())), preferred_element_type=f32
        )
        total = term if total is None else total + term
    refs[-1][...] = total.astype(bf16)


def weight_out_kernel(count, width, *refs):
    total = None
    for rows_ref, hidden_ref in zip(refs[:count], refs[count : 2 * count], strict=True):
        term = lax.dot_general(
            hidden_ref[...], rows_ref[:, width:], (((0,), (0,)), ((), ())), preferred_element_type=f32
        )
        total = term if total is None else total + term
    refs[-1][...] = total.astype(bf16)


def swap(value, axis, offset):
    size = lax.axis_size(axis)
    return lax.ppermute(value, axis, [(i, i ^ offset) for i in range(size)])


def body(
    layer_input,
    output_grad,
    gate_weights,
    expert_ids,
    slot_positions,
    keep_mask,
    weight_in,
    weight_out,
):
    token_count, width = layer_input.shape
    owners = lax.axis_size("expert")
    groups = lax.axis_size("dp")
    slot_cap = 3 * token_count // (2 * owners)
    chips = owners // 2
    half = chips * slot_cap
    block = 2 * slot_cap
    gate, ids, slots, keep = gate_weights.T, expert_ids.T, slot_positions.T, keep_mask.T
    win, wout = weight_in[0], weight_out[0]
    hidden_total = win.shape[1]

    own, other = pl.pallas_call(
        functools.partial(dispatch_kernel, slot_cap),
        out_shape=(vmem_out((half, 2 * width)),) * 2,
        in_specs=[vmem_whole] * 6,
        out_specs=(vmem_whole,) * 2,
        compiler_params=params(16),
        name="dispatch",
    )(layer_input, output_grad, gate, ids, slots, keep)
    got = swap(other, "expert", 1)

    arrived = []
    for m in range(chips):
        span = slice(m * slot_cap, (m + 1) * slot_cap)
        rows = jnp.concatenate([own[span], got[span]], axis=0)
        arrived.append(rows if m == 0 else swap(rows, "expert", 2 * m))

    chunk_count = 2
    per_chunk = chips // chunk_count
    chunks = [list(range(c * per_chunk, (c + 1) * per_chunk)) for c in range(chunk_count)]
    returned = [None] * chips
    all_rows, all_hidden, all_pre = [], [], []
    for chunk in chunks:
        mine = jnp.concatenate([arrived[m] for m in chunk], axis=0)
        count = mine.shape[0]
        pieces = [mine] + [swap(mine, "dp", o) for o in range(1, groups)]
        total = groups * count
        outs = pl.pallas_call(
            functools.partial(chunk_kernel, groups, 256),
            out_shape=(vmem_out((count, width)),) * groups
            + (vmem_out((total, 2 * width)), vmem_out((total, hidden_total)), vmem_out((total, hidden_total))),
            in_specs=[vmem_whole] * (groups + 2),
            out_specs=(vmem_whole,) * (groups + 3),
            scratch_shapes=[pltpu.VMEM((total, width), f32)],
            compiler_params=params(32),
            cost_estimate=cost(6 * total * width * hidden_total, 4 * width * hidden_total, total * hidden_total),
            name="chunk",
        )(*pieces, win, wout)
        parts = outs[:groups]
        all_rows.append(outs[groups])
        all_hidden.append(outs[groups + 1])
        all_pre.append(outs[groups + 2])
        summed = parts[0].astype(f32)
        for o in range(1, groups):
            summed = summed + swap(parts[o], "dp", o).astype(f32)
        summed = summed.astype(bf16)
        for i, m in enumerate(chunk):
            piece = summed[i * block : (i + 1) * block]
            returned[m] = piece if m == 0 else swap(piece, "expert", 2 * m)

    weight_call = dict(
        in_specs=[vmem_whole] * (2 * chunk_count),
        out_specs=vmem_whole,
        compiler_params=params(40),
        cost_estimate=cost(2 * block * chips * groups * width * hidden_total, 2 * width * hidden_total),
    )
    grad_in = pl.pallas_call(
        functools.partial(weight_in_kernel, chunk_count, width),
        out_shape=jax.ShapeDtypeStruct((width, hidden_total), bf16),
        name="weight_in_grad",
        **weight_call,
    )(*all_rows, *all_pre)
    grad_out = pl.pallas_call(
        functools.partial(weight_out_kernel, chunk_count, width),
        out_shape=jax.ShapeDtypeStruct((hidden_total, width), bf16),
        name="weight_out_grad",
        **weight_call,
    )(*all_rows, *all_hidden)

    for_partner = jnp.concatenate([r[slot_cap:] for r in returned], axis=0)
    back_other = swap(for_partner, "expert", 1)
    back_own = jnp.concatenate([r[:slot_cap] for r in returned], axis=0)
    input_grad = pl.pallas_call(
        functools.partial(combine_kernel, slot_cap),
        out_shape=jax.ShapeDtypeStruct((token_count, width), bf16),
        in_specs=[vmem_whole] * 5,
        out_specs=vmem_whole,
        compiler_params=params(16),
        name="combine",
    )(back_own, back_other, ids, slots, keep)
    return (input_grad, grad_in[None], grad_out[None])


def solution(mesh):
    tokens = P(("dp", "expert"), None)
    in_specs = (tokens,) * 6 + (P("expert", None, "dp"), P("expert", "dp", None))
    out_specs = (tokens, P("expert", None, "dp"), P("expert", "dp", None))
    return jax.shard_map(body, mesh=mesh, in_specs=in_specs, out_specs=out_specs, check_vma=False)
```

time: 108 us -> 68.8 us (0.64)
  blocking collectives: 39.9 us -> 0 us
  matrix products: 22.1 us -> 0 us
  Pallas kernels: 0 us -> 14.7 us
  starting transfers between devices: 14.2 us -> 27.6 us
  waiting for transfers between devices: 23 us -> 19.1 us
  other arithmetic: 1.69 us -> 0.21 us
    ppermute x0 -> x20, starting transfers between devices: none -> 27.6 us  [swap(): return lax.ppermute(value, axis, [(i, i ^ offset) for i in range(size)])]
    all_gather x2 -> x0, blocking collectives: 26.9 us -> none  [the longest x1 14.1 us: body(): lax.all_gather(arrived_input[None], 'dp', axis=0, tiled=True)]
    all_to_all x3 -> x0, waiting for transfers between devices: 23 us -> none  [the longest x1 17.2 us: body(): lax.all_to_all(lax.all_to_all(partial_value, 'dp', split_axis=0, concat_a...]
    dot_general x8 -> x0, matrix products: 22.1 us -> none  [the longest x1 5.52 us: expert_grads(): jnp.einsum('gjlcd,lfd->gjlcf', rows_cot, weight_out, preferred_element_ty...]
    ppermute x0 -> x20, waiting for transfers between devices: none -> 19.1 us  [swap(): return lax.ppermute(value, axis, [(i, i ^ offset) for i in range(size)])]
    pallas_call x0 -> x6, Pallas kernels: none -> 14.7 us  [the longest x2 7.11 us: body(): pl.pallas_call(functools.partial(chunk_kernel, groups, 256), out_shape=(v...]
    all_to_all x3 -> x0, starting transfers between devices: 14.2 us -> none  [the longest x1 6.33 us: body(): lax.all_to_all(send_input, 'expert', split_axis=0, concat_axis=0, tiled=T...]
    all_to_all x1 -> x0, blocking collectives: 13.1 us -> none  [body(): lax.all_to_all(partial_value, 'dp', split_axis=0, concat_axis=0, tiled=True)]
  transfers between devices with their start and end apart: 3 -> 20, of which waited for: 2 -> 6; matrix products, arithmetic and copies ran while one was open for 14% -> 0% of each run, Pallas kernels for 0% -> 20%
where the time goes in v1:
time: 68.8 us; the launch traced here: 68.6 us
  starting transfers between devices  27.6 us (40%)
  waiting for transfers between devices  19.1 us (28%)
  Pallas kernels  14.7 us (21%)
  local copies, waits for them, and re-layouts  6.1 us (9%)
  between operations  0.86 us (1%)
    ppermute x20, starting transfers between devices, swap(): return lax.ppermute(value, axis, [(i, i ^ offset) for i in range(size)])  27.6 us
    ppermute x20, waiting for transfers between devices, swap(): return lax.ppermute(value, axis, [(i, i ^ offset) for i in range(size)])  19.1 us
    pallas_call x2, Pallas kernels, body(): pl.pallas_call(functools.partial(chunk_kernel, groups, 256), out_shape=(v...  7.11 us
    unnamed x25, local copies, waits for them, and re-layouts  6 us
    pallas_call x1, Pallas kernels, body(): pl.pallas_call(functools.partial(weight_out_kernel, chunk_count, width),...  3.24 us
    pallas_call x1, Pallas kernels, body(): pl.pallas_call(functools.partial(weight_in_kernel, chunk_count, width), o...  3.07 us
  transfers between devices with their start and end apart: 20, of which 6 were waited for; matrix products, arithmetic and copies ran while one was open for 0% of the time, Pallas kernels for 20%

profile of v1, /device:TPU:0, one launch (start us, length us, event | category | flops | bytes accessed | tf_op | source)
XLA Modules:
  0.0 68.6 jit_solution(6860044631286913007)
XLA Ops:
  0.6 0.0 copy-start
  0.6 0.9 %copy-done = bf16[128,640]{1,0:T(8,128)(2,1)S(1)} copy-done((bf16[128,640]{1,0:T(8,128)(2,1)S(1)}, bf16[128,640]{1,0:T(8,128)(2,1)}, u32[]{:S(2)}) %copy-start) | copy-done | bytes 163864
  1.6 0.9 %copy-done.1 = bf16[128,640]{1,0:T(8,128)(2,1)S(1)} copy-done((bf16[128,640]{1,0:T(8,128)(2,1)S(1)}, bf16[128,640]{1,0:T(8,128)(2,1)}, u32[]{:S(2)}) %copy-start.1) | copy-done | bytes 163864
  2.5 0.7 copy-done.2
  3.1 0.7 copy-done.4
  3.8 0.7 copy-done.6
  4.5 0.7 copy-done.8
  5.2 0.3 dispatch.1
  5.5 0.5 collective-permute-start
  6.0 1.1 %collective-permute-done = bf16[96,1280]{1,0:T(8,128)(2,1)S(1)} collective-permute-done((bf16[96,1280]{1,0:T(8,128)(2,1)S(1)}, bf16[96,1280]{1,0:T(8,128)(2,1)S(1)}, u32[]{:S(2)}, u32[]{:S(2)}) %collective-permute-start) | collective-permute-done | bytes 245792 | tf_op jit(solution)/shard_map/ppermute | solution.py:128
  7.2 3.0 %collective-permute-start.1 = (bf16[48,1280]{1,0:T(8,128)(2,1)S(1)}, bf16[48,1280]{1,0:T(8,128)(2,1)S(1)}, u32[]{:S(2)}, u32[]{:S(2)}) collective-permute-start(bf16[48,1280]{1,0:T(8,128)(2,1)S(1)} %pad_maximum_fusion.1), channel_id=1, source_target_pairs={{0,2},{1,3},{2,0},{3,1},{4,6},{5,7},{6,4},{7,5},{8,10},{9,11},{10,... | collective-permute-start | bytes 368648 | tf_op jit(solution)/shard_map/ppermute | solution.py:128
  10.2 2.7 %collective-permute-start.9 = (bf16[48,1280]{1,0:T(8,128)(2,1)S(1)}, bf16[48,1280]{1,0:T(8,128)(2,1)S(1)}, u32[]{:S(2)}, u32[]{:S(2)}) collective-permute-start(bf16[48,1280]{1,0:T(8,128)(2,1)S(1)} %pad_maximum_fusion.2), channel_id=1, source_target_pairs={{0,4},{1,5},{2,6},{3,7},{4,0},{5,1},{6,2},{7,3},{8,12},{9,13},{10,... | collective-permute-start | bytes 368648 | tf_op jit(solution)/shard_map/ppermute | solution.py:128
  12.9 0.1 collective-permute-start.10
  12.9 2.5 %collective-permute-done.1 = bf16[48,1280]{1,0:T(8,128)(2,1)S(1)} collective-permute-done((bf16[48,1280]{1,0:T(8,128)(2,1)S(1)}, bf16[48,1280]{1,0:T(8,128)(2,1)S(1)}, u32[]{:S(2)}, u32[]{:S(2)}) %collective-permute-start.1) | collective-permute-done | bytes 122912 | tf_op jit(solution)/shard_map/ppermute | solution.py:128
  15.4 2.7 %collective-permute-start.4 = (bf16[96,1280]{1,0:T(8,128)(2,1)S(1)}, bf16[96,1280]{1,0:T(8,128)(2,1)S(1)}, u32[]{:S(2)}, u32[]{:S(2)}) collective-permute-start(bf16[96,1280]{1,0:T(8,128)(2,1)S(1)} %pad_maximum_fusion.refs_0_), channel_id=1, source_target_pairs={{0,24},{8,16},{16,8},{24,0},{1,25},{9,17},{17,9},{25,1},{2,26},{10... | collective-permute-start | bytes 737288 | tf_op jit(solution)/shard_map/ppermute | solution.py:128
  18.2 0.5 collective-permute-start.3
  18.7 0.3 collective-permute-start.2
  19.0 3.7 %collective-permute-done.9 = bf16[48,1280]{1,0:T(8,128)(2,1)S(1)} collective-permute-done((bf16[48,1280]{1,0:T(8,128)(2,1)S(1)}, bf16[48,1280]{1,0:T(8,128)(2,1)S(1)}, u32[]{:S(2)}, u32[]{:S(2)}) %collective-permute-start.9) | collective-permute-done | bytes 122912 | tf_op jit(solution)/shard_map/ppermute | solution.py:128
  22.6 0.0 collective-permute-done.10
  22.7 2.5 %collective-permute-start.13 = (bf16[96,1280]{1,0:T(8,128)(2,1)S(1)}, bf16[96,1280]{1,0:T(8,128)(2,1)S(1)}, u32[]{:S(2)}, u32[]{:S(2)}) collective-permute-start(bf16[96,1280]{1,0:T(8,128)(2,1)S(1)} %constant_dynamic-update-slice_fusion.refs_0_), channel_id=1, source_target_pairs={{0,24},{8,16},{16,8},{24,0},{1,25},{9,17},{17,9},{25,1},{2,26},{10... | collective-permute-start | bytes 737288 | tf_op jit(solution)/shard_map/ppermute | solution.py:128
  25.2 0.5 collective-permute-start.12
  25.7 0.0 collective-permute-done.4.refs_3_
  25.7 1.2 %collective-permute-start.11 = (bf16[96,1280]{1,0:T(8,128)(2,1)S(1)}, bf16[96,1280]{1,0:T(8,128)(2,1)S(1)}, u32[]{:S(2)}, u32[]{:S(2)}) collective-permute-start(bf16[96,1280]{1,0:T(8,128)(2,1)S(1)} %constant_dynamic-update-slice_fusion.refs_0_), channel_id=1, source_target_pairs={{0,8},{8,0},{16,24},{24,16},{1,9},{9,1},{17,25},{25,17},{2,10},{10... | collective-permute-start | bytes 737288 | tf_op jit(solution)/shard_map/ppermute | solution.py:128
  26.9 5.4 %collective-permute-done.3.refs_2_ = bf16[96,1280]{1,0:T(8,128)(2,1)S(1)} collective-permute-done((bf16[96,1280]{1,0:T(8,128)(2,1)S(1)}, bf16[96,1280]{1,0:T(8,128)(2,1)S(1)}, u32[]{:S(2)}, u32[]{:S(2)}) %collective-permute-start.3) | collective-permute-done | bytes 245792 | tf_op jit(solution)/shard_map/ppermute | solution.py:128
  32.4 0.0 collective-permute-done.2.refs_1_
  32.4 0.0 copy-done.9
  32.4 1.4 %copy-done.10 = bf16[1,1280,640]{2,1,0:T(8,128)(2,1)S(1)} copy-done((bf16[1,1280,640]{2,1,0:T(8,128)(2,1)S(1)}, bf16[1,1280,640]{2,1,0:T(8,128)(2,1)}, u32[]{:S(2)}) %copy-start.10) | copy-done | bytes 1638424
  33.8 3.6 %chunk.2 = (bf16[96,640]{1,0:T(8,128)(2,1)S(1)}, bf16[96,640]{1,0:T(8,128)(2,1)S(1)}, bf16[96,640]{1,0:T(8,128)(2,1)S(1)}, bf16[96,640]{1,0:T(8,128)(2,1)S(1)}, ...) custom-call(bf16[96,1280]{1,0:T(8,128)(2,1)S(1)} %pad_maximum_fusion.refs_0_, ...), custom_call_target="tpu_custom_call" | custom-call | flops 1887436800 | bytes 3276800 | tf_op jit(solution)/shard_map/chunk/pallas_call | solution.py:178
  37.4 0.7 %collective-permute-start.5 = (bf16[96,640]{1,0:T(8,128)(2,1)S(1)}, bf16[96,640]{1,0:T(8,128)(2,1)S(1)}, u32[]{:S(2)}, u32[]{:S(2)}) collective-permute-start(bf16[96,640]{1,0:T(8,128)(2,1)S(1)} %get-tuple-element.22), channel_id=1, source_target_pairs={{0,8},{8,0},{16,24},{24,16},{1,9},{9,1},{17,25},{25,17},{2,10},{10... | collective-permute-start | bytes 368648 | tf_op jit(solution)/shard_map/ppermute | solution.py:128
  38.1 0.2 collective-permute-start.6
  38.3 0.0 collective-permute-done.13.refs_3_
  38.3 2.7 %collective-permute-start.7 = (bf16[96,640]{1,0:T(8,128)(2,1)S(1)}, bf16[96,640]{1,0:T(8,128)(2,1)S(1)}, u32[]{:S(2)}, u32[]{:S(2)}) collective-permute-start(bf16[96,640]{1,0:T(8,128)(2,1)S(1)} %get-tuple-element.24), channel_id=1, source_target_pairs={{0,24},{8,16},{16,8},{24,0},{1,25},{9,17},{17,9},{25,1},{2,26},{10... | collective-permute-start | bytes 368648 | tf_op jit(solution)/shard_map/ppermute | solution.py:128
  40.9 0.0 collective-permute-done.12.refs_2_
  40.9 0.0 collective-permute-done.11.refs_1_
  40.9 0.0 copy-done.11
  40.9 3.6 %chunk.3 = (bf16[96,640]{1,0:T(8,128)(2,1)S(1)}, bf16[96,640]{1,0:T(8,128)(2,1)S(1)}, bf16[96,640]{1,0:T(8,128)(2,1)S(1)}, bf16[96,640]{1,0:T(8,128)(2,1)S(1)}, ...) custom-call(bf16[96,1280]{1,0:T(8,128)(2,1)S(1)} %constant_dynamic-update-slice_fusion.re, ...), custom_call_target="tpu_custom_call" | custom-call | flops 1887436800 | bytes 3276800 | tf_op jit(solution)/shard_map/chunk/pallas_call | solution.py:178
  44.5 0.7 %collective-permute-start.14 = (bf16[96,640]{1,0:T(8,128)(2,1)S(1)}, bf16[96,640]{1,0:T(8,128)(2,1)S(1)}, u32[]{:S(2)}, u32[]{:S(2)}) collective-permute-start(bf16[96,640]{1,0:T(8,128)(2,1)S(1)} %get-tuple-element.26), channel_id=1, source_target_pairs={{0,8},{8,0},{16,24},{24,16},{1,9},{9,1},{17,25},{25,17},{2,10},{10... | collective-permute-start | bytes 368648 | tf_op jit(solution)/shard_map/ppermute | solution.py:128
  45.2 0.2 collective-permute-start.15
  45.4 3.1 %weight_in_grad.1 = bf16[640,1280]{1,0:T(8,128)(2,1)} custom-call(bf16[384,1280]{1,0:T(8,128)(2,1)S(1)} %get-tuple-element.29.refs_0_, bf16[384,1280]{1,0:T(8,128)(2,1)S(1)} %get-tuple-element.30.refs_1_, bf16[384,1280]{1,0:T(8,128)(2,1)S(1)} %get-tuple-element.31.refs_2_, bf16[384,1280]{1,0:T(8,128)(2,1)S(1)} %get-tuple-element.32.refs_3_), custom_call_target="tpu_custom_call" | custom-call | flops 1258291200 | bytes 1638400 | tf_op jit(solution)/shard_map/weight_in_grad/pallas_call | solution.py:207
  48.5 0.0 collective-permute-done.5
  48.5 2.7 %collective-permute-start.16 = (bf16[96,640]{1,0:T(8,128)(2,1)S(1)}, bf16[96,640]{1,0:T(8,128)(2,1)S(1)}, u32[]{:S(2)}, u32[]{:S(2)}) collective-permute-start(bf16[96,640]{1,0:T(8,128)(2,1)S(1)} %get-tuple-element.28), channel_id=1, source_target_pairs={{0,24},{8,16},{16,8},{24,0},{1,25},{9,17},{17,9},{25,1},{2,26},{10... | collective-permute-start | bytes 368648 | tf_op jit(solution)/shard_map/ppermute | solution.py:128
  51.1 0.0 collective-permute-done.6
  51.1 0.0 collective-permute-done.7
  51.1 0.1 add_convert_fusion.1
  51.2 0.3 collective-permute-start.8
  51.5 0.0 collective-permute-done.14
  51.5 0.0 collective-permute-done.15
  51.5 2.7 %collective-permute-done.16 = bf16[96,640]{1,0:T(8,128)(2,1)S(1)} collective-permute-done((bf16[96,640]{1,0:T(8,128)(2,1)S(1)}, bf16[96,640]{1,0:T(8,128)(2,1)S(1)}, u32[]{:S(2)}, u32[]{:S(2)}) %collective-permute-start.16) | collective-permute-done | bytes 122912 | tf_op jit(solution)/shard_map/ppermute | solution.py:128
  54.2 0.1 add_convert_fusion
  54.4 3.8 %collective-permute-start.17 = (bf16[48,640]{1,0:T(8,128)(2,1)S(1)}, bf16[48,640]{1,0:T(8,128)(2,1)S(1)}, u32[]{:S(2)}, u32[]{:S(2)}) collective-permute-start(bf16[48,640]{1,0:T(8,128)(2,1)S(1)} %get-tuple-element.45), channel_id=1, source_target_pairs={{0,4},{1,5},{2,6},{3,7},{4,0},{5,1},{6,2},{7,3},{8,12},{9,13},{10,... | collective-permute-start | bytes 184328 | tf_op jit(solution)/shard_map/ppermute | solution.py:128
  58.1 2.3 %collective-permute-start.18 = (bf16[48,640]{1,0:T(8,128)(2,1)S(1)}, bf16[48,640]{1,0:T(8,128)(2,1)S(1)}, u32[]{:S(2)}, u32[]{:S(2)}) collective-permute-start(bf16[48,640]{1,0:T(8,128)(2,1)S(1)} %get-tuple-element.46), channel_id=1, source_target_pairs={{0,6},{1,7},{2,4},{3,5},{4,2},{5,3},{6,0},{7,1},{8,14},{9,15},{10,... | collective-permute-start | bytes 184328 | tf_op jit(solution)/shard_map/ppermute | solution.py:128
  60.4 0.0 collective-permute-done.8
  60.5 0.0 collective-permute-done.17
  60.5 3.7 %collective-permute-done.18 = bf16[48,640]{1,0:T(8,128)(2,1)S(1)} collective-permute-done((bf16[48,640]{1,0:T(8,128)(2,1)S(1)}, bf16[48,640]{1,0:T(8,128)(2,1)S(1)}, u32[]{:S(2)}, u32[]{:S(2)}) %collective-permute-start.18) | collective-permute-done | bytes 61472 | tf_op jit(solution)/shard_map/ppermute | solution.py:128
  64.2 0.1 collective-permute-start.19
  64.3 0.0 copy-start.3
  64.3 0.0 copy-start.5
  64.3 0.0 copy-start.7
  64.3 3.2 %weight_out_grad.1 = bf16[1280,640]{1,0:T(8,128)(2,1)} custom-call(bf16[384,1280]{1,0:T(8,128)(2,1)S(1)} %get-tuple-element.29.refs_0_, bf16[384,1280]{1,0:T(8,128)(2,1)S(1)} %get-tuple-element.30.refs_1_, bf16[384,1280]{1,0:T(8,128)(2,1)S(1)} %get-tuple-element.33.refs_2_, bf16[384,1280]{1,0:T(8,128)(2,1)S(1)} %get-tuple-element.34.refs_3_), custom_call_target="tpu_custom_call" | custom-call | flops 1258291200 | bytes 1638400 | tf_op jit(solution)/shard_map/weight_out_grad/pallas_call | solution.py:213
  67.6 0.0 collective-permute-done.19.other_ref
  67.6 0.0 copy-done.3
  67.6 0.0 copy-done.5
  67.6 0.0 copy-done.7
  67.6 1.0 %combine.1 = bf16[128,640]{1,0:T(8,128)(2,1)} custom-call(bf16[96,640]{1,0:T(8,128)(2,1)S(1)} %pad_maximum_fusion.4.own_ref, bf16[96,640]{1,0:T(8,128)(2,1)S(1)} %collective-permute-done.19.other_ref, s32[2,128]{1,0:T(2,128)S(1)} %bitcast.9, s32[2,128]{1,0:T(2,128)S(1)} %bitcast.11, s32[2,128]{1,0:T(2,128)S(1)} %bitcast.13), custom_call_target="tpu_custom_call" | custom-call | tf_op jit(solution)/shard_map/combine/pallas_call | solution.py:223
  (24 shorter events, 0.2 us)
Async XLA Ops:
  0.6 0.9 %copy-start = (bf16[128,640]{1,0:T(8,128)(2,1)S(1)}, bf16[128,640]{1,0:T(8,128)(2,1)}, u32[]{:S(2)}) copy-start(bf16[128,640]{1,0:T(8,128)(2,1)} %tokens_ref.1) | copy-start | bytes 491524
  1.5 0.9 %copy-start.1 = (bf16[128,640]{1,0:T(8,128)(2,1)S(1)}, bf16[128,640]{1,0:T(8,128)(2,1)}, u32[]{:S(2)}) copy-start(bf16[128,640]{1,0:T(8,128)(2,1)} %grads_ref.1) | copy-start | bytes 491524
  2.5 0.7 copy-start.2
  3.1 0.7 copy-start.4
  3.8 0.7 copy-start.6
  4.5 0.7 copy-start.8
  5.2 27.2 %copy-start.9 = (bf16[1,640,1280]{2,1,0:T(8,128)(2,1)S(1)}, bf16[1,640,1280]{2,1,0:T(8,128)(2,1)}, u32[]{:S(2)}) copy-start(bf16[1,640,1280]{2,1,0:T(8,128)(2,1)} %param.14) | copy-start | bytes 4915204
  5.5 1.7 %collective-permute-start = (bf16[96,1280]{1,0:T(8,128)(2,1)S(1)}, bf16[96,1280]{1,0:T(8,128)(2,1)S(1)}, u32[]{:S(2)}, u32[]{:S(2)}) collective-permute-start(bf16[96,1280]{1,0:T(8,128)(2,1)S(1)} %get-tuple-element.20), channel_id=1, source_target_pairs={{0,1},{1,0},{2,3},{3,2},{4,5},{5,4},{6,7},{7,6},{8,9},{9,8},{10,11... | collective-permute-start | bytes 737288 | tf_op jit(solution)/shard_map/ppermute | solution.py:128
  7.2 8.2 %collective-permute-start.1 = (bf16[48,1280]{1,0:T(8,128)(2,1)S(1)}, bf16[48,1280]{1,0:T(8,128)(2,1)S(1)}, u32[]{:S(2)}, u32[]{:S(2)}) collective-permute-start(bf16[48,1280]{1,0:T(8,128)(2,1)S(1)} %pad_maximum_fusion.1), channel_id=1, source_target_pairs={{0,2},{1,3},{2,0},{3,1},{4,6},{5,7},{6,4},{7,5},{8,10},{9,11},{10,... | collective-permute-start | bytes 368648 | tf_op jit(solution)/shard_map/ppermute | solution.py:128
  10.2 12.4 %collective-permute-start.9 = (bf16[48,1280]{1,0:T(8,128)(2,1)S(1)}, bf16[48,1280]{1,0:T(8,128)(2,1)S(1)}, u32[]{:S(2)}, u32[]{:S(2)}) collective-permute-start(bf16[48,1280]{1,0:T(8,128)(2,1)S(1)} %pad_maximum_fusion.2), channel_id=1, source_target_pairs={{0,4},{1,5},{2,6},{3,7},{4,0},{5,1},{6,2},{7,3},{8,12},{9,13},{10,... | collective-permute-start | bytes 368648 | tf_op jit(solution)/shard_map/ppermute | solution.py:128
  12.9 9.8 %collective-permute-start.10 = (bf16[48,1280]{1,0:T(8,128)(2,1)S(1)}, bf16[48,1280]{1,0:T(8,128)(2,1)S(1)}, u32[]{:S(2)}, u32[]{:S(2)}) collective-permute-start(bf16[48,1280]{1,0:T(8,128)(2,1)S(1)} %pad_maximum_fusion.3), channel_id=1, source_target_pairs={{0,6},{1,7},{2,4},{3,5},{4,2},{5,3},{6,0},{7,1},{8,14},{9,15},{10,... | collective-permute-start | bytes 368648 | tf_op jit(solution)/shard_map/ppermute | solution.py:128
  15.4 10.3 %collective-permute-start.4 = (bf16[96,1280]{1,0:T(8,128)(2,1)S(1)}, bf16[96,1280]{1,0:T(8,128)(2,1)S(1)}, u32[]{:S(2)}, u32[]{:S(2)}) collective-permute-start(bf16[96,1280]{1,0:T(8,128)(2,1)S(1)} %pad_maximum_fusion.refs_0_), channel_id=1, source_target_pairs={{0,24},{8,16},{16,8},{24,0},{1,25},{9,17},{17,9},{25,1},{2,26},{10... | collective-permute-start | bytes 737288 | tf_op jit(solution)/shard_map/ppermute | solution.py:128
  18.2 14.2 %collective-permute-start.3 = (bf16[96,1280]{1,0:T(8,128)(2,1)S(1)}, bf16[96,1280]{1,0:T(8,128)(2,1)S(1)}, u32[]{:S(2)}, u32[]{:S(2)}) collective-permute-start(bf16[96,1280]{1,0:T(8,128)(2,1)S(1)} %pad_maximum_fusion.refs_0_), channel_id=1, source_target_pairs={{0,16},{8,24},{16,0},{24,8},{1,17},{9,25},{17,1},{25,9},{2,18},{10... | collective-permute-start | bytes 737288 | tf_op jit(solution)/shard_map/ppermute | solution.py:128
  18.7 13.7 %collective-permute-start.2 = (bf16[96,1280]{1,0:T(8,128)(2,1)S(1)}, bf16[96,1280]{1,0:T(8,128)(2,1)S(1)}, u32[]{:S(2)}, u32[]{:S(2)}) collective-permute-start(bf16[96,1280]{1,0:T(8,128)(2,1)S(1)} %pad_maximum_fusion.refs_0_), channel_id=1, source_target_pairs={{0,8},{8,0},{16,24},{24,16},{1,9},{9,1},{17,25},{25,17},{2,10},{10... | collective-permute-start | bytes 737288 | tf_op jit(solution)/shard_map/ppermute | solution.py:128
  22.7 15.6 %collective-permute-start.13 = (bf16[96,1280]{1,0:T(8,128)(2,1)S(1)}, bf16[96,1280]{1,0:T(8,128)(2,1)S(1)}, u32[]{:S(2)}, u32[]{:S(2)}) collective-permute-start(bf16[96,1280]{1,0:T(8,128)(2,1)S(1)} %constant_dynamic-update-slice_fusion.refs_0_), channel_id=1, source_target_pairs={{0,24},{8,16},{16,8},{24,0},{1,25},{9,17},{17,9},{25,1},{2,26},{10... | collective-permute-start | bytes 737288 | tf_op jit(solution)/shard_map/ppermute | solution.py:128
  25.2 15.8 %collective-permute-start.12 = (bf16[96,1280]{1,0:T(8,128)(2,1)S(1)}, bf16[96,1280]{1,0:T(8,128)(2,1)S(1)}, u32[]{:S(2)}, u32[]{:S(2)}) collective-permute-start(bf16[96,1280]{1,0:T(8,128)(2,1)S(1)} %constant_dynamic-update-slice_fusion.refs_0_), channel_id=1, source_target_pairs={{0,16},{8,24},{16,0},{24,8},{1,17},{9,25},{17,1},{25,9},{2,18},{10... | collective-permute-start | bytes 737288 | tf_op jit(solution)/shard_map/ppermute | solution.py:128
  25.7 15.2 %collective-permute-start.11 = (bf16[96,1280]{1,0:T(8,128)(2,1)S(1)}, bf16[96,1280]{1,0:T(8,128)(2,1)S(1)}, u32[]{:S(2)}, u32[]{:S(2)}) collective-permute-start(bf16[96,1280]{1,0:T(8,128)(2,1)S(1)} %constant_dynamic-update-slice_fusion.refs_0_), channel_id=1, source_target_pairs={{0,8},{8,0},{16,24},{24,16},{1,9},{9,1},{17,25},{25,17},{2,10},{10... | collective-permute-start | bytes 737288 | tf_op jit(solution)/shard_map/ppermute | solution.py:128
  32.4 1.4 %copy-start.10 = (bf16[1,1280,640]{2,1,0:T(8,128)(2,1)S(1)}, bf16[1,1280,640]{2,1,0:T(8,128)(2,1)}, u32[]{:S(2)}) copy-start(bf16[1,1280,640]{2,1,0:T(8,128)(2,1)} %param.15) | copy-start | bytes 4915204
  33.8 7.1 %copy-start.11 = (bf16[1,1280,640]{2,1,0:T(8,128)(2,1)S(1)}, bf16[1,1280,640]{2,1,0:T(8,128)(2,1)}, u32[]{:S(2)}) copy-start(bf16[1,1280,640]{2,1,0:T(8,128)(2,1)} %param.15) | copy-start | bytes 4915204
  37.4 11.1 %collective-permute-start.5 = (bf16[96,640]{1,0:T(8,128)(2,1)S(1)}, bf16[96,640]{1,0:T(8,128)(2,1)S(1)}, u32[]{:S(2)}, u32[]{:S(2)}) collective-permute-start(bf16[96,640]{1,0:T(8,128)(2,1)S(1)} %get-tuple-element.22), channel_id=1, source_target_pairs={{0,8},{8,0},{16,24},{24,16},{1,9},{9,1},{17,25},{25,17},{2,10},{10... | collective-permute-start | bytes 368648 | tf_op jit(solution)/shard_map/ppermute | solution.py:128
  38.1 13.0 %collective-permute-start.6 = (bf16[96,640]{1,0:T(8,128)(2,1)S(1)}, bf16[96,640]{1,0:T(8,128)(2,1)S(1)}, u32[]{:S(2)}, u32[]{:S(2)}) collective-permute-start(bf16[96,640]{1,0:T(8,128)(2,1)S(1)} %get-tuple-element.23), channel_id=1, source_target_pairs={{0,16},{8,24},{16,0},{24,8},{1,17},{9,25},{17,1},{25,9},{2,18},{10... | collective-permute-start | bytes 368648 | tf_op jit(solution)/shard_map/ppermute | solution.py:128
  38.3 12.9 %collective-permute-start.7 = (bf16[96,640]{1,0:T(8,128)(2,1)S(1)}, bf16[96,640]{1,0:T(8,128)(2,1)S(1)}, u32[]{:S(2)}, u32[]{:S(2)}) collective-permute-start(bf16[96,640]{1,0:T(8,128)(2,1)S(1)} %get-tuple-element.24), channel_id=1, source_target_pairs={{0,24},{8,16},{16,8},{24,0},{1,25},{9,17},{17,9},{25,1},{2,26},{10... | collective-permute-start | bytes 368648 | tf_op jit(solution)/shard_map/ppermute | solution.py:128
  44.5 7.0 %collective-permute-start.14 = (bf16[96,640]{1,0:T(8,128)(2,1)S(1)}, bf16[96,640]{1,0:T(8,128)(2,1)S(1)}, u32[]{:S(2)}, u32[]{:S(2)}) collective-permute-start(bf16[96,640]{1,0:T(8,128)(2,1)S(1)} %get-tuple-element.26), channel_id=1, source_target_pairs={{0,8},{8,0},{16,24},{24,16},{1,9},{9,1},{17,25},{25,17},{2,10},{10... | collective-permute-start | bytes 368648 | tf_op jit(solution)/shard_map/ppermute | solution.py:128
  45.2 6.3 %collective-permute-start.15 = (bf16[96,640]{1,0:T(8,128)(2,1)S(1)}, bf16[96,640]{1,0:T(8,128)(2,1)S(1)}, u32[]{:S(2)}, u32[]{:S(2)}) collective-permute-start(bf16[96,640]{1,0:T(8,128)(2,1)S(1)} %get-tuple-element.27), channel_id=1, source_target_pairs={{0,16},{8,24},{16,0},{24,8},{1,17},{9,25},{17,1},{25,9},{2,18},{10... | collective-permute-start | bytes 368648 | tf_op jit(solution)/shard_map/ppermute | solution.py:128
  48.5 5.8 %collective-permute-start.16 = (bf16[96,640]{1,0:T(8,128)(2,1)S(1)}, bf16[96,640]{1,0:T(8,128)(2,1)S(1)}, u32[]{:S(2)}, u32[]{:S(2)}) collective-permute-start(bf16[96,640]{1,0:T(8,128)(2,1)S(1)} %get-tuple-element.28), channel_id=1, source_target_pairs={{0,24},{8,16},{16,8},{24,0},{1,25},{9,17},{17,9},{25,1},{2,26},{10... | collective-permute-start | bytes 368648 | tf_op jit(solution)/shard_map/ppermute | solution.py:128
  51.2 9.2 %collective-permute-start.8 = (bf16[48,640]{1,0:T(8,128)(2,1)S(1)}, bf16[48,640]{1,0:T(8,128)(2,1)S(1)}, u32[]{:S(2)}, u32[]{:S(2)}) collective-permute-start(bf16[48,640]{1,0:T(8,128)(2,1)S(1)} %slice.82), channel_id=1, source_target_pairs={{0,2},{1,3},{2,0},{3,1},{4,6},{5,7},{6,4},{7,5},{8,10},{9,11},{10,... | collective-permute-start | bytes 184328 | tf_op jit(solution)/shard_map/ppermute | solution.py:128
  54.4 6.1 %collective-permute-start.17 = (bf16[48,640]{1,0:T(8,128)(2,1)S(1)}, bf16[48,640]{1,0:T(8,128)(2,1)S(1)}, u32[]{:S(2)}, u32[]{:S(2)}) collective-permute-start(bf16[48,640]{1,0:T(8,128)(2,1)S(1)} %get-tuple-element.45), channel_id=1, source_target_pairs={{0,4},{1,5},{2,6},{3,7},{4,0},{5,1},{6,2},{7,3},{8,12},{9,13},{10,... | collective-permute-start | bytes 184328 | tf_op jit(solution)/shard_map/ppermute | solution.py:128
  58.1 6.0 %collective-permute-start.18 = (bf16[48,640]{1,0:T(8,128)(2,1)S(1)}, bf16[48,640]{1,0:T(8,128)(2,1)S(1)}, u32[]{:S(2)}, u32[]{:S(2)}) collective-permute-start(bf16[48,640]{1,0:T(8,128)(2,1)S(1)} %get-tuple-element.46), channel_id=1, source_target_pairs={{0,6},{1,7},{2,4},{3,5},{4,2},{5,3},{6,0},{7,1},{8,14},{9,15},{10,... | collective-permute-start | bytes 184328 | tf_op jit(solution)/shard_map/ppermute | solution.py:128
  64.2 3.4 %collective-permute-start.19 = (bf16[96,640]{1,0:T(8,128)(2,1)S(1)}, bf16[96,640]{1,0:T(8,128)(2,1)S(1)}, u32[]{:S(2)}, u32[]{:S(2)}) collective-permute-start(bf16[96,640]{1,0:T(8,128)(2,1)S(1)} %pad_maximum_fusion.5), channel_id=1, source_target_pairs={{0,1},{1,0},{2,3},{3,2},{4,5},{5,4},{6,7},{7,6},{8,9},{9,8},{10,11... | collective-permute-start | bytes 368648 | tf_op jit(solution)/shard_map/ppermute | solution.py:128
  64.3 3.3 %copy-start.3 = (s32[128,2]{0,1:T(2,128)S(1)}, s32[128,2]{0,1:T(2,128)}, u32[]{:S(2)}) copy-start(s32[128,2]{0,1:T(2,128)} %param.11) | copy-start | bytes 3076
  64.3 3.3 %copy-start.5 = (s32[128,2]{0,1:T(2,128)S(1)}, s32[128,2]{0,1:T(2,128)}, u32[]{:S(2)}) copy-start(s32[128,2]{0,1:T(2,128)} %param.12) | copy-start | bytes 3076
  64.3 3.3 %copy-start.7 = (s32[128,2]{0,1:T(2,128)S(1)}, s32[128,2]{0,1:T(2,128)}, u32[]{:S(2)}) copy-start(s32[128,2]{0,1:T(2,128)} %param.13) | copy-start | bytes 3076

commit v2 on v1

v2 whole, which is shorter than its diff:
```python
import functools

import jax
import jax.numpy as jnp
from jax import lax
from jax.experimental import pallas as pl
from jax.experimental.pallas import tpu as pltpu
from jax.sharding import PartitionSpec as P

root_coef = 0.7978845608028654
cube_coef = 0.044715
vmem_whole = pl.BlockSpec(memory_space=pltpu.VMEM)
anywhere = pl.BlockSpec(memory_space=pl.ANY)
f32 = jnp.float32
CHUNKS = (((0, 1),), ((2, 3),))
DIRECT = (True, True)
LANES = ((True,), (True,))
AFTER = (0, -1)
TILE = 1280
LOAD = None
GATE = False
bf16 = jnp.bfloat16


def in_hbm(value):
    return pltpu.with_memory_space_constraint(value, pltpu.HBM)


def vmem_out(shape, dtype=bf16):
    return pltpu.VMEM(shape, dtype)


def params(mib):
    return pltpu.CompilerParams(vmem_limit_bytes=mib * 1024 * 1024)


def cost(flops, moved, trans=0):
    return pl.CostEstimate(flops=flops, bytes_accessed=moved, transcendentals=trans)


def selector_columns(ids, slots, keep, me, slot_cap, half):
    relative = ids ^ me
    column = (relative & 1) * half + (relative >> 1) * slot_cap + slots
    return jnp.where(keep > 0, column, -1)


def dispatch_kernel(slot_cap, *refs):
    sources, (own_ref, other_ref), held, sem = refs[:6], refs[6:8], refs[8:14], refs[14]
    copies = [pltpu.make_async_copy(a, b, sem.at[i]) for i, (a, b) in enumerate(zip(sources, held, strict=True))]
    for copy in copies:
        copy.start()
    for copy in copies:
        copy.wait()
    tokens_ref, grads_ref, gate_ref, ids_ref, slots_ref, keep_ref = held
    half = own_ref.shape[0]
    token_count, width = tokens_ref.shape
    me = lax.axis_index("expert")
    column = selector_columns(ids_ref[...], slots_ref[...], keep_ref[...], me, slot_cap, half)
    gate = gate_ref[...]
    for base, out_ref in ((half, other_ref), (0, own_ref)):
        rows = lax.broadcasted_iota(jnp.int32, (half, token_count), 0) + base
        first, second = rows == column[0:1], rows == column[1:2]
        picked = (first | second).astype(f32).astype(bf16)
        scale = jnp.sum(
            jnp.where(first, gate[0:1], 0.0) + jnp.where(second, gate[1:2], 0.0), axis=1, keepdims=True
        )
        out_ref[:, :width] = jnp.dot(picked, tokens_ref[...], preferred_element_type=f32).astype(bf16)
        row_grad = jnp.dot(picked, grads_ref[...], preferred_element_type=f32)
        out_ref[:, width:] = (scale * row_grad).astype(bf16)


def combine_kernel(slot_cap, own_ref, other_ref, ids_ref, slots_ref, keep_ref, out_ref):
    half = own_ref.shape[0]
    token_count = out_ref.shape[0]
    me = lax.axis_index("expert")
    column = selector_columns(ids_ref[...], slots_ref[...], keep_ref[...], me, slot_cap, half)
    total = jnp.zeros(out_ref.shape, f32)
    for base, rows_ref in ((0, own_ref), (half, other_ref)):
        rows = lax.broadcasted_iota(jnp.int32, (half, token_count), 0) + base
        picked = ((rows == column[0:1]) | (rows == column[1:2])).astype(f32).astype(bf16)
        total += lax.dot_general(picked, rows_ref[...], (((0,), (0,)), ((), ())), preferred_element_type=f32)
    out_ref[...] = total.astype(bf16)


def gathered_order(bits):
    order = [0]
    steps = []
    for bit in bits:
        steps.append([o ^ bit for o in order])
        order = order + steps[-1]
    return steps


def scattered_order(bits, groups):
    left = list(range(groups))
    steps = []
    for bit in bits:
        steps.append([o for o in left if o & bit])
        left = [o for o in left if not o & bit]
    return steps


def load_kernel(*refs):
    sources, targets, sem = refs[:2], refs[-3:-1], refs[-1]
    copies = [pltpu.make_async_copy(a, b, sem.at[i]) for i, (a, b) in enumerate(zip(sources, targets, strict=True))]
    for copy in copies:
        copy.start()
    for copy in copies:
        copy.wait()


def chunk_kernel(tile, groups, cuts, places, *refs):
    moved, refs = refs[: len(places)], refs[len(places) :]
    (win_ref, wout_ref), outs = refs[:2], refs[2:]
    sends, kept_ref = outs[:-5], outs[-5]
    rows_ref, hidden_ref, pre_ref, acc_ref = outs[-4:]
    width, hidden_total = win_ref.shape
    count = rows_ref.shape[0] // groups
    for ref, (start, size, low, high, offsets) in zip(moved, places, strict=True):
        for i, o in enumerate(offsets):
            rows_ref[o * count + start : o * count + start + size, low:high] = ref[i * size : (i + 1) * size, :]
    for base in range(0, hidden_total, tile):
        cols = slice(base, base + tile)
        preact = jnp.dot(rows_ref[:, :width], win_ref[:, cols], preferred_element_type=f32)
        backprop = lax.dot_general(
            rows_ref[:, width:], wout_ref[cols, :], (((1,), (1,)), ((), ())), preferred_element_type=f32
        )
        square = preact * preact
        tanh_value = jnp.tanh(root_coef * (preact + cube_coef * preact * square))
        one_plus = 0.5 * (1.0 + tanh_value)
        hidden_ref[:, cols] = (preact * one_plus).astype(bf16)
        slope = one_plus + 0.5 * preact * (1.0 - tanh_value * tanh_value) * (
            root_coef + (3.0 * cube_coef * root_coef) * square
        )
        grad_pre = (slope * backprop).astype(bf16)
        pre_ref[:, cols] = grad_pre
        term = lax.dot_general(
            grad_pre, win_ref[:, cols], (((1,), (1,)), ((), ())), preferred_element_type=f32
        )
        if base == 0:
            acc_ref[...] = term
        else:
            acc_ref[...] += term
    kept_ref[...] = acc_ref[:count, :].astype(bf16)
    for (low, high, offsets), ref in zip(cuts, sends, strict=True):
        for i, o in enumerate(offsets):
            ref[i * (high - low) : (i + 1) * (high - low), :] = acc_ref[o * count + low : o * count + high, :].astype(
                bf16
            )


def stacked(refs, cols):
    return jnp.concatenate([ref[:, cols] for ref in refs], axis=0)


def weight_in_kernel(count, width, *refs):
    rows, pre = stacked(refs[:count], slice(0, width)), stacked(refs[count : 2 * count], slice(None))
    out_ref, done_ref = refs[-2:]
    total = lax.dot_general(rows, pre, (((0,), (0,)), ((), ())), preferred_element_type=f32)
    out_ref[...] = total.astype(bf16)
    done_ref[...] = jnp.zeros(done_ref.shape, bf16)


def weight_out_kernel(count, width, *refs):
    cot = stacked(refs[:count], slice(width, 2 * width))
    hidden = stacked(refs[count : 2 * count], slice(None))
    out_ref, done_ref = refs[-2:]
    total = lax.dot_general(hidden, cot, (((0,), (0,)), ((), ())), preferred_element_type=f32)
    out_ref[...] = total.astype(bf16)
    done_ref[...] = jnp.zeros(done_ref.shape, bf16)


def sum_kernel(*refs):
    total = refs[0][...].astype(f32)
    for ref in refs[1:-2]:
        total = total + ref[...].astype(f32)
    refs[-1][...] = total.astype(bf16)


def pack_kernel(slot_cap, *refs):
    returned, (own_ref, other_ref) = refs[:-3], refs[-2:]
    rows = jnp.concatenate([ref[...].astype(f32) for ref in returned], axis=0)
    rows = rows.reshape(len(returned), 2, slot_cap, rows.shape[-1])
    for part, ref in ((0, own_ref), (1, other_ref)):
        ref[...] = rows[:, part].reshape(ref.shape).astype(bf16)


def added(value, offsets, received, size):
    total = value.astype(f32)
    for held, part in received:
        at = [held.index(o) * size for o in offsets]
        total = total + jnp.concatenate([part[i : i + size] for i in at], axis=0).astype(f32)
    return total.astype(bf16)


def swap(value, axis, offset):
    size = lax.axis_size(axis)
    return lax.ppermute(value, axis, [(i, i ^ offset) for i in range(size)])


def body(
    layer_input,
    output_grad,
    gate_weights,
    expert_ids,
    slot_positions,
    keep_mask,
    weight_in,
    weight_out,
):
    token_count, width = layer_input.shape
    owners = lax.axis_size("expert")
    groups = lax.axis_size("dp")
    slot_cap = 3 * token_count // (2 * owners)
    chips = owners // 2
    half = chips * slot_cap
    block = 2 * slot_cap
    gate, ids, slots, keep = gate_weights.T, expert_ids.T, slot_positions.T, keep_mask.T
    win, wout = weight_in[0], weight_out[0]
    hidden_total = win.shape[1]

    arguments = (layer_input, output_grad, gate, ids, slots, keep)
    own, other = pl.pallas_call(
        functools.partial(dispatch_kernel, slot_cap),
        out_shape=(vmem_out((half, 2 * width)),) * 2,
        in_specs=[pl.BlockSpec(memory_space=pltpu.HBM)] * 6,
        out_specs=(vmem_whole,) * 2,
        scratch_shapes=[pltpu.VMEM(a.shape, a.dtype) for a in arguments] + [pltpu.SemaphoreType.DMA((6,))],
        compiler_params=params(16),
        name="dispatch",
    )(*[in_hbm(a) for a in arguments])
    got = swap(other, "expert", 1)

    arrived = []
    for m in range(chips):
        span = slice(m * slot_cap, (m + 1) * slot_cap)
        rows = jnp.concatenate([own[span], got[span]], axis=0)
        arrived.append(rows if m == 0 else swap(rows, "expert", 2 * m))

    quarter = chips // 4
    chunks = [[[q * quarter + i for q in quarters for i in range(quarter)] for quarters in c] for c in CHUNKS]
    chunk_count = len(chunks)
    returned = [None] * chips
    all_rows, all_hidden, all_pre = [], [], []
    bits = [1 << i for i in range(groups.bit_length() - 1)]
    lanes = (bits, bits[::-1])
    steps = len(bits)
    weights = pl.pallas_call(
        load_kernel,
        out_shape=(vmem_out(win.shape), vmem_out(wout.shape)),
        in_specs=[pl.BlockSpec(memory_space=pltpu.HBM)] * 2 + [anywhere],
        out_specs=(vmem_whole,) * 2,
        scratch_shapes=[pltpu.SemaphoreType.DMA((2,))],
        compiler_params=params(16),
        cost_estimate=cost(0, 8 * width * hidden_total),
        name="load",
    )(in_hbm(win), in_hbm(wout), got if LOAD is None else arrived[LOAD * quarter])
    sums_of = []
    all_count = block * chips * groups
    weight_call = dict(
        in_specs=[vmem_whole] * (2 * chunk_count) + [anywhere],
        out_specs=(vmem_whole,) * 2,
        compiler_params=params(40),
        cost_estimate=cost(2 * all_count * width * hidden_total, 2 * width * hidden_total),
    )

    def weight_in_call(after):
        return pl.pallas_call(
            functools.partial(weight_in_kernel, chunk_count, width),
            out_shape=(jax.ShapeDtypeStruct((width, hidden_total), bf16), vmem_out((16, 128))),
            name="weight_in_grad",
            **weight_call,
        )(*all_rows, *all_pre, after)

    def weight_out_call(after):
        return pl.pallas_call(
            functools.partial(weight_out_kernel, chunk_count, width),
            out_shape=(jax.ShapeDtypeStruct((hidden_total, width), bf16), vmem_out((16, 128))),
            name="weight_out_grad",
            **weight_call,
        )(*all_rows, *all_hidden, after)

    for number, chunk in enumerate(chunks):
        moved, places, start = [], [], 0
        for by_lanes, group in zip(LANES[number], chunk, strict=True):
            mine = jnp.concatenate([arrived[m] for m in group], axis=0)
            size = mine.shape[0]
            if by_lanes:
                for lane in range(2):
                    held, low = [mine[:, lane * width : (lane + 1) * width]], lane * width
                    orders = [[0]] + gathered_order(lanes[lane])
                    for step in range(steps):
                        held.append(swap(jnp.concatenate(held, axis=0), "dp", lanes[lane][step]))
                    moved += held
                    places += [(start, size, low, low + width, offsets) for offsets in orders]
            else:
                for o in range(groups):
                    moved.append(swap(mine, "dp", o) if o else mine)
                    places.append((start, size, 0, 2 * width, [o]))
            start += size
        inside = [m for group in chunk for m in group]
        count = len(inside) * block
        total = groups * count
        cut = count // 32 * 16
        if DIRECT[number]:
            cuts = [(0, count, [o]) for o in range(1, groups)]
        else:
            cuts = [
                (low, high, offsets)
                for lane, (low, high) in zip(lanes, ((0, cut), (cut, count)), strict=True)
                for offsets in scattered_order(lane, groups)
            ]
        outs = pl.pallas_call(
            functools.partial(chunk_kernel, TILE, groups, cuts, places),
            out_shape=tuple(vmem_out((len(offsets) * (high - low), width)) for low, high, offsets in cuts)
            + (
                vmem_out((count, width)),
                vmem_out((total, 2 * width)),
                vmem_out((total, hidden_total)),
                vmem_out((total, hidden_total)),
            ),
            in_specs=[vmem_whole] * (len(moved) + 2),
            out_specs=(vmem_whole,) * (len(cuts) + 4),
            scratch_shapes=[pltpu.VMEM((total, width), f32)],
            compiler_params=params(32),
            cost_estimate=cost(6 * total * width * hidden_total, 4 * width * hidden_total, total * hidden_total),
            name="chunk",
        )(*moved, *weights)
        sends, (kept, rows_all, hidden, pre) = outs[:-4], outs[-4:]
        all_rows.append(rows_all)
        all_hidden.append(hidden)
        all_pre.append(pre)
        if DIRECT[number]:
            terms = [kept] + [swap(v, "dp", offsets[0]) for (_, _, offsets), v in zip(cuts, sends, strict=True)]
            if number == len(chunks) - 1:
                grad_in, done = weight_in_call(sums_of[0])
                summed = pl.pallas_call(
                    sum_kernel,
                    out_shape=vmem_out((count, width)),
                    in_specs=[vmem_whole] * groups + [anywhere],
                    out_specs=vmem_whole,
                    compiler_params=params(16),
                    name="sum",
                )(*terms, done)
            else:
                summed = sum(t.astype(f32) for t in terms).astype(bf16)
        else:
            finals = []
            for lane, bits_of in enumerate(lanes):
                low, high = (0, cut) if lane == 0 else (cut, count)
                received = []
                for step in range(steps):
                    value, offsets = sends[lane * steps + step], cuts[lane * steps + step][2]
                    if received:
                        value = added(value, offsets, received, high - low)
                    received.append(([o ^ bits_of[step] for o in offsets], swap(value, "dp", bits_of[step])))
                finals.append(added(kept[low:high], [0], received, high - low))
            summed = jnp.concatenate(finals, axis=0)
        sums_of.append(summed)
        for i, m in enumerate(inside):
            piece = summed[i * block : (i + 1) * block]
            returned[m] = piece if m == 0 else swap(piece, "expert", 2 * m)

    grad_out, done = weight_out_call(sums_of[-1])
    back_own, for_partner = pl.pallas_call(
        functools.partial(pack_kernel, slot_cap),
        out_shape=(vmem_out((half, width)),) * 2,
        in_specs=[vmem_whole] * chips + [anywhere],
        out_specs=(vmem_whole,) * 2,
        compiler_params=params(16),
        name="pack",
    )(*returned, done)
    back_other = swap(for_partner, "expert", 1)
    input_grad = pl.pallas_call(
        functools.partial(combine_kernel, slot_cap),
        out_shape=jax.ShapeDtypeStruct((token_count, width), bf16),
        in_specs=[vmem_whole] * 5,
        out_specs=vmem_whole,
        compiler_params=params(16),
        name="combine",
    )(back_own, back_other, ids, slots, keep)
    return (input_grad, grad_in[None], grad_out[None])


def solution(mesh):
    tokens = P(("dp", "expert"), None)
    in_specs = (tokens,) * 6 + (P("expert", None, "dp"), P("expert", "dp", None))
    out_specs = (tokens, P("expert", None, "dp"), P("expert", "dp", None))
    return jax.shard_map(body, mesh=mesh, in_specs=in_specs, out_specs=out_specs, check_vma=False)
```

time: 68.8 us -> 61 us (0.89)
  local copies, waits for them, and re-layouts: 6.1 us -> 0.14 us
  waiting for transfers between devices: 19.1 us -> 13.8 us
  starting transfers between devices: 27.6 us -> 30.7 us
    unnamed x25 -> x7, local copies, waits for them, and re-layouts: 6 us -> 0.02 us
    ppermute x20 -> x22, waiting for transfers between devices: 19.1 us -> 13.8 us  [swap(): return lax.ppermute(value, axis, [(i, i ^ offset) for i in range(size)])]
    ppermute x20 -> x22, starting transfers between devices: 27.6 us -> 30.7 us  [swap(): return lax.ppermute(value, axis, [(i, i ^ offset) for i in range(size)])]
    pallas_call x1, Pallas kernels: 0.29 us -> 1.35 us  [body(): pl.pallas_call(functools.partial(dispatch_kernel, slot_cap), out_shape=(v...]
    pallas_call x4 -> x7, Pallas kernels: 13.4 us -> 13 us  [the longest x2 5.38 us: body(): pl.pallas_call(functools.partial(chunk_kernel, TILE, groups, cuts, places...]
  transfers between devices with their start and end apart: 20 -> 22, of which waited for: 6 -> 8; matrix products, arithmetic and copies ran while one was open for 0% -> 1% of each run, Pallas kernels for 20% -> 21%
where the time goes in v2:
time: 61 us; the launch traced here: 60.8 us
  starting transfers between devices  30.7 us (50%)
  Pallas kernels  15.3 us (25%)
  waiting for transfers between devices  13.8 us (23%)
  between operations  0.81 us (1%)
    ppermute x22, starting transfers between devices, swap(): return lax.ppermute(value, axis, [(i, i ^ offset) for i in range(size)])  30.7 us
    ppermute x22, waiting for transfers between devices, swap(): return lax.ppermute(value, axis, [(i, i ^ offset) for i in range(size)])  13.8 us
    pallas_call x2, Pallas kernels, body(): pl.pallas_call(functools.partial(chunk_kernel, TILE, groups, cuts, places...  5.38 us
    pallas_call x1, Pallas kernels, weight_out_call(): pl.pallas_call(functools.partial(weight_out_kernel, chunk_count, width),...  2.9 us
    pallas_call x1, Pallas kernels, weight_in_call(): pl.pallas_call(functools.partial(weight_in_kernel, chunk_count, width), o...  2.65 us
    pallas_call x1, Pallas kernels, body(): pl.pallas_call(load_kernel, out_shape=(vmem_out(win.shape), vmem_out(wout...  1.94 us
    pallas_call x1, Pallas kernels, body(): pl.pallas_call(functools.partial(dispatch_kernel, slot_cap), out_shape=(v...  1.35 us
  transfers between devices with their start and end apart: 22, of which 8 were waited for; matrix products, arithmetic and copies ran while one was open for 1% of the time, Pallas kernels for 21%

profile of v2, /device:TPU:0, one launch (start us, length us, event | category | flops | bytes accessed | tf_op | source)
XLA Modules:
  0.0 60.8 jit_solution(5082198891472114231)
XLA Ops:
  0.6 1.3 %dispatch.1 = (bf16[96,1280]{1,0:T(8,128)(2,1)S(1)}, bf16[96,1280]{1,0:T(8,128)(2,1)S(1)}) custom-call(bf16[128,640]{1,0:T(8,128)(2,1)} %refs_0_.1, bf16[128,640]{1,0:T(8,128)(2,1)} %refs_1_.1, f32[2,128]{1,0:T(2,128)} %bitcast.16, s32[2,128]{1,0:T(2,128)} %bitcast.8, s32[2,128]{1,0:T(2,128)} %bitcast.10, s32[2,128]{1,0:T(2,128)} %bitcast.12), custom_call_target="tpu_custom_call" | custom-call | tf_op jit(solution)/shard_map/dispatch/pallas_call | solution.py:223
  2.0 0.5 collective-permute-start
  2.5 1.1 %collective-permute-done.refs_2_ = bf16[96,1280]{1,0:T(8,128)(2,1)S(1)} collective-permute-done((bf16[96,1280]{1,0:T(8,128)(2,1)S(1)}, bf16[96,1280]{1,0:T(8,128)(2,1)S(1)}, u32[]{:S(2)}, u32[]{:S(2)}) %collective-permute-start) | collective-permute-done | bytes 245792 | tf_op jit(solution)/shard_map/ppermute | solution.py:198
  3.7 3.0 %collective-permute-start.1 = (bf16[48,1280]{1,0:T(8,128)(2,1)S(1)}, bf16[48,1280]{1,0:T(8,128)(2,1)S(1)}, u32[]{:S(2)}, u32[]{:S(2)}) collective-permute-start(bf16[48,1280]{1,0:T(8,128)(2,1)S(1)} %pad_maximum_fusion.5), channel_id=1, source_target_pairs={{0,2},{1,3},{2,0},{3,1},{4,6},{5,7},{6,4},{7,5},{8,10},{9,11},{10,... | collective-permute-start | bytes 368648 | tf_op jit(solution)/shard_map/ppermute | solution.py:198
  6.7 2.7 %collective-permute-start.10 = (bf16[48,1280]{1,0:T(8,128)(2,1)S(1)}, bf16[48,1280]{1,0:T(8,128)(2,1)S(1)}, u32[]{:S(2)}, u32[]{:S(2)}) collective-permute-start(bf16[48,1280]{1,0:T(8,128)(2,1)S(1)} %pad_maximum_fusion.6), channel_id=1, source_target_pairs={{0,4},{1,5},{2,6},{3,7},{4,0},{5,1},{6,2},{7,3},{8,12},{9,13},{10,... | collective-permute-start | bytes 368648 | tf_op jit(solution)/shard_map/ppermute | solution.py:198
  9.4 0.1 collective-permute-start.11
  9.4 2.5 %collective-permute-done.1 = bf16[48,1280]{1,0:T(8,128)(2,1)S(1)} collective-permute-done((bf16[48,1280]{1,0:T(8,128)(2,1)S(1)}, bf16[48,1280]{1,0:T(8,128)(2,1)S(1)}, u32[]{:S(2)}, u32[]{:S(2)}) %collective-permute-start.1) | collective-permute-done | bytes 122912 | tf_op jit(solution)/shard_map/ppermute | solution.py:198
  12.0 1.8 %collective-permute-start.2 = (bf16[96,640]{1,0:T(8,128)(2,1)S(1)}, bf16[96,640]{1,0:T(8,128)(2,1)S(1)}, u32[]{:S(2)}, u32[]{:S(2)}) collective-permute-start(bf16[96,640]{1,0:T(8,128)(2,1)S(1)} %get-tuple-element.62.refs_0_), channel_id=1, source_target_pairs={{0,8},{8,0},{16,24},{24,16},{1,9},{9,1},{17,25},{25,17},{2,10},{10... | collective-permute-start | bytes 368648 | tf_op jit(solution)/shard_map/ppermute | solution.py:198
  13.7 1.5 %collective-permute-start.4 = (bf16[96,640]{1,0:T(8,128)(2,1)S(1)}, bf16[96,640]{1,0:T(8,128)(2,1)S(1)}, u32[]{:S(2)}, u32[]{:S(2)}) collective-permute-start(bf16[96,640]{1,0:T(8,128)(2,1)S(1)} %get-tuple-element.61.refs_3_), channel_id=1, source_target_pairs={{0,16},{8,24},{16,0},{24,8},{1,17},{9,25},{17,1},{25,9},{2,18},{10... | collective-permute-start | bytes 368648 | tf_op jit(solution)/shard_map/ppermute | solution.py:198
  15.3 3.9 %collective-permute-done.10 = bf16[48,1280]{1,0:T(8,128)(2,1)S(1)} collective-permute-done((bf16[48,1280]{1,0:T(8,128)(2,1)S(1)}, bf16[48,1280]{1,0:T(8,128)(2,1)S(1)}, u32[]{:S(2)}, u32[]{:S(2)}) %collective-permute-start.10) | collective-permute-done | bytes 122912 | tf_op jit(solution)/shard_map/ppermute | solution.py:198
  19.2 0.0 collective-permute-done.11
  19.2 1.6 %collective-permute-start.12 = (bf16[96,640]{1,0:T(8,128)(2,1)S(1)}, bf16[96,640]{1,0:T(8,128)(2,1)S(1)}, u32[]{:S(2)}, u32[]{:S(2)}) collective-permute-start(bf16[96,640]{1,0:T(8,128)(2,1)S(1)} %get-tuple-element.52.refs_0_), channel_id=1, source_target_pairs={{0,8},{8,0},{16,24},{24,16},{1,9},{9,1},{17,25},{25,17},{2,10},{10... | collective-permute-start | bytes 368648 | tf_op jit(solution)/shard_map/ppermute | solution.py:198
  20.8 1.5 %collective-permute-start.14 = (bf16[96,640]{1,0:T(8,128)(2,1)S(1)}, bf16[96,640]{1,0:T(8,128)(2,1)S(1)}, u32[]{:S(2)}, u32[]{:S(2)}) collective-permute-start(bf16[96,640]{1,0:T(8,128)(2,1)S(1)} %get-tuple-element.51.refs_3_), channel_id=1, source_target_pairs={{0,16},{8,24},{16,0},{24,8},{1,17},{9,25},{17,1},{25,9},{2,18},{10... | collective-permute-start | bytes 368648 | tf_op jit(solution)/shard_map/ppermute | solution.py:198
  22.3 0.0 collective-permute-done.2.refs_1_
  22.3 0.6 collective-permute-start.3
  22.9 0.0 collective-permute-done.4.refs_4_
  22.9 0.6 %collective-permute-start.5 = (bf16[192,640]{1,0:T(8,128)(2,1)S(1)}, bf16[192,640]{1,0:T(8,128)(2,1)S(1)}, u32[]{:S(2)}, u32[]{:S(2)}) collective-permute-start(bf16[192,640]{1,0:T(8,128)(2,1)S(1)} %pad_maximum_fusion.2), channel_id=1, source_target_pairs={{0,8},{8,0},{16,24},{24,16},{1,9},{9,1},{17,25},{25,17},{2,10},{10... | collective-permute-start | bytes 737288 | tf_op jit(solution)/shard_map/ppermute | solution.py:198
  23.5 1.9 %collective-permute-done.12.refs_1_ = bf16[96,640]{1,0:T(8,128)(2,1)S(1)} collective-permute-done((bf16[96,640]{1,0:T(8,128)(2,1)S(1)}, bf16[96,640]{1,0:T(8,128)(2,1)S(1)}, u32[]{:S(2)}, u32[]{:S(2)}) %collective-permute-start.12) | collective-permute-done | bytes 122912 | tf_op jit(solution)/shard_map/ppermute | solution.py:198
  25.5 1.6 %collective-permute-start.13 = (bf16[192,640]{1,0:T(8,128)(2,1)S(1)}, bf16[192,640]{1,0:T(8,128)(2,1)S(1)}, u32[]{:S(2)}, u32[]{:S(2)}) collective-permute-start(bf16[192,640]{1,0:T(8,128)(2,1)S(1)} %pad_maximum_fusion.3), channel_id=1, source_target_pairs={{0,16},{8,24},{16,0},{24,8},{1,17},{9,25},{17,1},{25,9},{2,18},{10... | collective-permute-start | bytes 737288 | tf_op jit(solution)/shard_map/ppermute | solution.py:198
  27.1 0.0 collective-permute-done.14.refs_4_
  27.1 1.6 %collective-permute-start.15 = (bf16[192,640]{1,0:T(8,128)(2,1)S(1)}, bf16[192,640]{1,0:T(8,128)(2,1)S(1)}, u32[]{:S(2)}, u32[]{:S(2)}) collective-permute-start(bf16[192,640]{1,0:T(8,128)(2,1)S(1)} %pad_maximum_fusion.4), channel_id=1, source_target_pairs={{0,8},{8,0},{16,24},{24,16},{1,9},{9,1},{17,25},{25,17},{2,10},{10... | collective-permute-start | bytes 737288 | tf_op jit(solution)/shard_map/ppermute | solution.py:198
  28.7 1.9 %load.1 = (bf16[640,1280]{1,0:T(8,128)(2,1)S(1)}, bf16[1280,640]{1,0:T(8,128)(2,1)S(1)}) custom-call(bf16[640,1280]{1,0:T(8,128)(2,1)} %bitcast.14, bf16[1280,640]{1,0:T(8,128)(2,1)} %bitcast.15, bf16[96,1280]{1,0:T(8,128)(2,1)S(1)} %collective-permute-done.refs_2_), custom_call_target="tpu_custom_call" | custom-call | bytes 6553600 | tf_op jit(solution)/shard_map/load/pallas_call | solution.py:248
  30.6 1.0 %collective-permute-done.3.refs_2_ = bf16[192,640]{1,0:T(8,128)(2,1)S(1)} collective-permute-done((bf16[192,640]{1,0:T(8,128)(2,1)S(1)}, bf16[192,640]{1,0:T(8,128)(2,1)S(1)}, u32[]{:S(2)}, u32[]{:S(2)}) %collective-permute-start.3) | collective-permute-done | bytes 245792 | tf_op jit(solution)/shard_map/ppermute | solution.py:198
  31.6 0.3 collective-permute-done.5.refs_5_
  31.9 2.7 %chunk.2 = (bf16[96,640]{1,0:T(8,128)(2,1)S(1)}, bf16[96,640]{1,0:T(8,128)(2,1)S(1)}, bf16[96,640]{1,0:T(8,128)(2,1)S(1)}, bf16[96,640]{1,0:T(8,128)(2,1)S(1)}, ...) custom-call(bf16[96,640]{1,0:T(8,128)(2,1)S(1)} %get-tuple-element.62.refs_0_, ...), custom_call_target="tpu_custom_call" | custom-call | flops 1887436800 | bytes 3276800 | tf_op jit(solution)/shard_map/chunk/pallas_call | solution.py:313
  34.6 1.6 %collective-permute-start.8 = (bf16[96,640]{1,0:T(8,128)(2,1)S(1)}, bf16[96,640]{1,0:T(8,128)(2,1)S(1)}, u32[]{:S(2)}, u32[]{:S(2)}) collective-permute-start(bf16[96,640]{1,0:T(8,128)(2,1)S(1)} %get-tuple-element.34), channel_id=1, source_target_pairs={{0,24},{8,16},{16,8},{24,0},{1,25},{9,17},{17,9},{25,1},{2,26},{10... | collective-permute-start | bytes 368648 | tf_op jit(solution)/shard_map/ppermute | solution.py:198
  36.1 0.5 collective-permute-start.7
  36.6 1.5 %collective-permute-start.6 = (bf16[96,640]{1,0:T(8,128)(2,1)S(1)}, bf16[96,640]{1,0:T(8,128)(2,1)S(1)}, u32[]{:S(2)}, u32[]{:S(2)}) collective-permute-start(bf16[96,640]{1,0:T(8,128)(2,1)S(1)} %get-tuple-element.32), channel_id=1, source_target_pairs={{0,8},{8,0},{16,24},{24,16},{1,9},{9,1},{17,25},{25,17},{2,10},{10... | collective-permute-start | bytes 368648 | tf_op jit(solution)/shard_map/ppermute | solution.py:198
  38.1 0.0 collective-permute-done.13.refs_2_
  38.1 0.0 collective-permute-done.15.refs_5_
  38.1 2.7 %chunk.3 = (bf16[96,640]{1,0:T(8,128)(2,1)S(1)}, bf16[96,640]{1,0:T(8,128)(2,1)S(1)}, bf16[96,640]{1,0:T(8,128)(2,1)S(1)}, bf16[96,640]{1,0:T(8,128)(2,1)S(1)}, ...) custom-call(bf16[96,640]{1,0:T(8,128)(2,1)S(1)} %get-tuple-element.52.refs_0_, ...), custom_call_target="tpu_custom_call" | custom-call | flops 1887436800 | bytes 3276800 | tf_op jit(solution)/shard_map/chunk/pallas_call | solution.py:313
  40.8 0.6 %collective-permute-start.16 = (bf16[96,640]{1,0:T(8,128)(2,1)S(1)}, bf16[96,640]{1,0:T(8,128)(2,1)S(1)}, u32[]{:S(2)}, u32[]{:S(2)}) collective-permute-start(bf16[96,640]{1,0:T(8,128)(2,1)S(1)} %get-tuple-element.36), channel_id=1, source_target_pairs={{0,8},{8,0},{16,24},{24,16},{1,9},{9,1},{17,25},{25,17},{2,10},{10... | collective-permute-start | bytes 368648 | tf_op jit(solution)/shard_map/ppermute | solution.py:198
  41.4 1.5 %collective-permute-start.17 = (bf16[96,640]{1,0:T(8,128)(2,1)S(1)}, bf16[96,640]{1,0:T(8,128)(2,1)S(1)}, u32[]{:S(2)}, u32[]{:S(2)}) collective-permute-start(bf16[96,640]{1,0:T(8,128)(2,1)S(1)} %get-tuple-element.37), channel_id=1, source_target_pairs={{0,16},{8,24},{16,0},{24,8},{1,17},{9,25},{17,1},{25,9},{2,18},{10... | collective-permute-start | bytes 368648 | tf_op jit(solution)/shard_map/ppermute | solution.py:198
  43.0 0.0 collective-permute-done.8
  43.0 1.4 %collective-permute-start.18 = (bf16[96,640]{1,0:T(8,128)(2,1)S(1)}, bf16[96,640]{1,0:T(8,128)(2,1)S(1)}, u32[]{:S(2)}, u32[]{:S(2)}) collective-permute-start(bf16[96,640]{1,0:T(8,128)(2,1)S(1)} %get-tuple-element.38), channel_id=1, source_target_pairs={{0,24},{8,16},{16,8},{24,0},{1,25},{9,17},{17,9},{25,1},{2,26},{10... | collective-permute-start | bytes 368648 | tf_op jit(solution)/shard_map/ppermute | solution.py:198
  44.4 0.0 collective-permute-done.7
  44.4 0.0 collective-permute-done.6
  44.4 0.1 add_convert_fusion.refs_4_
  44.5 2.7 %collective-permute-start.9 = (bf16[48,640]{1,0:T(8,128)(2,1)S(1)}, bf16[48,640]{1,0:T(8,128)(2,1)S(1)}, u32[]{:S(2)}, u32[]{:S(2)}) collective-permute-start(bf16[48,640]{1,0:T(8,128)(2,1)S(1)} %get-tuple-element.65), channel_id=1, source_target_pairs={{0,2},{1,3},{2,0},{3,1},{4,6},{5,7},{6,4},{7,5},{8,10},{9,11},{10,... | collective-permute-start | bytes 184328 | tf_op jit(solution)/shard_map/ppermute | solution.py:198
  47.2 2.7 %weight_in_grad.1 = (bf16[640,1280]{1,0:T(8,128)(2,1)}, bf16[16,128]{1,0:T(8,128)(2,1)S(1)}) custom-call(bf16[384,1280]{1,0:T(8,128)(2,1)S(1)} %get-tuple-element.39.refs_0_, bf16[384,1280]{1,0:T(8,128)(2,1)S(1)} %get-tuple-element.40.refs_1_, bf16[384,1280]{1,0:T(8,128)(2,1)S(1)} %get-tuple-element.41.refs_2_, ...), custom_call_target="tpu_custom_call" | custom-call | flops 1258291200 | bytes 1638400 | tf_op jit(solution)/shard_map/weight_in_grad/pallas_call | solution.py:268
  49.8 0.0 collective-permute-done.16.refs_1_
  49.8 0.0 collective-permute-done.17.refs_2_
  49.8 0.0 collective-permute-done.18.refs_3_
  49.8 0.1 sum.1.refs_4_
  49.9 2.5 %collective-permute-start.19 = (bf16[48,640]{1,0:T(8,128)(2,1)S(1)}, bf16[48,640]{1,0:T(8,128)(2,1)S(1)}, u32[]{:S(2)}, u32[]{:S(2)}) collective-permute-start(bf16[48,640]{1,0:T(8,128)(2,1)S(1)} %get-tuple-element.64), channel_id=1, source_target_pairs={{0,4},{1,5},{2,6},{3,7},{4,0},{5,1},{6,2},{7,3},{8,12},{9,13},{10,... | collective-permute-start | bytes 184328 | tf_op jit(solution)/shard_map/ppermute | solution.py:198
  52.4 1.4 %collective-permute-start.20 = (bf16[48,640]{1,0:T(8,128)(2,1)S(1)}, bf16[48,640]{1,0:T(8,128)(2,1)S(1)}, u32[]{:S(2)}, u32[]{:S(2)}) collective-permute-start(bf16[48,640]{1,0:T(8,128)(2,1)S(1)} %get-tuple-element.63), channel_id=1, source_target_pairs={{0,6},{1,7},{2,4},{3,5},{4,2},{5,3},{6,0},{7,1},{8,14},{9,15},{10,... | collective-permute-start | bytes 184328 | tf_op jit(solution)/shard_map/ppermute | solution.py:198
  53.8 0.0 copy-start
  53.8 0.0 copy-start.1
  53.8 0.0 copy-start.2
  53.8 2.9 %weight_out_grad.1 = (bf16[1280,640]{1,0:T(8,128)(2,1)}, bf16[16,128]{1,0:T(8,128)(2,1)S(1)}) custom-call(bf16[384,1280]{1,0:T(8,128)(2,1)S(1)} %get-tuple-element.39.refs_0_, bf16[384,1280]{1,0:T(8,128)(2,1)S(1)} %get-tuple-element.40.refs_1_, bf16[384,1280]{1,0:T(8,128)(2,1)S(1)} %get-tuple-element.44.refs_2_, ...), custom_call_target="tpu_custom_call" | custom-call | flops 1258291200 | bytes 1638400 | tf_op jit(solution)/shard_map/weight_out_grad/pallas_call | solution.py:276
  56.7 0.0 collective-permute-done.9.refs_1_
  56.7 0.0 collective-permute-done.19.refs_2_
  56.7 1.7 %collective-permute-done.20.refs_3_ = bf16[48,640]{1,0:T(8,128)(2,1)S(1)} collective-permute-done((bf16[48,640]{1,0:T(8,128)(2,1)S(1)}, bf16[48,640]{1,0:T(8,128)(2,1)S(1)}, u32[]{:S(2)}, u32[]{:S(2)}) %collective-permute-start.20) | collective-permute-done | bytes 61472 | tf_op jit(solution)/shard_map/ppermute | solution.py:198
  58.5 0.1 collective-permute-start.21
  58.5 1.3 %collective-permute-done.21.other_ref = bf16[96,640]{1,0:T(8,128)(2,1)S(1)} collective-permute-done((bf16[96,640]{1,0:T(8,128)(2,1)S(1)}, bf16[96,640]{1,0:T(8,128)(2,1)S(1)}, u32[]{:S(2)}, u32[]{:S(2)}) %collective-permute-start.21) | collective-permute-done | bytes 122912 | tf_op jit(solution)/shard_map/ppermute | solution.py:198
  59.9 0.0 copy-done
  59.9 0.0 copy-done.1
  59.9 0.0 copy-done.2
  59.9 1.0 %combine.1 = bf16[128,640]{1,0:T(8,128)(2,1)} custom-call(bf16[96,640]{1,0:T(8,128)(2,1)S(1)} %get-tuple-element.47.own_ref, bf16[96,640]{1,0:T(8,128)(2,1)S(1)} %collective-permute-done.21.other_ref, s32[2,128]{1,0:T(2,128)S(1)} %bitcast.9, s32[2,128]{1,0:T(2,128)S(1)} %bitcast.11, s32[2,128]{1,0:T(2,128)S(1)} %bitcast.13), custom_call_target="tpu_custom_call" | custom-call | tf_op jit(solution)/shard_map/combine/pallas_call | solution.py:374
  (17 shorter events, 0.3 us)
Async XLA Ops:
  2.0 1.7 %collective-permute-start = (bf16[96,1280]{1,0:T(8,128)(2,1)S(1)}, bf16[96,1280]{1,0:T(8,128)(2,1)S(1)}, u32[]{:S(2)}, u32[]{:S(2)}) collective-permute-start(bf16[96,1280]{1,0:T(8,128)(2,1)S(1)} %get-tuple-element.28), channel_id=1, source_target_pairs={{0,1},{1,0},{2,3},{3,2},{4,5},{5,4},{6,7},{7,6},{8,9},{9,8},{10,11... | collective-permute-start | bytes 737288 | tf_op jit(solution)/shard_map/ppermute | solution.py:198
  3.7 8.2 %collective-permute-start.1 = (bf16[48,1280]{1,0:T(8,128)(2,1)S(1)}, bf16[48,1280]{1,0:T(8,128)(2,1)S(1)}, u32[]{:S(2)}, u32[]{:S(2)}) collective-permute-start(bf16[48,1280]{1,0:T(8,128)(2,1)S(1)} %pad_maximum_fusion.5), channel_id=1, source_target_pairs={{0,2},{1,3},{2,0},{3,1},{4,6},{5,7},{6,4},{7,5},{8,10},{9,11},{10,... | collective-permute-start | bytes 368648 | tf_op jit(solution)/shard_map/ppermute | solution.py:198
  6.7 12.4 %collective-permute-start.10 = (bf16[48,1280]{1,0:T(8,128)(2,1)S(1)}, bf16[48,1280]{1,0:T(8,128)(2,1)S(1)}, u32[]{:S(2)}, u32[]{:S(2)}) collective-permute-start(bf16[48,1280]{1,0:T(8,128)(2,1)S(1)} %pad_maximum_fusion.6), channel_id=1, source_target_pairs={{0,4},{1,5},{2,6},{3,7},{4,0},{5,1},{6,2},{7,3},{8,12},{9,13},{10,... | collective-permute-start | bytes 368648 | tf_op jit(solution)/shard_map/ppermute | solution.py:198
  9.4 9.8 %collective-permute-start.11 = (bf16[48,1280]{1,0:T(8,128)(2,1)S(1)}, bf16[48,1280]{1,0:T(8,128)(2,1)S(1)}, u32[]{:S(2)}, u32[]{:S(2)}) collective-permute-start(bf16[48,1280]{1,0:T(8,128)(2,1)S(1)} %pad_maximum_fusion.7), channel_id=1, source_target_pairs={{0,6},{1,7},{2,4},{3,5},{4,2},{5,3},{6,0},{7,1},{8,14},{9,15},{10,... | collective-permute-start | bytes 368648 | tf_op jit(solution)/shard_map/ppermute | solution.py:198
  12.0 10.3 %collective-permute-start.2 = (bf16[96,640]{1,0:T(8,128)(2,1)S(1)}, bf16[96,640]{1,0:T(8,128)(2,1)S(1)}, u32[]{:S(2)}, u32[]{:S(2)}) collective-permute-start(bf16[96,640]{1,0:T(8,128)(2,1)S(1)} %get-tuple-element.62.refs_0_), channel_id=1, source_target_pairs={{0,8},{8,0},{16,24},{24,16},{1,9},{9,1},{17,25},{25,17},{2,10},{10... | collective-permute-start | bytes 368648 | tf_op jit(solution)/shard_map/ppermute | solution.py:198
  13.7 9.1 %collective-permute-start.4 = (bf16[96,640]{1,0:T(8,128)(2,1)S(1)}, bf16[96,640]{1,0:T(8,128)(2,1)S(1)}, u32[]{:S(2)}, u32[]{:S(2)}) collective-permute-start(bf16[96,640]{1,0:T(8,128)(2,1)S(1)} %get-tuple-element.61.refs_3_), channel_id=1, source_target_pairs={{0,16},{8,24},{16,0},{24,8},{1,17},{9,25},{17,1},{25,9},{2,18},{10... | collective-permute-start | bytes 368648 | tf_op jit(solution)/shard_map/ppermute | solution.py:198
  19.2 6.3 %collective-permute-start.12 = (bf16[96,640]{1,0:T(8,128)(2,1)S(1)}, bf16[96,640]{1,0:T(8,128)(2,1)S(1)}, u32[]{:S(2)}, u32[]{:S(2)}) collective-permute-start(bf16[96,640]{1,0:T(8,128)(2,1)S(1)} %get-tuple-element.52.refs_0_), channel_id=1, source_target_pairs={{0,8},{8,0},{16,24},{24,16},{1,9},{9,1},{17,25},{25,17},{2,10},{10... | collective-permute-start | bytes 368648 | tf_op jit(solution)/shard_map/ppermute | solution.py:198
  20.8 6.3 %collective-permute-start.14 = (bf16[96,640]{1,0:T(8,128)(2,1)S(1)}, bf16[96,640]{1,0:T(8,128)(2,1)S(1)}, u32[]{:S(2)}, u32[]{:S(2)}) collective-permute-start(bf16[96,640]{1,0:T(8,128)(2,1)S(1)} %get-tuple-element.51.refs_3_), channel_id=1, source_target_pairs={{0,16},{8,24},{16,0},{24,8},{1,17},{9,25},{17,1},{25,9},{2,18},{10... | collective-permute-start | bytes 368648 | tf_op jit(solution)/shard_map/ppermute | solution.py:198
  22.3 9.3 %collective-permute-start.3 = (bf16[192,640]{1,0:T(8,128)(2,1)S(1)}, bf16[192,640]{1,0:T(8,128)(2,1)S(1)}, u32[]{:S(2)}, u32[]{:S(2)}) collective-permute-start(bf16[192,640]{1,0:T(8,128)(2,1)S(1)} %pad_maximum_fusion.1), channel_id=1, source_target_pairs={{0,16},{8,24},{16,0},{24,8},{1,17},{9,25},{17,1},{25,9},{2,18},{10... | collective-permute-start | bytes 737288 | tf_op jit(solution)/shard_map/ppermute | solution.py:198
  22.9 9.0 %collective-permute-start.5 = (bf16[192,640]{1,0:T(8,128)(2,1)S(1)}, bf16[192,640]{1,0:T(8,128)(2,1)S(1)}, u32[]{:S(2)}, u32[]{:S(2)}) collective-permute-start(bf16[192,640]{1,0:T(8,128)(2,1)S(1)} %pad_maximum_fusion.2), channel_id=1, source_target_pairs={{0,8},{8,0},{16,24},{24,16},{1,9},{9,1},{17,25},{25,17},{2,10},{10... | collective-permute-start | bytes 737288 | tf_op jit(solution)/shard_map/ppermute | solution.py:198
  25.5 12.6 %collective-permute-start.13 = (bf16[192,640]{1,0:T(8,128)(2,1)S(1)}, bf16[192,640]{1,0:T(8,128)(2,1)S(1)}, u32[]{:S(2)}, u32[]{:S(2)}) collective-permute-start(bf16[192,640]{1,0:T(8,128)(2,1)S(1)} %pad_maximum_fusion.3), channel_id=1, source_target_pairs={{0,16},{8,24},{16,0},{24,8},{1,17},{9,25},{17,1},{25,9},{2,18},{10... | collective-permute-start | bytes 737288 | tf_op jit(solution)/shard_map/ppermute | solution.py:198
  27.1 11.0 %collective-permute-start.15 = (bf16[192,640]{1,0:T(8,128)(2,1)S(1)}, bf16[192,640]{1,0:T(8,128)(2,1)S(1)}, u32[]{:S(2)}, u32[]{:S(2)}) collective-permute-start(bf16[192,640]{1,0:T(8,128)(2,1)S(1)} %pad_maximum_fusion.4), channel_id=1, source_target_pairs={{0,8},{8,0},{16,24},{24,16},{1,9},{9,1},{17,25},{25,17},{2,10},{10... | collective-permute-start | bytes 737288 | tf_op jit(solution)/shard_map/ppermute | solution.py:198
  34.6 8.4 %collective-permute-start.8 = (bf16[96,640]{1,0:T(8,128)(2,1)S(1)}, bf16[96,640]{1,0:T(8,128)(2,1)S(1)}, u32[]{:S(2)}, u32[]{:S(2)}) collective-permute-start(bf16[96,640]{1,0:T(8,128)(2,1)S(1)} %get-tuple-element.34), channel_id=1, source_target_pairs={{0,24},{8,16},{16,8},{24,0},{1,25},{9,17},{17,9},{25,1},{2,26},{10... | collective-permute-start | bytes 368648 | tf_op jit(solution)/shard_map/ppermute | solution.py:198
  36.1 8.3 %collective-permute-start.7 = (bf16[96,640]{1,0:T(8,128)(2,1)S(1)}, bf16[96,640]{1,0:T(8,128)(2,1)S(1)}, u32[]{:S(2)}, u32[]{:S(2)}) collective-permute-start(bf16[96,640]{1,0:T(8,128)(2,1)S(1)} %get-tuple-element.33), channel_id=1, source_target_pairs={{0,16},{8,24},{16,0},{24,8},{1,17},{9,25},{17,1},{25,9},{2,18},{10... | collective-permute-start | bytes 368648 | tf_op jit(solution)/shard_map/ppermute | solution.py:198
  36.6 7.7 %collective-permute-start.6 = (bf16[96,640]{1,0:T(8,128)(2,1)S(1)}, bf16[96,640]{1,0:T(8,128)(2,1)S(1)}, u32[]{:S(2)}, u32[]{:S(2)}) collective-permute-start(bf16[96,640]{1,0:T(8,128)(2,1)S(1)} %get-tuple-element.32), channel_id=1, source_target_pairs={{0,8},{8,0},{16,24},{24,16},{1,9},{9,1},{17,25},{25,17},{2,10},{10... | collective-permute-start | bytes 368648 | tf_op jit(solution)/shard_map/ppermute | solution.py:198
  40.8 9.0 %collective-permute-start.16 = (bf16[96,640]{1,0:T(8,128)(2,1)S(1)}, bf16[96,640]{1,0:T(8,128)(2,1)S(1)}, u32[]{:S(2)}, u32[]{:S(2)}) collective-permute-start(bf16[96,640]{1,0:T(8,128)(2,1)S(1)} %get-tuple-element.36), channel_id=1, source_target_pairs={{0,8},{8,0},{16,24},{24,16},{1,9},{9,1},{17,25},{25,17},{2,10},{10... | collective-permute-start | bytes 368648 | tf_op jit(solution)/shard_map/ppermute | solution.py:198
  41.4 8.4 %collective-permute-start.17 = (bf16[96,640]{1,0:T(8,128)(2,1)S(1)}, bf16[96,640]{1,0:T(8,128)(2,1)S(1)}, u32[]{:S(2)}, u32[]{:S(2)}) collective-permute-start(bf16[96,640]{1,0:T(8,128)(2,1)S(1)} %get-tuple-element.37), channel_id=1, source_target_pairs={{0,16},{8,24},{16,0},{24,8},{1,17},{9,25},{17,1},{25,9},{2,18},{10... | collective-permute-start | bytes 368648 | tf_op jit(solution)/shard_map/ppermute | solution.py:198
  43.0 6.9 %collective-permute-start.18 = (bf16[96,640]{1,0:T(8,128)(2,1)S(1)}, bf16[96,640]{1,0:T(8,128)(2,1)S(1)}, u32[]{:S(2)}, u32[]{:S(2)}) collective-permute-start(bf16[96,640]{1,0:T(8,128)(2,1)S(1)} %get-tuple-element.38), channel_id=1, source_target_pairs={{0,24},{8,16},{16,8},{24,0},{1,25},{9,17},{17,9},{25,1},{2,26},{10... | collective-permute-start | bytes 368648 | tf_op jit(solution)/shard_map/ppermute | solution.py:198
  44.5 12.2 %collective-permute-start.9 = (bf16[48,640]{1,0:T(8,128)(2,1)S(1)}, bf16[48,640]{1,0:T(8,128)(2,1)S(1)}, u32[]{:S(2)}, u32[]{:S(2)}) collective-permute-start(bf16[48,640]{1,0:T(8,128)(2,1)S(1)} %get-tuple-element.65), channel_id=1, source_target_pairs={{0,2},{1,3},{2,0},{3,1},{4,6},{5,7},{6,4},{7,5},{8,10},{9,11},{10,... | collective-permute-start | bytes 184328 | tf_op jit(solution)/shard_map/ppermute | solution.py:198
  49.9 6.8 %collective-permute-start.19 = (bf16[48,640]{1,0:T(8,128)(2,1)S(1)}, bf16[48,640]{1,0:T(8,128)(2,1)S(1)}, u32[]{:S(2)}, u32[]{:S(2)}) collective-permute-start(bf16[48,640]{1,0:T(8,128)(2,1)S(1)} %get-tuple-element.64), channel_id=1, source_target_pairs={{0,4},{1,5},{2,6},{3,7},{4,0},{5,1},{6,2},{7,3},{8,12},{9,13},{10,... | collective-permute-start | bytes 184328 | tf_op jit(solution)/shard_map/ppermute | solution.py:198
  52.4 6.0 %collective-permute-start.20 = (bf16[48,640]{1,0:T(8,128)(2,1)S(1)}, bf16[48,640]{1,0:T(8,128)(2,1)S(1)}, u32[]{:S(2)}, u32[]{:S(2)}) collective-permute-start(bf16[48,640]{1,0:T(8,128)(2,1)S(1)} %get-tuple-element.63), channel_id=1, source_target_pairs={{0,6},{1,7},{2,4},{3,5},{4,2},{5,3},{6,0},{7,1},{8,14},{9,15},{10,... | collective-permute-start | bytes 184328 | tf_op jit(solution)/shard_map/ppermute | solution.py:198
  53.8 6.1 %copy-start = (s32[128,2]{0,1:T(2,128)S(1)}, s32[128,2]{0,1:T(2,128)}, u32[]{:S(2)}) copy-start(s32[128,2]{0,1:T(2,128)} %param.11) | copy-start | bytes 3076
  53.8 6.1 %copy-start.1 = (s32[128,2]{0,1:T(2,128)S(1)}, s32[128,2]{0,1:T(2,128)}, u32[]{:S(2)}) copy-start(s32[128,2]{0,1:T(2,128)} %param.12) | copy-start | bytes 3076
  53.8 6.1 %copy-start.2 = (s32[128,2]{0,1:T(2,128)S(1)}, s32[128,2]{0,1:T(2,128)}, u32[]{:S(2)}) copy-start(s32[128,2]{0,1:T(2,128)} %param.13) | copy-start | bytes 3076
  58.5 1.4 %collective-permute-start.21 = (bf16[96,640]{1,0:T(8,128)(2,1)S(1)}, bf16[96,640]{1,0:T(8,128)(2,1)S(1)}, u32[]{:S(2)}, u32[]{:S(2)}) collective-permute-start(bf16[96,640]{1,0:T(8,128)(2,1)S(1)} %get-tuple-element.48), channel_id=1, source_target_pairs={{0,1},{1,0},{2,3},{3,2},{4,5},{5,4},{6,7},{7,6},{8,9},{9,8},{10,11... | collective-permute-start | bytes 368648 | tf_op jit(solution)/shard_map/ppermute | solution.py:198

commit v3 on v2

--- a/solution.py
+++ b/solution.py
@@ -12,13 +12,20 @@
 vmem_whole = pl.BlockSpec(memory_space=pltpu.VMEM)
 anywhere = pl.BlockSpec(memory_space=pl.ANY)
 f32 = jnp.float32
-CHUNKS = (((0, 1),), ((2, 3),))
-DIRECT = (True, True)
-LANES = ((True,), (True,))
-AFTER = (0, -1)
+CHUNKS = (((0,), (1,)), ((2,), (3,)))
+DIRECT = (False, True)
 TILE = 1280
+C_CHUNK = 1.0
+C_LOAD = 1.0
+C_W = 1.0
 LOAD = None
-GATE = False
+WAIT_Z = False
+DEFER = 1
+HOLD = False
+EARLY_LOAD = False
+FIRST_LOAD = True
+HOLD2 = 0
+Z3 = False
 bf16 = jnp.bfloat16
 
 
@@ -82,24 +89,6 @@
     out_ref[...] = total.astype(bf16)
 
 
-def gathered_order(bits):
-    order = [0]
-    steps = []
-    for bit in bits:
-        steps.append([o ^ bit for o in order])
-        order = order + steps[-1]
-    return steps
-
-
-def scattered_order(bits, groups):
-    left = list(range(groups))
-    steps = []
-    for bit in bits:
-        steps.append([o for o in left if o & bit])
-        left = [o for o in left if not o & bit]
-    return steps
-
-
 def load_kernel(*refs):
     sources, targets, sem = refs[:2], refs[-3:-1], refs[-1]
     copies = [pltpu.make_async_copy(a, b, sem.at[i]) for i, (a, b) in enumerate(zip(sources, targets, strict=True))]
@@ -109,16 +98,17 @@
         copy.wait()
 
 
-def chunk_kernel(tile, groups, cuts, places, *refs):
+def chunk_kernel(tile, groups, levels, places, *refs):
     moved, refs = refs[: len(places)], refs[len(places) :]
     (win_ref, wout_ref), outs = refs[:2], refs[2:]
     sends, kept_ref = outs[:-5], outs[-5]
     rows_ref, hidden_ref, pre_ref, acc_ref = outs[-4:]
     width, hidden_total = win_ref.shape
     count = rows_ref.shape[0] // groups
-    for ref, (start, size, low, high, offsets) in zip(moved, places, strict=True):
-        for i, o in enumerate(offsets):
-            rows_ref[o * count + start : o * count + start + size, low:high] = ref[i * size : (i + 1) * size, :]
+    for ref, (start, size, first) in zip(moved, places, strict=True):
+        for i in range(ref.shape[0] // size):
+            at = (first + i) * count + start
+            rows_ref[at : at + size, :] = ref[i * size : (i + 1) * size, :]
     for base in range(0, hidden_total, tile):
         cols = slice(base, base + tile)
         preact = jnp.dot(rows_ref[:, :width], win_ref[:, cols], preferred_element_type=f32)
@@ -142,11 +132,8 @@
         else:
             acc_ref[...] += term
     kept_ref[...] = acc_ref[:count, :].astype(bf16)
-    for (low, high, offsets), ref in zip(cuts, sends, strict=True):
-        for i, o in enumerate(offsets):
-            ref[i * (high - low) : (i + 1) * (high - low), :] = acc_ref[o * count + low : o * count + high, :].astype(
-                bf16
-            )
+    for (low, high), ref in zip(levels, sends, strict=True):
+        ref[...] = acc_ref[low * count : high * count, :].astype(bf16)
 
 
 def stacked(refs, cols):
@@ -170,6 +157,36 @@
     done_ref[...] = jnp.zeros(done_ref.shape, bf16)
 
 
+def join_kernel(count, *refs):
+    start = 0
+    for ref in refs[:count]:
+        refs[-1][start : start + ref.shape[0], :] = ref[...]
+        start += ref.shape[0]
+
+
+def join(values, after):
+    rows = sum(v.shape[0] for v in values)
+    return pl.pallas_call(
+        functools.partial(join_kernel, len(values)),
+        out_shape=vmem_out((rows, values[0].shape[1])),
+        in_specs=[vmem_whole] * len(values) + [anywhere] * len(after),
+        out_specs=vmem_whole,
+        compiler_params=params(16),
+        name="join",
+    )(*values, *after)
+
+
+def add_rows(values, after):
+    return pl.pallas_call(
+        sum_kernel,
+        out_shape=vmem_out(values[0].shape),
+        in_specs=[vmem_whole] * len(values) + [anywhere],
+        out_specs=vmem_whole,
+        compiler_params=params(16),
+        name="sum",
+    )(*values, after)
+
+
 def sum_kernel(*refs):
     total = refs[0][...].astype(f32)
     for ref in refs[1:-2]:
@@ -185,17 +202,17 @@
         ref[...] = rows[:, part].reshape(ref.shape).astype(bf16)
 
 
-def added(value, offsets, received, size):
-    total = value.astype(f32)
-    for held, part in received:
-        at = [held.index(o) * size for o in offsets]
-        total = total + jnp.concatenate([part[i : i + size] for i in at], axis=0).astype(f32)
-    return total.astype(bf16)
-
-
 def swap(value, axis, offset):
     size = lax.axis_size(axis)
     return lax.ppermute(value, axis, [(i, i ^ offset) for i in range(size)])
+
+
+def swap_groups(value, position):
+    groups, owners = lax.axis_size("dp"), lax.axis_size("expert")
+    bits = [1 << i for i in range(groups.bit_length() - 1)]
+    offsets = [sum(b for i, b in enumerate(order) if position >> i & 1) for order in (bits, bits[::-1])]
+    pairs = [(d * owners + e, (d ^ offsets[e & 1]) * owners + e) for d in range(groups) for e in range(owners)]
+    return lax.ppermute(value, ("dp", "expert"), pairs)
 
 
 def body(
@@ -235,6 +252,8 @@
     for m in range(chips):
         span = slice(m * slot_cap, (m + 1) * slot_cap)
         rows = jnp.concatenate([own[span], got[span]], axis=0)
+        if Z3 and m == chips - 1:
+            rows = join([rows], [arrived[1]])
         arrived.append(rows if m == 0 else swap(rows, "expert", 2 * m))
 
     quarter = chips // 4
@@ -242,9 +261,7 @@
     chunk_count = len(chunks)
     returned = [None] * chips
     all_rows, all_hidden, all_pre = [], [], []
-    bits = [1 << i for i in range(groups.bit_length() - 1)]
-    lanes = (bits, bits[::-1])
-    steps = len(bits)
+    steps = groups.bit_length() - 1
     weights = pl.pallas_call(
         load_kernel,
         out_shape=(vmem_out(win.shape), vmem_out(wout.shape)),
@@ -252,7 +269,7 @@
         out_specs=(vmem_whole,) * 2,
         scratch_shapes=[pltpu.SemaphoreType.DMA((2,))],
         compiler_params=params(16),
-        cost_estimate=cost(0, 8 * width * hidden_total),
+        cost_estimate=cost(0, int(C_LOAD * 8 * width * hidden_total)),
         name="load",
     )(in_hbm(win), in_hbm(wout), got if LOAD is None else arrived[LOAD * quarter])
     sums_of = []
@@ -261,7 +278,7 @@
         in_specs=[vmem_whole] * (2 * chunk_count) + [anywhere],
         out_specs=(vmem_whole,) * 2,
         compiler_params=params(40),
-        cost_estimate=cost(2 * all_count * width * hidden_total, 2 * width * hidden_total),
+        cost_estimate=cost(int(C_W * 2 * all_count * width * hidden_total), int(C_W * 2 * width * hidden_total)),
     )
 
     def weight_in_call(after):
@@ -280,39 +297,40 @@
             **weight_call,
         )(*all_rows, *all_hidden, after)
 
+    deferred = []
     for number, chunk in enumerate(chunks):
         moved, places, start = [], [], 0
-        for by_lanes, group in zip(LANES[number], chunk, strict=True):
-            mine = jnp.concatenate([arrived[m] for m in group], axis=0)
-            size = mine.shape[0]
-            if by_lanes:
-                for lane in range(2):
-                    held, low = [mine[:, lane * width : (lane + 1) * width]], lane * width
-                    orders = [[0]] + gathered_order(lanes[lane])
-                    for step in range(steps):
-                        held.append(swap(jnp.concatenate(held, axis=0), "dp", lanes[lane][step]))
-                    moved += held
-                    places += [(start, size, low, low + width, offsets) for offsets in orders]
-            else:
-                for o in range(groups):
-                    moved.append(swap(mine, "dp", o) if o else mine)
-                    places.append((start, size, 0, 2 * width, [o]))
+        for group in chunk:
+            held = [jnp.concatenate([arrived[m] for m in group], axis=0)]
+            size = held[0].shape[0]
+            if HOLD and number:
+                held = [join(held, early)]
+            if EARLY_LOAD and not number and group is chunk[-1]:
+                held = [join(held, weights[:1])]
+            if FIRST_LOAD and not number and group is chunk[0]:
+                held = [join(held, weights[:1])]
+            if HOLD2 and number:
+                held = [join(held, first[1 : HOLD2 + 1])]
+            for step in range(steps):
+                after = [arrived[m] for group in chunks[-1] for m in group] if WAIT_Z and not number and step else []
+                both = join(held, after) if after else jnp.concatenate(held, axis=0)
+                held.append(swap_groups(both, 1 << step))
+            early = [held[1]]
+            if not number and group is chunk[0]:
+                first = held
+            moved += held
+            places += [(start, size, 0)] + [(start, size, 1 << step) for step in range(steps)]
             start += size
         inside = [m for group in chunk for m in group]
         count = len(inside) * block
         total = groups * count
-        cut = count // 32 * 16
         if DIRECT[number]:
-            cuts = [(0, count, [o]) for o in range(1, groups)]
+            levels = [(p, p + 1) for p in range(1, groups)]
         else:
-            cuts = [
-                (low, high, offsets)
-                for lane, (low, high) in zip(lanes, ((0, cut), (cut, count)), strict=True)
-                for offsets in scattered_order(lane, groups)
-            ]
+            levels = [(1 << step, 2 << step) for step in reversed(range(steps))]
         outs = pl.pallas_call(
-            functools.partial(chunk_kernel, TILE, groups, cuts, places),
-            out_shape=tuple(vmem_out((len(offsets) * (high - low), width)) for low, high, offsets in cuts)
+            functools.partial(chunk_kernel, TILE, groups, levels, places),
+            out_shape=tuple(vmem_out(((high - low) * count, width)) for low, high in levels)
             + (
                 vmem_out((count, width)),
                 vmem_out((total, 2 * width)),
@@ -320,43 +338,42 @@
                 vmem_out((total, hidden_total)),
             ),
             in_specs=[vmem_whole] * (len(moved) + 2),
-            out_specs=(vmem_whole,) * (len(cuts) + 4),
+            out_specs=(vmem_whole,) * (len(levels) + 4),
             scratch_shapes=[pltpu.VMEM((total, width), f32)],
             compiler_params=params(32),
-            cost_estimate=cost(6 * total * width * hidden_total, 4 * width * hidden_total, total * hidden_total),
+            cost_estimate=cost(int(C_CHUNK * 6 * total * width * hidden_total), int(C_CHUNK * 4 * width * hidden_total), int(C_CHUNK * total * hidden_total)),
             name="chunk",
         )(*moved, *weights)
         sends, (kept, rows_all, hidden, pre) = outs[:-4], outs[-4:]
         all_rows.append(rows_all)
         all_hidden.append(hidden)
         all_pre.append(pre)
+        deferred.append((inside, count, levels, sends, kept))
+
+    def reduced(number, after):
+        inside, count, levels, sends, kept = deferred[number]
+        terms = [kept]
         if DIRECT[number]:
-            terms = [kept] + [swap(v, "dp", offsets[0]) for (_, _, offsets), v in zip(cuts, sends, strict=True)]
-            if number == len(chunks) - 1:
-                grad_in, done = weight_in_call(sums_of[0])
-                summed = pl.pallas_call(
-                    sum_kernel,
-                    out_shape=vmem_out((count, width)),
-                    in_specs=[vmem_whole] * groups + [anywhere],
-                    out_specs=vmem_whole,
-                    compiler_params=params(16),
-                    name="sum",
-                )(*terms, done)
-            else:
-                summed = sum(t.astype(f32) for t in terms).astype(bf16)
+            terms += [swap_groups(value, p) for (p, _), value in zip(levels, sends, strict=True)]
         else:
-            finals = []
-            for lane, bits_of in enumerate(lanes):
-                low, high = (0, cut) if lane == 0 else (cut, count)
-                received = []
-                for step in range(steps):
-                    value, offsets = sends[lane * steps + step], cuts[lane * steps + step][2]
-                    if received:
-                        value = added(value, offsets, received, high - low)
-                    received.append(([o ^ bits_of[step] for o in offsets], swap(value, "dp", bits_of[step])))
-                finals.append(added(kept[low:high], [0], received, high - low))
-            summed = jnp.concatenate(finals, axis=0)
-        sums_of.append(summed)
+            parts = []
+            for (low, high), value in zip(levels, sends, strict=True):
+                if parts:
+                    value = add_rows([value] + [part[low * count : high * count] for part in parts], after[0])
+                elif DEFER > 1:
+                    value = join([value], after)
+                parts.append(swap_groups(value, low))
+            terms += [part if part.shape[0] == count else part[:count] for part in parts]
+        return terms
+
+    last = len(chunks) - 1
+    for number in range(last):
+        terms = reduced(number, [deferred[last if DEFER else number][-1]])
+        sums_of.append(sum(t.astype(f32) for t in terms).astype(bf16))
+    terms = reduced(last, [deferred[last][-1]])
+    grad_in, done = weight_in_call(sums_of[0])
+    sums_of.append(add_rows(terms, done))
+    for (inside, *_), summed in zip(deferred, sums_of, strict=True):
         for i, m in enumerate(inside):
             piece = summed[i * block : (i + 1) * block]
             returned[m] = piece if m == 0 else swap(piece, "expert", 2 * m)

time: 61 us -> 58.8 us (0.964)
  starting transfers between devices: 30.7 us -> 25 us
  waiting for transfers between devices: 13.8 us -> 17.4 us
    ppermute x22 -> x8, starting transfers between devices: 30.7 us -> 11.2 us  [swap(): return lax.ppermute(value, axis, [(i, i ^ offset) for i in range(size)])]
    ppermute x0 -> x13, starting transfers between devices: none -> 13.8 us  [swap_groups(): return lax.ppermute(value, ('dp', 'expert'), pairs)]
    ppermute x0 -> x13, waiting for transfers between devices: none -> 12.2 us  [swap_groups(): return lax.ppermute(value, ('dp', 'expert'), pairs)]
    ppermute x22 -> x8, waiting for transfers between devices: 13.8 us -> 5.24 us  [swap(): return lax.ppermute(value, axis, [(i, i ^ offset) for i in range(size)])]
    pallas_call x3 -> x5, Pallas kernels: 5.45 us -> 5.41 us  [the longest x2 5.3 us: body(): pl.pallas_call(functools.partial(chunk_kernel, TILE, groups, levels, plac...]
  transfers between devices with their start and end apart: 22 -> 21, of which waited for: 8 -> 12; matrix products, arithmetic and copies ran while one was open for 1% -> 0% of each run, Pallas kernels for 21% -> 22%
where the time goes in v3:
time: 58.8 us; the launch traced here: 58.7 us
  starting transfers between devices  25 us (43%)
  waiting for transfers between devices  17.4 us (30%)
  Pallas kernels  15.3 us (26%)
  between operations  0.79 us (1%)
    ppermute x13, starting transfers between devices, swap_groups(): return lax.ppermute(value, ('dp', 'expert'), pairs)  13.8 us
    ppermute x13, waiting for transfers between devices, swap_groups(): return lax.ppermute(value, ('dp', 'expert'), pairs)  12.2 us
    ppermute x8, starting transfers between devices, swap(): return lax.ppermute(value, axis, [(i, i ^ offset) for i in range(size)])  11.2 us
    pallas_call x2, Pallas kernels, body(): pl.pallas_call(functools.partial(chunk_kernel, TILE, groups, levels, plac...  5.3 us
    ppermute x8, waiting for transfers between devices, swap(): return lax.ppermute(value, axis, [(i, i ^ offset) for i in range(size)])  5.24 us
    pallas_call x1, Pallas kernels, weight_out_call(): pl.pallas_call(functools.partial(weight_out_kernel, chunk_count, width),...  2.91 us
    pallas_call x1, Pallas kernels, weight_in_call(): pl.pallas_call(functools.partial(weight_in_kernel, chunk_count, width), o...  2.66 us
    pallas_call x1, Pallas kernels, body(): pl.pallas_call(load_kernel, out_shape=(vmem_out(win.shape), vmem_out(wout...  1.94 us
  transfers between devices with their start and end apart: 21, of which 12 were waited for; matrix products, arithmetic and copies ran while one was open for 0% of the time, Pallas kernels for 22%

profile of v3, /device:TPU:0, one launch (start us, length us, event | category | flops | bytes accessed | tf_op | source)
XLA Modules:
  0.0 58.7 jit_solution(121518201947192326)
XLA Ops:
  0.6 1.3 %dispatch.1 = (bf16[96,1280]{1,0:T(8,128)(2,1)S(1)}, bf16[96,1280]{1,0:T(8,128)(2,1)S(1)}) custom-call(bf16[128,640]{1,0:T(8,128)(2,1)} %refs_0_.1, bf16[128,640]{1,0:T(8,128)(2,1)} %refs_1_.1, f32[2,128]{1,0:T(2,128)} %bitcast.16, s32[2,128]{1,0:T(2,128)} %bitcast.8, s32[2,128]{1,0:T(2,128)} %bitcast.10, s32[2,128]{1,0:T(2,128)} %bitcast.12), custom_call_target="tpu_custom_call" | custom-call | tf_op jit(solution)/shard_map/dispatch/pallas_call | solution.py:240
  2.0 0.5 collective-permute-start
  2.5 1.1 %collective-permute-done.refs_2_ = bf16[96,1280]{1,0:T(8,128)(2,1)S(1)} collective-permute-done((bf16[96,1280]{1,0:T(8,128)(2,1)S(1)}, bf16[96,1280]{1,0:T(8,128)(2,1)S(1)}, u32[]{:S(2)}, u32[]{:S(2)}) %collective-permute-start) | collective-permute-done | bytes 245792 | tf_op jit(solution)/shard_map/ppermute | solution.py:207
  3.7 3.0 %collective-permute-start.3 = (bf16[48,1280]{1,0:T(8,128)(2,1)S(1)}, bf16[48,1280]{1,0:T(8,128)(2,1)S(1)}, u32[]{:S(2)}, u32[]{:S(2)}) collective-permute-start(bf16[48,1280]{1,0:T(8,128)(2,1)S(1)} %pad_maximum_fusion.5), channel_id=1, source_target_pairs={{0,2},{1,3},{2,0},{3,1},{4,6},{5,7},{6,4},{7,5},{8,10},{9,11},{10,... | collective-permute-start | bytes 368648 | tf_op jit(solution)/shard_map/ppermute | solution.py:207
  6.7 2.7 %collective-permute-start.7 = (bf16[48,1280]{1,0:T(8,128)(2,1)S(1)}, bf16[48,1280]{1,0:T(8,128)(2,1)S(1)}, u32[]{:S(2)}, u32[]{:S(2)}) collective-permute-start(bf16[48,1280]{1,0:T(8,128)(2,1)S(1)} %pad_maximum_fusion.6), channel_id=1, source_target_pairs={{0,4},{1,5},{2,6},{3,7},{4,0},{5,1},{6,2},{7,3},{8,12},{9,13},{10,... | collective-permute-start | bytes 368648 | tf_op jit(solution)/shard_map/ppermute | solution.py:207
  9.4 1.9 %load.1 = (bf16[640,1280]{1,0:T(8,128)(2,1)S(1)}, bf16[1280,640]{1,0:T(8,128)(2,1)S(1)}) custom-call(bf16[640,1280]{1,0:T(8,128)(2,1)} %bitcast.14, bf16[1280,640]{1,0:T(8,128)(2,1)} %bitcast.15, bf16[96,1280]{1,0:T(8,128)(2,1)S(1)} %collective-permute-done.refs_2_), custom_call_target="tpu_custom_call" | custom-call | bytes 6553600 | tf_op jit(solution)/shard_map/load/pallas_call | solution.py:265
  11.3 1.6 %collective-permute-start.1 = (bf16[48,1280]{1,0:T(8,128)(2,1)S(1)}, bf16[48,1280]{1,0:T(8,128)(2,1)S(1)}, u32[]{:S(2)}, u32[]{:S(2)}) collective-permute-start(bf16[48,1280]{1,0:T(8,128)(2,1)S(1)} %join.1.refs_0_), channel_id=1, source_target_pairs={{0,8},{1,17},{2,10},{3,19},{4,12},{5,21},{6,14},{7,23},{8,0},{9,25... | collective-permute-start | bytes 368648 | tf_op jit(solution)/shard_map/ppermute | solution.py:215
  12.9 0.3 collective-permute-start.10
  13.2 0.0 collective-permute-done.3.refs_3_
  13.2 0.6 %collective-permute-start.4 = (bf16[48,1280]{1,0:T(8,128)(2,1)S(1)}, bf16[48,1280]{1,0:T(8,128)(2,1)S(1)}, u32[]{:S(2)}, u32[]{:S(2)}) collective-permute-start(bf16[48,1280]{1,0:T(8,128)(2,1)S(1)} %collective-permute-done.3.refs_3_), channel_id=1, source_target_pairs={{0,8},{1,17},{2,10},{3,19},{4,12},{5,21},{6,14},{7,23},{8,0},{9,25... | collective-permute-start | bytes 368648 | tf_op jit(solution)/shard_map/ppermute | solution.py:215
  13.8 2.5 %collective-permute-done.1.refs_1_ = bf16[48,1280]{1,0:T(8,128)(2,1)S(1)} collective-permute-done((bf16[48,1280]{1,0:T(8,128)(2,1)S(1)}, bf16[48,1280]{1,0:T(8,128)(2,1)S(1)}, u32[]{:S(2)}, u32[]{:S(2)}) %collective-permute-start.1) | collective-permute-done | bytes 122912 | tf_op jit(solution)/shard_map/ppermute | solution.py:215
  16.3 1.6 %collective-permute-start.2 = (bf16[96,1280]{1,0:T(8,128)(2,1)S(1)}, bf16[96,1280]{1,0:T(8,128)(2,1)S(1)}, u32[]{:S(2)}, u32[]{:S(2)}) collective-permute-start(bf16[96,1280]{1,0:T(8,128)(2,1)S(1)} %pad_maximum_fusion), channel_id=1, source_target_pairs={{0,16},{1,9},{2,18},{3,11},{4,20},{5,13},{6,22},{7,15},{8,24},{9,1... | collective-permute-start | bytes 737288 | tf_op jit(solution)/shard_map/ppermute | solution.py:215
  17.9 0.0 collective-permute-done.7.refs_0_
  17.9 1.5 %collective-permute-start.8 = (bf16[48,1280]{1,0:T(8,128)(2,1)S(1)}, bf16[48,1280]{1,0:T(8,128)(2,1)S(1)}, u32[]{:S(2)}, u32[]{:S(2)}) collective-permute-start(bf16[48,1280]{1,0:T(8,128)(2,1)S(1)} %collective-permute-done.7.refs_0_), channel_id=1, source_target_pairs={{0,8},{1,17},{2,10},{3,19},{4,12},{5,21},{6,14},{7,23},{8,0},{9,25... | collective-permute-start | bytes 368648 | tf_op jit(solution)/shard_map/ppermute | solution.py:215
  19.4 0.3 collective-permute-done.10.refs_3_
  19.7 1.2 %collective-permute-start.11 = (bf16[48,1280]{1,0:T(8,128)(2,1)S(1)}, bf16[48,1280]{1,0:T(8,128)(2,1)S(1)}, u32[]{:S(2)}, u32[]{:S(2)}) collective-permute-start(bf16[48,1280]{1,0:T(8,128)(2,1)S(1)} %collective-permute-done.10.refs_3_), channel_id=1, source_target_pairs={{0,8},{1,17},{2,10},{3,19},{4,12},{5,21},{6,14},{7,23},{8,0},{9,25... | collective-permute-start | bytes 368648 | tf_op jit(solution)/shard_map/ppermute | solution.py:215
  20.9 0.0 collective-permute-done.4.refs_4_
  20.9 0.9 %collective-permute-start.5 = (bf16[96,1280]{1,0:T(8,128)(2,1)S(1)}, bf16[96,1280]{1,0:T(8,128)(2,1)S(1)}, u32[]{:S(2)}, u32[]{:S(2)}) collective-permute-start(bf16[96,1280]{1,0:T(8,128)(2,1)S(1)} %pad_maximum_fusion.1), channel_id=1, source_target_pairs={{0,16},{1,9},{2,18},{3,11},{4,20},{5,13},{6,22},{7,15},{8,24},{9,1... | collective-permute-start | bytes 737288 | tf_op jit(solution)/shard_map/ppermute | solution.py:215
  21.9 2.2 %collective-permute-done.8.refs_1_ = bf16[48,1280]{1,0:T(8,128)(2,1)S(1)} collective-permute-done((bf16[48,1280]{1,0:T(8,128)(2,1)S(1)}, bf16[48,1280]{1,0:T(8,128)(2,1)S(1)}, u32[]{:S(2)}, u32[]{:S(2)}) %collective-permute-start.8) | collective-permute-done | bytes 122912 | tf_op jit(solution)/shard_map/ppermute | solution.py:215
  24.1 0.1 collective-permute-start.9
  24.2 2.5 %collective-permute-done.11.refs_4_ = bf16[48,1280]{1,0:T(8,128)(2,1)S(1)} collective-permute-done((bf16[48,1280]{1,0:T(8,128)(2,1)S(1)}, bf16[48,1280]{1,0:T(8,128)(2,1)S(1)}, u32[]{:S(2)}, u32[]{:S(2)}) %collective-permute-start.11) | collective-permute-done | bytes 122912 | tf_op jit(solution)/shard_map/ppermute | solution.py:215
  26.7 0.9 %collective-permute-start.12 = (bf16[96,1280]{1,0:T(8,128)(2,1)S(1)}, bf16[96,1280]{1,0:T(8,128)(2,1)S(1)}, u32[]{:S(2)}, u32[]{:S(2)}) collective-permute-start(bf16[96,1280]{1,0:T(8,128)(2,1)S(1)} %pad_maximum_fusion.3), channel_id=1, source_target_pairs={{0,16},{1,9},{2,18},{3,11},{4,20},{5,13},{6,22},{7,15},{8,24},{9,1... | collective-permute-start | bytes 737288 | tf_op jit(solution)/shard_map/ppermute | solution.py:215
  27.6 0.0 collective-permute-done.2.refs_2_
  27.6 0.0 collective-permute-done.5.refs_5_
  27.6 2.6 %chunk.2 = (bf16[192,640]{1,0:T(8,128)(2,1)S(1)}, bf16[96,640]{1,0:T(8,128)(2,1)S(1)}, bf16[96,640]{1,0:T(8,128)(2,1)S(1)}, bf16[384,1280]{1,0:T(8,128)(2,1)S(1)...) custom-call(bf16[48,1280]{1,0:T(8,128)(2,1)S(1)} %join.1.refs_0_, ...), custom_call_target="tpu_custom_call" | custom-call | flops 1887436800 | bytes 3276800 | tf_op jit(solution)/shard_map/chunk/pallas_call | solution.py:331
  30.3 1.3 %collective-permute-start.6 = (bf16[192,640]{1,0:T(8,128)(2,1)S(1)}, bf16[192,640]{1,0:T(8,128)(2,1)S(1)}, u32[]{:S(2)}, u32[]{:S(2)}) collective-permute-start(bf16[192,640]{1,0:T(8,128)(2,1)S(1)} %get-tuple-element.31), channel_id=1, source_target_pairs={{0,16},{1,9},{2,18},{3,11},{4,20},{5,13},{6,22},{7,15},{8,24},{9,1... | collective-permute-start | bytes 737288 | tf_op jit(solution)/shard_map/ppermute | solution.py:215
  31.6 0.0 collective-permute-done.9.refs_2_
  31.6 1.4 %collective-permute-done.12.refs_5_ = bf16[96,1280]{1,0:T(8,128)(2,1)S(1)} collective-permute-done((bf16[96,1280]{1,0:T(8,128)(2,1)S(1)}, bf16[96,1280]{1,0:T(8,128)(2,1)S(1)}, u32[]{:S(2)}, u32[]{:S(2)}) %collective-permute-start.12) | collective-permute-done | bytes 245792 | tf_op jit(solution)/shard_map/ppermute | solution.py:215
  33.0 2.7 %chunk.3 = (bf16[96,640]{1,0:T(8,128)(2,1)S(1)}, bf16[96,640]{1,0:T(8,128)(2,1)S(1)}, bf16[96,640]{1,0:T(8,128)(2,1)S(1)}, bf16[96,640]{1,0:T(8,128)(2,1)S(1)}, ...) custom-call(bf16[48,1280]{1,0:T(8,128)(2,1)S(1)} %collective-permute-done.7.refs_0_, ...), custom_call_target="tpu_custom_call" | custom-call | flops 1887436800 | bytes 3276800 | tf_op jit(solution)/shard_map/chunk/pallas_call | solution.py:331
  35.7 0.9 %collective-permute-done.6 = bf16[192,640]{1,0:T(8,128)(2,1)S(1)} collective-permute-done((bf16[192,640]{1,0:T(8,128)(2,1)S(1)}, bf16[192,640]{1,0:T(8,128)(2,1)S(1)}, u32[]{:S(2)}, u32[]{:S(2)}) %collective-permute-start.6) | collective-permute-done | bytes 245792 | tf_op jit(solution)/shard_map/ppermute | solution.py:215
  36.6 0.7 %collective-permute-start.13 = (bf16[96,640]{1,0:T(8,128)(2,1)S(1)}, bf16[96,640]{1,0:T(8,128)(2,1)S(1)}, u32[]{:S(2)}, u32[]{:S(2)}) collective-permute-start(bf16[96,640]{1,0:T(8,128)(2,1)S(1)} %sum.2), channel_id=1, source_target_pairs={{0,8},{1,17},{2,10},{3,19},{4,12},{5,21},{6,14},{7,23},{8,0},{9,25... | collective-permute-start | bytes 368648 | tf_op jit(solution)/shard_map/ppermute | solution.py:215
  37.3 1.4 %collective-permute-start.15 = (bf16[96,640]{1,0:T(8,128)(2,1)S(1)}, bf16[96,640]{1,0:T(8,128)(2,1)S(1)}, u32[]{:S(2)}, u32[]{:S(2)}) collective-permute-start(bf16[96,640]{1,0:T(8,128)(2,1)S(1)} %get-tuple-element.34), channel_id=1, source_target_pairs={{0,8},{1,17},{2,10},{3,19},{4,12},{5,21},{6,14},{7,23},{8,0},{9,25... | collective-permute-start | bytes 368648 | tf_op jit(solution)/shard_map/ppermute | solution.py:215
  38.7 1.2 %collective-permute-start.16 = (bf16[96,640]{1,0:T(8,128)(2,1)S(1)}, bf16[96,640]{1,0:T(8,128)(2,1)S(1)}, u32[]{:S(2)}, u32[]{:S(2)}) collective-permute-start(bf16[96,640]{1,0:T(8,128)(2,1)S(1)} %get-tuple-element.35), channel_id=1, source_target_pairs={{0,16},{1,9},{2,18},{3,11},{4,20},{5,13},{6,22},{7,15},{8,24},{9,1... | collective-permute-start | bytes 368648 | tf_op jit(solution)/shard_map/ppermute | solution.py:215
  39.9 0.9 %collective-permute-start.17 = (bf16[96,640]{1,0:T(8,128)(2,1)S(1)}, bf16[96,640]{1,0:T(8,128)(2,1)S(1)}, u32[]{:S(2)}, u32[]{:S(2)}) collective-permute-start(bf16[96,640]{1,0:T(8,128)(2,1)S(1)} %get-tuple-element.36), channel_id=1, source_target_pairs={{0,24},{1,25},{2,26},{3,27},{4,28},{5,29},{6,30},{7,31},{8,16},{9,... | collective-permute-start | bytes 368648 | tf_op jit(solution)/shard_map/ppermute | solution.py:215
  40.8 2.1 %collective-permute-done.13 = bf16[96,640]{1,0:T(8,128)(2,1)S(1)} collective-permute-done((bf16[96,640]{1,0:T(8,128)(2,1)S(1)}, bf16[96,640]{1,0:T(8,128)(2,1)S(1)}, u32[]{:S(2)}, u32[]{:S(2)}) %collective-permute-start.13) | collective-permute-done | bytes 122912 | tf_op jit(solution)/shard_map/ppermute | solution.py:215
  42.9 0.1 add_convert_fusion.refs_4_
  42.9 2.7 %weight_in_grad.1 = (bf16[640,1280]{1,0:T(8,128)(2,1)}, bf16[16,128]{1,0:T(8,128)(2,1)S(1)}) custom-call(bf16[384,1280]{1,0:T(8,128)(2,1)S(1)} %get-tuple-element.37.refs_0_, bf16[384,1280]{1,0:T(8,128)(2,1)S(1)} %get-tuple-element.38.refs_1_, bf16[384,1280]{1,0:T(8,128)(2,1)S(1)} %get-tuple-element.39.refs_2_, ...), custom_call_target="tpu_custom_call" | custom-call | flops 1258291200 | bytes 1638400 | tf_op jit(solution)/shard_map/weight_in_grad/pallas_call | solution.py:285
  45.6 0.0 collective-permute-done.15.refs_1_
  45.6 0.0 collective-permute-done.16.refs_2_
  45.6 0.5 collective-permute-done.17.refs_3_
  46.1 0.1 sum.3.refs_4_
  46.2 1.8 %collective-permute-start.14 = (bf16[48,640]{1,0:T(8,128)(2,1)S(1)}, bf16[48,640]{1,0:T(8,128)(2,1)S(1)}, u32[]{:S(2)}, u32[]{:S(2)}) collective-permute-start(bf16[48,640]{1,0:T(8,128)(2,1)S(1)} %get-tuple-element.59), channel_id=1, source_target_pairs={{0,2},{1,3},{2,0},{3,1},{4,6},{5,7},{6,4},{7,5},{8,10},{9,11},{10,... | collective-permute-start | bytes 184328 | tf_op jit(solution)/shard_map/ppermute | solution.py:207
  48.0 2.5 %collective-permute-start.19 = (bf16[48,640]{1,0:T(8,128)(2,1)S(1)}, bf16[48,640]{1,0:T(8,128)(2,1)S(1)}, u32[]{:S(2)}, u32[]{:S(2)}) collective-permute-start(bf16[48,640]{1,0:T(8,128)(2,1)S(1)} %get-tuple-element.57), channel_id=1, source_target_pairs={{0,6},{1,7},{2,4},{3,5},{4,2},{5,3},{6,0},{7,1},{8,14},{9,15},{10,... | collective-permute-start | bytes 184328 | tf_op jit(solution)/shard_map/ppermute | solution.py:207
  50.5 0.4 collective-permute-start.18
  50.9 0.0 copy-start
  50.9 0.0 copy-start.1
  50.9 0.0 copy-start.2
  50.9 2.9 %weight_out_grad.1 = (bf16[1280,640]{1,0:T(8,128)(2,1)}, bf16[16,128]{1,0:T(8,128)(2,1)S(1)}) custom-call(bf16[384,1280]{1,0:T(8,128)(2,1)S(1)} %get-tuple-element.37.refs_0_, bf16[384,1280]{1,0:T(8,128)(2,1)S(1)} %get-tuple-element.38.refs_1_, bf16[384,1280]{1,0:T(8,128)(2,1)S(1)} %get-tuple-element.42.refs_2_, ...), custom_call_target="tpu_custom_call" | custom-call | flops 1258291200 | bytes 1638400 | tf_op jit(solution)/shard_map/weight_out_grad/pallas_call | solution.py:293
  53.8 0.0 collective-permute-done.14.refs_1_
  53.8 0.2 collective-permute-done.19.refs_3_
  54.0 2.2 %collective-permute-done.18.refs_2_ = bf16[48,640]{1,0:T(8,128)(2,1)S(1)} collective-permute-done((bf16[48,640]{1,0:T(8,128)(2,1)S(1)}, bf16[48,640]{1,0:T(8,128)(2,1)S(1)}, u32[]{:S(2)}, u32[]{:S(2)}) %collective-permute-start.18) | collective-permute-done | bytes 61472 | tf_op jit(solution)/shard_map/ppermute | solution.py:207
  56.3 0.1 collective-permute-start.20
  56.4 1.3 %collective-permute-done.20.other_ref = bf16[96,640]{1,0:T(8,128)(2,1)S(1)} collective-permute-done((bf16[96,640]{1,0:T(8,128)(2,1)S(1)}, bf16[96,640]{1,0:T(8,128)(2,1)S(1)}, u32[]{:S(2)}, u32[]{:S(2)}) %collective-permute-start.20) | collective-permute-done | bytes 122912 | tf_op jit(solution)/shard_map/ppermute | solution.py:207
  57.7 0.0 copy-done
  57.7 0.0 copy-done.1
  57.7 0.0 copy-done.2
  57.7 1.0 %combine.1 = bf16[128,640]{1,0:T(8,128)(2,1)} custom-call(bf16[96,640]{1,0:T(8,128)(2,1)S(1)} %get-tuple-element.45.own_ref, bf16[96,640]{1,0:T(8,128)(2,1)S(1)} %collective-permute-done.20.other_ref, s32[2,128]{1,0:T(2,128)S(1)} %bitcast.9, s32[2,128]{1,0:T(2,128)S(1)} %bitcast.11, s32[2,128]{1,0:T(2,128)S(1)} %bitcast.13), custom_call_target="tpu_custom_call" | custom-call | tf_op jit(solution)/shard_map/combine/pallas_call | solution.py:391
  (16 shorter events, 0.2 us)
Async XLA Ops:
  2.0 1.7 %collective-permute-start = (bf16[96,1280]{1,0:T(8,128)(2,1)S(1)}, bf16[96,1280]{1,0:T(8,128)(2,1)S(1)}, u32[]{:S(2)}, u32[]{:S(2)}) collective-permute-start(bf16[96,1280]{1,0:T(8,128)(2,1)S(1)} %get-tuple-element.27), channel_id=1, source_target_pairs={{0,1},{1,0},{2,3},{3,2},{4,5},{5,4},{6,7},{7,6},{8,9},{9,8},{10,11... | collective-permute-start | bytes 737288 | tf_op jit(solution)/shard_map/ppermute | solution.py:207
  3.7 9.5 %collective-permute-start.3 = (bf16[48,1280]{1,0:T(8,128)(2,1)S(1)}, bf16[48,1280]{1,0:T(8,128)(2,1)S(1)}, u32[]{:S(2)}, u32[]{:S(2)}) collective-permute-start(bf16[48,1280]{1,0:T(8,128)(2,1)S(1)} %pad_maximum_fusion.5), channel_id=1, source_target_pairs={{0,2},{1,3},{2,0},{3,1},{4,6},{5,7},{6,4},{7,5},{8,10},{9,11},{10,... | collective-permute-start | bytes 368648 | tf_op jit(solution)/shard_map/ppermute | solution.py:207
  6.7 11.2 %collective-permute-start.7 = (bf16[48,1280]{1,0:T(8,128)(2,1)S(1)}, bf16[48,1280]{1,0:T(8,128)(2,1)S(1)}, u32[]{:S(2)}, u32[]{:S(2)}) collective-permute-start(bf16[48,1280]{1,0:T(8,128)(2,1)S(1)} %pad_maximum_fusion.6), channel_id=1, source_target_pairs={{0,4},{1,5},{2,6},{3,7},{4,0},{5,1},{6,2},{7,3},{8,12},{9,13},{10,... | collective-permute-start | bytes 368648 | tf_op jit(solution)/shard_map/ppermute | solution.py:207
  11.3 4.9 %collective-permute-start.1 = (bf16[48,1280]{1,0:T(8,128)(2,1)S(1)}, bf16[48,1280]{1,0:T(8,128)(2,1)S(1)}, u32[]{:S(2)}, u32[]{:S(2)}) collective-permute-start(bf16[48,1280]{1,0:T(8,128)(2,1)S(1)} %join.1.refs_0_), channel_id=1, source_target_pairs={{0,8},{1,17},{2,10},{3,19},{4,12},{5,21},{6,14},{7,23},{8,0},{9,25... | collective-permute-start | bytes 368648 | tf_op jit(solution)/shard_map/ppermute | solution.py:215
  12.9 6.8 %collective-permute-start.10 = (bf16[48,1280]{1,0:T(8,128)(2,1)S(1)}, bf16[48,1280]{1,0:T(8,128)(2,1)S(1)}, u32[]{:S(2)}, u32[]{:S(2)}) collective-permute-start(bf16[48,1280]{1,0:T(8,128)(2,1)S(1)} %pad_maximum_fusion.7), channel_id=1, source_target_pairs={{0,6},{1,7},{2,4},{3,5},{4,2},{5,3},{6,0},{7,1},{8,14},{9,15},{10,... | collective-permute-start | bytes 368648 | tf_op jit(solution)/shard_map/ppermute | solution.py:207
  13.2 7.7 %collective-permute-start.4 = (bf16[48,1280]{1,0:T(8,128)(2,1)S(1)}, bf16[48,1280]{1,0:T(8,128)(2,1)S(1)}, u32[]{:S(2)}, u32[]{:S(2)}) collective-permute-start(bf16[48,1280]{1,0:T(8,128)(2,1)S(1)} %collective-permute-done.3.refs_3_), channel_id=1, source_target_pairs={{0,8},{1,17},{2,10},{3,19},{4,12},{5,21},{6,14},{7,23},{8,0},{9,25... | collective-permute-start | bytes 368648 | tf_op jit(solution)/shard_map/ppermute | solution.py:215
  16.3 11.3 %collective-permute-start.2 = (bf16[96,1280]{1,0:T(8,128)(2,1)S(1)}, bf16[96,1280]{1,0:T(8,128)(2,1)S(1)}, u32[]{:S(2)}, u32[]{:S(2)}) collective-permute-start(bf16[96,1280]{1,0:T(8,128)(2,1)S(1)} %pad_maximum_fusion), channel_id=1, source_target_pairs={{0,16},{1,9},{2,18},{3,11},{4,20},{5,13},{6,22},{7,15},{8,24},{9,1... | collective-permute-start | bytes 737288 | tf_op jit(solution)/shard_map/ppermute | solution.py:215
  17.9 6.2 %collective-permute-start.8 = (bf16[48,1280]{1,0:T(8,128)(2,1)S(1)}, bf16[48,1280]{1,0:T(8,128)(2,1)S(1)}, u32[]{:S(2)}, u32[]{:S(2)}) collective-permute-start(bf16[48,1280]{1,0:T(8,128)(2,1)S(1)} %collective-permute-done.7.refs_0_), channel_id=1, source_target_pairs={{0,8},{1,17},{2,10},{3,19},{4,12},{5,21},{6,14},{7,23},{8,0},{9,25... | collective-permute-start | bytes 368648 | tf_op jit(solution)/shard_map/ppermute | solution.py:215
  19.7 7.0 %collective-permute-start.11 = (bf16[48,1280]{1,0:T(8,128)(2,1)S(1)}, bf16[48,1280]{1,0:T(8,128)(2,1)S(1)}, u32[]{:S(2)}, u32[]{:S(2)}) collective-permute-start(bf16[48,1280]{1,0:T(8,128)(2,1)S(1)} %collective-permute-done.10.refs_3_), channel_id=1, source_target_pairs={{0,8},{1,17},{2,10},{3,19},{4,12},{5,21},{6,14},{7,23},{8,0},{9,25... | collective-permute-start | bytes 368648 | tf_op jit(solution)/shard_map/ppermute | solution.py:215
  20.9 6.7 %collective-permute-start.5 = (bf16[96,1280]{1,0:T(8,128)(2,1)S(1)}, bf16[96,1280]{1,0:T(8,128)(2,1)S(1)}, u32[]{:S(2)}, u32[]{:S(2)}) collective-permute-start(bf16[96,1280]{1,0:T(8,128)(2,1)S(1)} %pad_maximum_fusion.1), channel_id=1, source_target_pairs={{0,16},{1,9},{2,18},{3,11},{4,20},{5,13},{6,22},{7,15},{8,24},{9,1... | collective-permute-start | bytes 737288 | tf_op jit(solution)/shard_map/ppermute | solution.py:215
  24.1 7.5 %collective-permute-start.9 = (bf16[96,1280]{1,0:T(8,128)(2,1)S(1)}, bf16[96,1280]{1,0:T(8,128)(2,1)S(1)}, u32[]{:S(2)}, u32[]{:S(2)}) collective-permute-start(bf16[96,1280]{1,0:T(8,128)(2,1)S(1)} %pad_maximum_fusion.2), channel_id=1, source_target_pairs={{0,16},{1,9},{2,18},{3,11},{4,20},{5,13},{6,22},{7,15},{8,24},{9,1... | collective-permute-start | bytes 737288 | tf_op jit(solution)/shard_map/ppermute | solution.py:215
  26.7 6.3 %collective-permute-start.12 = (bf16[96,1280]{1,0:T(8,128)(2,1)S(1)}, bf16[96,1280]{1,0:T(8,128)(2,1)S(1)}, u32[]{:S(2)}, u32[]{:S(2)}) collective-permute-start(bf16[96,1280]{1,0:T(8,128)(2,1)S(1)} %pad_maximum_fusion.3), channel_id=1, source_target_pairs={{0,16},{1,9},{2,18},{3,11},{4,20},{5,13},{6,22},{7,15},{8,24},{9,1... | collective-permute-start | bytes 737288 | tf_op jit(solution)/shard_map/ppermute | solution.py:215
  30.3 6.3 %collective-permute-start.6 = (bf16[192,640]{1,0:T(8,128)(2,1)S(1)}, bf16[192,640]{1,0:T(8,128)(2,1)S(1)}, u32[]{:S(2)}, u32[]{:S(2)}) collective-permute-start(bf16[192,640]{1,0:T(8,128)(2,1)S(1)} %get-tuple-element.31), channel_id=1, source_target_pairs={{0,16},{1,9},{2,18},{3,11},{4,20},{5,13},{6,22},{7,15},{8,24},{9,1... | collective-permute-start | bytes 737288 | tf_op jit(solution)/shard_map/ppermute | solution.py:215
  36.6 6.2 %collective-permute-start.13 = (bf16[96,640]{1,0:T(8,128)(2,1)S(1)}, bf16[96,640]{1,0:T(8,128)(2,1)S(1)}, u32[]{:S(2)}, u32[]{:S(2)}) collective-permute-start(bf16[96,640]{1,0:T(8,128)(2,1)S(1)} %sum.2), channel_id=1, source_target_pairs={{0,8},{1,17},{2,10},{3,19},{4,12},{5,21},{6,14},{7,23},{8,0},{9,25... | collective-permute-start | bytes 368648 | tf_op jit(solution)/shard_map/ppermute | solution.py:215
  37.3 8.3 %collective-permute-start.15 = (bf16[96,640]{1,0:T(8,128)(2,1)S(1)}, bf16[96,640]{1,0:T(8,128)(2,1)S(1)}, u32[]{:S(2)}, u32[]{:S(2)}) collective-permute-start(bf16[96,640]{1,0:T(8,128)(2,1)S(1)} %get-tuple-element.34), channel_id=1, source_target_pairs={{0,8},{1,17},{2,10},{3,19},{4,12},{5,21},{6,14},{7,23},{8,0},{9,25... | collective-permute-start | bytes 368648 | tf_op jit(solution)/shard_map/ppermute | solution.py:215
  38.7 6.9 %collective-permute-start.16 = (bf16[96,640]{1,0:T(8,128)(2,1)S(1)}, bf16[96,640]{1,0:T(8,128)(2,1)S(1)}, u32[]{:S(2)}, u32[]{:S(2)}) collective-permute-start(bf16[96,640]{1,0:T(8,128)(2,1)S(1)} %get-tuple-element.35), channel_id=1, source_target_pairs={{0,16},{1,9},{2,18},{3,11},{4,20},{5,13},{6,22},{7,15},{8,24},{9,1... | collective-permute-start | bytes 368648 | tf_op jit(solution)/shard_map/ppermute | solution.py:215
  39.9 6.2 %collective-permute-start.17 = (bf16[96,640]{1,0:T(8,128)(2,1)S(1)}, bf16[96,640]{1,0:T(8,128)(2,1)S(1)}, u32[]{:S(2)}, u32[]{:S(2)}) collective-permute-start(bf16[96,640]{1,0:T(8,128)(2,1)S(1)} %get-tuple-element.36), channel_id=1, source_target_pairs={{0,24},{1,25},{2,26},{3,27},{4,28},{5,29},{6,30},{7,31},{8,16},{9,... | collective-permute-start | bytes 368648 | tf_op jit(solution)/shard_map/ppermute | solution.py:215
  46.2 7.6 %collective-permute-start.14 = (bf16[48,640]{1,0:T(8,128)(2,1)S(1)}, bf16[48,640]{1,0:T(8,128)(2,1)S(1)}, u32[]{:S(2)}, u32[]{:S(2)}) collective-permute-start(bf16[48,640]{1,0:T(8,128)(2,1)S(1)} %get-tuple-element.59), channel_id=1, source_target_pairs={{0,2},{1,3},{2,0},{3,1},{4,6},{5,7},{6,4},{7,5},{8,10},{9,11},{10,... | collective-permute-start | bytes 184328 | tf_op jit(solution)/shard_map/ppermute | solution.py:207
  48.0 6.0 %collective-permute-start.19 = (bf16[48,640]{1,0:T(8,128)(2,1)S(1)}, bf16[48,640]{1,0:T(8,128)(2,1)S(1)}, u32[]{:S(2)}, u32[]{:S(2)}) collective-permute-start(bf16[48,640]{1,0:T(8,128)(2,1)S(1)} %get-tuple-element.57), channel_id=1, source_target_pairs={{0,6},{1,7},{2,4},{3,5},{4,2},{5,3},{6,0},{7,1},{8,14},{9,15},{10,... | collective-permute-start | bytes 184328 | tf_op jit(solution)/shard_map/ppermute | solution.py:207
  50.5 5.8 %collective-permute-start.18 = (bf16[48,640]{1,0:T(8,128)(2,1)S(1)}, bf16[48,640]{1,0:T(8,128)(2,1)S(1)}, u32[]{:S(2)}, u32[]{:S(2)}) collective-permute-start(bf16[48,640]{1,0:T(8,128)(2,1)S(1)} %get-tuple-element.58), channel_id=1, source_target_pairs={{0,4},{1,5},{2,6},{3,7},{4,0},{5,1},{6,2},{7,3},{8,12},{9,13},{10,... | collective-permute-start | bytes 184328 | tf_op jit(solution)/shard_map/ppermute | solution.py:207
  50.9 6.8 %copy-start = (s32[128,2]{0,1:T(2,128)S(1)}, s32[128,2]{0,1:T(2,128)}, u32[]{:S(2)}) copy-start(s32[128,2]{0,1:T(2,128)} %param.11) | copy-start | bytes 3076
  50.9 6.8 %copy-start.1 = (s32[128,2]{0,1:T(2,128)S(1)}, s32[128,2]{0,1:T(2,128)}, u32[]{:S(2)}) copy-start(s32[128,2]{0,1:T(2,128)} %param.12) | copy-start | bytes 3076
  50.9 6.8 %copy-start.2 = (s32[128,2]{0,1:T(2,128)S(1)}, s32[128,2]{0,1:T(2,128)}, u32[]{:S(2)}) copy-start(s32[128,2]{0,1:T(2,128)} %param.13) | copy-start | bytes 3076
  56.3 1.4 %collective-permute-start.20 = (bf16[96,640]{1,0:T(8,128)(2,1)S(1)}, bf16[96,640]{1,0:T(8,128)(2,1)S(1)}, u32[]{:S(2)}, u32[]{:S(2)}) collective-permute-start(bf16[96,640]{1,0:T(8,128)(2,1)S(1)} %get-tuple-element.46), channel_id=1, source_target_pairs={{0,1},{1,0},{2,3},{3,2},{4,5},{5,4},{6,7},{7,6},{8,9},{9,8},{10,11... | collective-permute-start | bytes 368648 | tf_op jit(solution)/shard_map/ppermute | solution.py:207

commit v4 on v3

--- a/solution.py
+++ b/solution.py
@@ -20,9 +20,13 @@
 C_W = 1.0
 LOAD = None
 WAIT_Z = False
-DEFER = 1
+DEFER = 3
 HOLD = False
 EARLY_LOAD = False
+Z1LAST = False
+W_AFTER = -1
+IN_TURN = True
+FIRST_SEND = True
 FIRST_LOAD = True
 HOLD2 = 0
 Z3 = False
@@ -100,7 +104,7 @@
 
 def chunk_kernel(tile, groups, levels, places, *refs):
     moved, refs = refs[: len(places)], refs[len(places) :]
-    (win_ref, wout_ref), outs = refs[:2], refs[2:]
+    (win_ref, wout_ref), outs = refs[:2], refs[3:]
     sends, kept_ref = outs[:-5], outs[-5]
     rows_ref, hidden_ref, pre_ref, acc_ref = outs[-4:]
     width, hidden_total = win_ref.shape
@@ -337,43 +341,49 @@
                 vmem_out((total, hidden_total)),
                 vmem_out((total, hidden_total)),
             ),
-            in_specs=[vmem_whole] * (len(moved) + 2),
+            in_specs=[vmem_whole] * (len(moved) + 2) + [anywhere],
             out_specs=(vmem_whole,) * (len(levels) + 4),
             scratch_shapes=[pltpu.VMEM((total, width), f32)],
             compiler_params=params(32),
             cost_estimate=cost(int(C_CHUNK * 6 * total * width * hidden_total), int(C_CHUNK * 4 * width * hidden_total), int(C_CHUNK * total * hidden_total)),
             name="chunk",
-        )(*moved, *weights)
+        )(*moved, *weights, deferred[-1][-1] if deferred and IN_TURN else weights[0])
         sends, (kept, rows_all, hidden, pre) = outs[:-4], outs[-4:]
         all_rows.append(rows_all)
         all_hidden.append(hidden)
         all_pre.append(pre)
         deferred.append((inside, count, levels, sends, kept))
 
-    def reduced(number, after):
-        inside, count, levels, sends, kept = deferred[number]
-        terms = [kept]
-        if DIRECT[number]:
-            terms += [swap_groups(value, p) for (p, _), value in zip(levels, sends, strict=True)]
-        else:
-            parts = []
-            for (low, high), value in zip(levels, sends, strict=True):
-                if parts:
-                    value = add_rows([value] + [part[low * count : high * count] for part in parts], after[0])
-                elif DEFER > 1:
-                    value = join([value], after)
-                parts.append(swap_groups(value, low))
-            terms += [part if part.shape[0] == count else part[:count] for part in parts]
-        return terms
+    def first_send(number):
+        _, _, levels, sends, _ = deferred[number]
+        return swap_groups(sends[0], levels[0][0])
+
+    def rest(number, first, after):
+        _, count, levels, sends, kept = deferred[number]
+        parts = [first]
+        for (low, high), value in zip(levels[1:], sends[1:], strict=True):
+            if not DIRECT[number]:
+                value = add_rows([value] + [part[low * count : high * count] for part in parts], after)
+            parts.append(swap_groups(value, low))
+        return [kept] + [part if part.shape[0] == count else part[:count] for part in parts]
 
     last = len(chunks) - 1
+    firsts = [first_send(number) for number in range(last + 1)]
+    kept_last = deferred[last][-1]
+    after = {0: deferred[0][-1], 1: kept_last, 3: firsts[last]}.get(DEFER)
+    if after is None:
+        terms = rest(last, firsts[last], kept_last)
+        after = terms[-1]
     for number in range(last):
-        terms = reduced(number, [deferred[last if DEFER else number][-1]])
-        sums_of.append(sum(t.astype(f32) for t in terms).astype(bf16))
-    terms = reduced(last, [deferred[last][-1]])
-    grad_in, done = weight_in_call(sums_of[0])
+        others = rest(number, firsts[number], after)
+        sums_of.append(sum(t.astype(f32) for t in others).astype(bf16))
+    if DEFER != 4:
+        terms = rest(last, firsts[last], kept_last)
+    grad_in, done = weight_in_call({0: sums_of[0], -1: kept_last}.get(W_AFTER, terms[W_AFTER]))
     sums_of.append(add_rows(terms, done))
     for (inside, *_), summed in zip(deferred, sums_of, strict=True):
+        if Z1LAST and summed is not sums_of[-1]:
+            summed = join([summed], sums_of[-1:])
         for i, m in enumerate(inside):
             piece = summed[i * block : (i + 1) * block]
             returned[m] = piece if m == 0 else swap(piece, "expert", 2 * m)

time: 58.8 us -> 57 us (0.969)
  waiting for transfers between devices: 17.4 us -> 14.6 us
  starting transfers between devices: 25 us -> 25.9 us
    ppermute x8, waiting for transfers between devices: 5.24 us -> 3.08 us  [swap(): return lax.ppermute(value, axis, [(i, i ^ offset) for i in range(size)])]
    ppermute x13, waiting for transfers between devices: 12.2 us -> 11.5 us  [swap_groups(): return lax.ppermute(value, ('dp', 'expert'), pairs)]
  transfers between devices with their start and end apart: 21 -> 21, of which waited for: 12 -> 10; matrix products, arithmetic and copies ran while one was open for 0% -> 0% of each run, Pallas kernels for 22% -> 23%
where the time goes in v4:
time: 57 us; the launch traced here: 56.9 us
  starting transfers between devices  25.9 us (45%)
  Pallas kernels  15.4 us (27%)
  waiting for transfers between devices  14.6 us (26%)
  between operations  0.79 us (1%)
    ppermute x13, starting transfers between devices, swap_groups(): return lax.ppermute(value, ('dp', 'expert'), pairs)  14.3 us
    ppermute x8, starting transfers between devices, swap(): return lax.ppermute(value, axis, [(i, i ^ offset) for i in range(size)])  11.6 us
    ppermute x13, waiting for transfers between devices, swap_groups(): return lax.ppermute(value, ('dp', 'expert'), pairs)  11.5 us
    pallas_call x2, Pallas kernels, body(): pl.pallas_call(functools.partial(chunk_kernel, TILE, groups, levels, plac...  5.42 us
    ppermute x8, waiting for transfers between devices, swap(): return lax.ppermute(value, axis, [(i, i ^ offset) for i in range(size)])  3.08 us
    pallas_call x1, Pallas kernels, weight_out_call(): pl.pallas_call(functools.partial(weight_out_kernel, chunk_count, width),...  2.91 us
    pallas_call x1, Pallas kernels, weight_in_call(): pl.pallas_call(functools.partial(weight_in_kernel, chunk_count, width), o...  2.66 us
    pallas_call x1, Pallas kernels, body(): pl.pallas_call(load_kernel, out_shape=(vmem_out(win.shape), vmem_out(wout...  1.94 us
  transfers between devices with their start and end apart: 21, of which 10 were waited for; matrix products, arithmetic and copies ran while one was open for 0% of the time, Pallas kernels for 23%

profile of v4, /device:TPU:0, one launch (start us, length us, event | category | flops | bytes accessed | tf_op | source)
XLA Modules:
  0.0 56.9 jit_solution(7118760843989200294)
XLA Ops:
  0.6 1.3 %dispatch.1 = (bf16[96,1280]{1,0:T(8,128)(2,1)S(1)}, bf16[96,1280]{1,0:T(8,128)(2,1)S(1)}) custom-call(bf16[128,640]{1,0:T(8,128)(2,1)} %refs_0_.1, bf16[128,640]{1,0:T(8,128)(2,1)} %refs_1_.1, f32[2,128]{1,0:T(2,128)} %bitcast.16, s32[2,128]{1,0:T(2,128)} %bitcast.8, s32[2,128]{1,0:T(2,128)} %bitcast.10, s32[2,128]{1,0:T(2,128)} %bitcast.12), custom_call_target="tpu_custom_call" | custom-call | tf_op jit(solution)/shard_map/dispatch/pallas_call | solution.py:244
  2.0 0.5 collective-permute-start
  2.5 1.1 %collective-permute-done.refs_2_ = bf16[96,1280]{1,0:T(8,128)(2,1)S(1)} collective-permute-done((bf16[96,1280]{1,0:T(8,128)(2,1)S(1)}, bf16[96,1280]{1,0:T(8,128)(2,1)S(1)}, u32[]{:S(2)}, u32[]{:S(2)}) %collective-permute-start) | collective-permute-done | bytes 245792 | tf_op jit(solution)/shard_map/ppermute | solution.py:211
  3.7 3.0 %collective-permute-start.3 = (bf16[48,1280]{1,0:T(8,128)(2,1)S(1)}, bf16[48,1280]{1,0:T(8,128)(2,1)S(1)}, u32[]{:S(2)}, u32[]{:S(2)}) collective-permute-start(bf16[48,1280]{1,0:T(8,128)(2,1)S(1)} %pad_maximum_fusion.5), channel_id=1, source_target_pairs={{0,2},{1,3},{2,0},{3,1},{4,6},{5,7},{6,4},{7,5},{8,10},{9,11},{10,... | collective-permute-start | bytes 368648 | tf_op jit(solution)/shard_map/ppermute | solution.py:211
  6.7 2.7 %collective-permute-start.7 = (bf16[48,1280]{1,0:T(8,128)(2,1)S(1)}, bf16[48,1280]{1,0:T(8,128)(2,1)S(1)}, u32[]{:S(2)}, u32[]{:S(2)}) collective-permute-start(bf16[48,1280]{1,0:T(8,128)(2,1)S(1)} %pad_maximum_fusion.6), channel_id=1, source_target_pairs={{0,4},{1,5},{2,6},{3,7},{4,0},{5,1},{6,2},{7,3},{8,12},{9,13},{10,... | collective-permute-start | bytes 368648 | tf_op jit(solution)/shard_map/ppermute | solution.py:211
  9.4 1.9 %load.1 = (bf16[640,1280]{1,0:T(8,128)(2,1)S(1)}, bf16[1280,640]{1,0:T(8,128)(2,1)S(1)}) custom-call(bf16[640,1280]{1,0:T(8,128)(2,1)} %bitcast.14, bf16[1280,640]{1,0:T(8,128)(2,1)} %bitcast.15, bf16[96,1280]{1,0:T(8,128)(2,1)S(1)} %collective-permute-done.refs_2_), custom_call_target="tpu_custom_call" | custom-call | bytes 6553600 | tf_op jit(solution)/shard_map/load/pallas_call | solution.py:269
  11.3 1.6 %collective-permute-start.1 = (bf16[48,1280]{1,0:T(8,128)(2,1)S(1)}, bf16[48,1280]{1,0:T(8,128)(2,1)S(1)}, u32[]{:S(2)}, u32[]{:S(2)}) collective-permute-start(bf16[48,1280]{1,0:T(8,128)(2,1)S(1)} %join.1.refs_0_), channel_id=1, source_target_pairs={{0,8},{1,17},{2,10},{3,19},{4,12},{5,21},{6,14},{7,23},{8,0},{9,25... | collective-permute-start | bytes 368648 | tf_op jit(solution)/shard_map/ppermute | solution.py:219
  12.9 0.3 collective-permute-start.10
  13.2 0.0 collective-permute-done.3.refs_3_
  13.2 0.6 %collective-permute-start.4 = (bf16[48,1280]{1,0:T(8,128)(2,1)S(1)}, bf16[48,1280]{1,0:T(8,128)(2,1)S(1)}, u32[]{:S(2)}, u32[]{:S(2)}) collective-permute-start(bf16[48,1280]{1,0:T(8,128)(2,1)S(1)} %collective-permute-done.3.refs_3_), channel_id=1, source_target_pairs={{0,8},{1,17},{2,10},{3,19},{4,12},{5,21},{6,14},{7,23},{8,0},{9,25... | collective-permute-start | bytes 368648 | tf_op jit(solution)/shard_map/ppermute | solution.py:219
  13.8 2.5 %collective-permute-done.1.refs_1_ = bf16[48,1280]{1,0:T(8,128)(2,1)S(1)} collective-permute-done((bf16[48,1280]{1,0:T(8,128)(2,1)S(1)}, bf16[48,1280]{1,0:T(8,128)(2,1)S(1)}, u32[]{:S(2)}, u32[]{:S(2)}) %collective-permute-start.1) | collective-permute-done | bytes 122912 | tf_op jit(solution)/shard_map/ppermute | solution.py:219
  16.3 1.6 %collective-permute-start.2 = (bf16[96,1280]{1,0:T(8,128)(2,1)S(1)}, bf16[96,1280]{1,0:T(8,128)(2,1)S(1)}, u32[]{:S(2)}, u32[]{:S(2)}) collective-permute-start(bf16[96,1280]{1,0:T(8,128)(2,1)S(1)} %pad_maximum_fusion), channel_id=1, source_target_pairs={{0,16},{1,9},{2,18},{3,11},{4,20},{5,13},{6,22},{7,15},{8,24},{9,1... | collective-permute-start | bytes 737288 | tf_op jit(solution)/shard_map/ppermute | solution.py:219
  17.9 0.0 collective-permute-done.7.refs_0_
  17.9 1.5 %collective-permute-start.8 = (bf16[48,1280]{1,0:T(8,128)(2,1)S(1)}, bf16[48,1280]{1,0:T(8,128)(2,1)S(1)}, u32[]{:S(2)}, u32[]{:S(2)}) collective-permute-start(bf16[48,1280]{1,0:T(8,128)(2,1)S(1)} %collective-permute-done.7.refs_0_), channel_id=1, source_target_pairs={{0,8},{1,17},{2,10},{3,19},{4,12},{5,21},{6,14},{7,23},{8,0},{9,25... | collective-permute-start | bytes 368648 | tf_op jit(solution)/shard_map/ppermute | solution.py:219
  19.4 0.3 collective-permute-done.10.refs_3_
  19.7 1.2 %collective-permute-start.11 = (bf16[48,1280]{1,0:T(8,128)(2,1)S(1)}, bf16[48,1280]{1,0:T(8,128)(2,1)S(1)}, u32[]{:S(2)}, u32[]{:S(2)}) collective-permute-start(bf16[48,1280]{1,0:T(8,128)(2,1)S(1)} %collective-permute-done.10.refs_3_), channel_id=1, source_target_pairs={{0,8},{1,17},{2,10},{3,19},{4,12},{5,21},{6,14},{7,23},{8,0},{9,25... | collective-permute-start | bytes 368648 | tf_op jit(solution)/shard_map/ppermute | solution.py:219
  20.9 0.0 collective-permute-done.4.refs_4_
  20.9 0.9 %collective-permute-start.5 = (bf16[96,1280]{1,0:T(8,128)(2,1)S(1)}, bf16[96,1280]{1,0:T(8,128)(2,1)S(1)}, u32[]{:S(2)}, u32[]{:S(2)}) collective-permute-start(bf16[96,1280]{1,0:T(8,128)(2,1)S(1)} %pad_maximum_fusion.1), channel_id=1, source_target_pairs={{0,16},{1,9},{2,18},{3,11},{4,20},{5,13},{6,22},{7,15},{8,24},{9,1... | collective-permute-start | bytes 737288 | tf_op jit(solution)/shard_map/ppermute | solution.py:219
  21.9 2.2 %collective-permute-done.8.refs_1_ = bf16[48,1280]{1,0:T(8,128)(2,1)S(1)} collective-permute-done((bf16[48,1280]{1,0:T(8,128)(2,1)S(1)}, bf16[48,1280]{1,0:T(8,128)(2,1)S(1)}, u32[]{:S(2)}, u32[]{:S(2)}) %collective-permute-start.8) | collective-permute-done | bytes 122912 | tf_op jit(solution)/shard_map/ppermute | solution.py:219
  24.1 0.1 collective-permute-start.9
  24.2 2.5 %collective-permute-done.11.refs_4_ = bf16[48,1280]{1,0:T(8,128)(2,1)S(1)} collective-permute-done((bf16[48,1280]{1,0:T(8,128)(2,1)S(1)}, bf16[48,1280]{1,0:T(8,128)(2,1)S(1)}, u32[]{:S(2)}, u32[]{:S(2)}) %collective-permute-start.11) | collective-permute-done | bytes 122912 | tf_op jit(solution)/shard_map/ppermute | solution.py:219
  26.7 0.9 %collective-permute-start.12 = (bf16[96,1280]{1,0:T(8,128)(2,1)S(1)}, bf16[96,1280]{1,0:T(8,128)(2,1)S(1)}, u32[]{:S(2)}, u32[]{:S(2)}) collective-permute-start(bf16[96,1280]{1,0:T(8,128)(2,1)S(1)} %pad_maximum_fusion.3), channel_id=1, source_target_pairs={{0,16},{1,9},{2,18},{3,11},{4,20},{5,13},{6,22},{7,15},{8,24},{9,1... | collective-permute-start | bytes 737288 | tf_op jit(solution)/shard_map/ppermute | solution.py:219
  27.6 0.0 collective-permute-done.2.refs_2_
  27.6 0.0 collective-permute-done.5.refs_5_
  27.6 2.7 %chunk.2 = (bf16[192,640]{1,0:T(8,128)(2,1)S(1)}, bf16[96,640]{1,0:T(8,128)(2,1)S(1)}, bf16[96,640]{1,0:T(8,128)(2,1)S(1)}, bf16[384,1280]{1,0:T(8,128)(2,1)S(1)...) custom-call(bf16[48,1280]{1,0:T(8,128)(2,1)S(1)} %join.1.refs_0_, ...), custom_call_target="tpu_custom_call" | custom-call | flops 1887436800 | bytes 3276800 | tf_op jit(solution)/shard_map/chunk/pallas_call | solution.py:335
  30.4 1.3 %collective-permute-start.6 = (bf16[192,640]{1,0:T(8,128)(2,1)S(1)}, bf16[192,640]{1,0:T(8,128)(2,1)S(1)}, u32[]{:S(2)}, u32[]{:S(2)}) collective-permute-start(bf16[192,640]{1,0:T(8,128)(2,1)S(1)} %get-tuple-element.31), channel_id=1, source_target_pairs={{0,16},{1,9},{2,18},{3,11},{4,20},{5,13},{6,22},{7,15},{8,24},{9,1... | collective-permute-start | bytes 737288 | tf_op jit(solution)/shard_map/ppermute | solution.py:219
  31.6 0.0 collective-permute-done.9.refs_2_
  31.6 1.4 %collective-permute-done.12.refs_5_ = bf16[96,1280]{1,0:T(8,128)(2,1)S(1)} collective-permute-done((bf16[96,1280]{1,0:T(8,128)(2,1)S(1)}, bf16[96,1280]{1,0:T(8,128)(2,1)S(1)}, u32[]{:S(2)}, u32[]{:S(2)}) %collective-permute-start.12) | collective-permute-done | bytes 245792 | tf_op jit(solution)/shard_map/ppermute | solution.py:219
  33.0 2.7 %chunk.3 = (bf16[96,640]{1,0:T(8,128)(2,1)S(1)}, bf16[96,640]{1,0:T(8,128)(2,1)S(1)}, bf16[96,640]{1,0:T(8,128)(2,1)S(1)}, bf16[96,640]{1,0:T(8,128)(2,1)S(1)}, ...) custom-call(bf16[48,1280]{1,0:T(8,128)(2,1)S(1)} %collective-permute-done.7.refs_0_, ...), custom_call_target="tpu_custom_call" | custom-call | flops 1887436800 | bytes 3276800 | tf_op jit(solution)/shard_map/chunk/pallas_call | solution.py:335
  35.7 1.5 %collective-permute-start.13 = (bf16[96,640]{1,0:T(8,128)(2,1)S(1)}, bf16[96,640]{1,0:T(8,128)(2,1)S(1)}, u32[]{:S(2)}, u32[]{:S(2)}) collective-permute-start(bf16[96,640]{1,0:T(8,128)(2,1)S(1)} %get-tuple-element.33), channel_id=1, source_target_pairs={{0,8},{1,17},{2,10},{3,19},{4,12},{5,21},{6,14},{7,23},{8,0},{9,25... | collective-permute-start | bytes 368648 | tf_op jit(solution)/shard_map/ppermute | solution.py:219
  37.2 0.4 collective-permute-start.16
  37.6 1.6 %collective-permute-start.17 = (bf16[96,640]{1,0:T(8,128)(2,1)S(1)}, bf16[96,640]{1,0:T(8,128)(2,1)S(1)}, u32[]{:S(2)}, u32[]{:S(2)}) collective-permute-start(bf16[96,640]{1,0:T(8,128)(2,1)S(1)} %get-tuple-element.36), channel_id=1, source_target_pairs={{0,24},{1,25},{2,26},{3,27},{4,28},{5,29},{6,30},{7,31},{8,16},{9,... | collective-permute-start | bytes 368648 | tf_op jit(solution)/shard_map/ppermute | solution.py:219
  39.3 2.7 %weight_in_grad.1 = (bf16[640,1280]{1,0:T(8,128)(2,1)}, bf16[16,128]{1,0:T(8,128)(2,1)S(1)}) custom-call(bf16[384,1280]{1,0:T(8,128)(2,1)S(1)} %get-tuple-element.37.refs_0_, bf16[384,1280]{1,0:T(8,128)(2,1)S(1)} %get-tuple-element.38.refs_1_, bf16[384,1280]{1,0:T(8,128)(2,1)S(1)} %get-tuple-element.39.refs_2_, ...), custom_call_target="tpu_custom_call" | custom-call | flops 1258291200 | bytes 1638400 | tf_op jit(solution)/shard_map/weight_in_grad/pallas_call | solution.py:289
  41.9 0.0 collective-permute-done.13.refs_2_.refs_1_
  41.9 2.4 %collective-permute-done.16.refs_2_ = bf16[96,640]{1,0:T(8,128)(2,1)S(1)} collective-permute-done((bf16[96,640]{1,0:T(8,128)(2,1)S(1)}, bf16[96,640]{1,0:T(8,128)(2,1)S(1)}, u32[]{:S(2)}, u32[]{:S(2)}) %collective-permute-start.16) | collective-permute-done | bytes 122912 | tf_op jit(solution)/shard_map/ppermute | solution.py:219
  44.3 0.0 collective-permute-done.17.refs_3_
  44.3 0.1 sum.3.refs_4_
  44.4 0.0 collective-permute-done.6
  44.5 1.2 %collective-permute-start.14 = (bf16[96,640]{1,0:T(8,128)(2,1)S(1)}, bf16[96,640]{1,0:T(8,128)(2,1)S(1)}, u32[]{:S(2)}, u32[]{:S(2)}) collective-permute-start(bf16[96,640]{1,0:T(8,128)(2,1)S(1)} %sum.2), channel_id=1, source_target_pairs={{0,8},{1,17},{2,10},{3,19},{4,12},{5,21},{6,14},{7,23},{8,0},{9,25... | collective-permute-start | bytes 368648 | tf_op jit(solution)/shard_map/ppermute | solution.py:219
  45.7 3.1 %collective-permute-start.19 = (bf16[48,640]{1,0:T(8,128)(2,1)S(1)}, bf16[48,640]{1,0:T(8,128)(2,1)S(1)}, u32[]{:S(2)}, u32[]{:S(2)}) collective-permute-start(bf16[48,640]{1,0:T(8,128)(2,1)S(1)} %get-tuple-element.57), channel_id=1, source_target_pairs={{0,6},{1,7},{2,4},{3,5},{4,2},{5,3},{6,0},{7,1},{8,14},{9,15},{10,... | collective-permute-start | bytes 184328 | tf_op jit(solution)/shard_map/ppermute | solution.py:211
  48.8 0.2 collective-permute-start.18
  49.0 0.5 collective-permute-done.14
  49.5 1.7 %collective-permute-start.15 = (bf16[48,640]{1,0:T(8,128)(2,1)S(1)}, bf16[48,640]{1,0:T(8,128)(2,1)S(1)}, u32[]{:S(2)}, u32[]{:S(2)}) collective-permute-start(bf16[48,640]{1,0:T(8,128)(2,1)S(1)} %get-tuple-element.59), channel_id=1, source_target_pairs={{0,2},{1,3},{2,0},{3,1},{4,6},{5,7},{6,4},{7,5},{8,10},{9,11},{10,... | collective-permute-start | bytes 184328 | tf_op jit(solution)/shard_map/ppermute | solution.py:211
  51.2 0.0 copy-start
  51.2 0.0 copy-start.1
  51.2 0.0 copy-start.2
  51.2 2.9 %weight_out_grad.1 = (bf16[1280,640]{1,0:T(8,128)(2,1)}, bf16[16,128]{1,0:T(8,128)(2,1)S(1)}) custom-call(bf16[384,1280]{1,0:T(8,128)(2,1)S(1)} %get-tuple-element.37.refs_0_, bf16[384,1280]{1,0:T(8,128)(2,1)S(1)} %get-tuple-element.38.refs_1_, bf16[384,1280]{1,0:T(8,128)(2,1)S(1)} %get-tuple-element.42.refs_2_, ...), custom_call_target="tpu_custom_call" | custom-call | flops 1258291200 | bytes 1638400 | tf_op jit(solution)/shard_map/weight_out_grad/pallas_call | solution.py:297
  54.1 0.0 collective-permute-done.19.refs_3_
  54.1 0.0 collective-permute-done.18.refs_2_
  54.1 0.3 collective-permute-done.15.refs_1_
  54.5 0.1 collective-permute-start.20
  54.5 1.3 %collective-permute-done.20.other_ref = bf16[96,640]{1,0:T(8,128)(2,1)S(1)} collective-permute-done((bf16[96,640]{1,0:T(8,128)(2,1)S(1)}, bf16[96,640]{1,0:T(8,128)(2,1)S(1)}, u32[]{:S(2)}, u32[]{:S(2)}) %collective-permute-start.20) | collective-permute-done | bytes 122912 | tf_op jit(solution)/shard_map/ppermute | solution.py:211
  55.9 0.0 copy-done
  55.9 0.0 copy-done.1
  55.9 0.0 copy-done.2
  55.9 1.0 %combine.1 = bf16[128,640]{1,0:T(8,128)(2,1)} custom-call(bf16[96,640]{1,0:T(8,128)(2,1)S(1)} %get-tuple-element.45.own_ref, bf16[96,640]{1,0:T(8,128)(2,1)S(1)} %collective-permute-done.20.other_ref, s32[2,128]{1,0:T(2,128)S(1)} %bitcast.9, s32[2,128]{1,0:T(2,128)S(1)} %bitcast.11, s32[2,128]{1,0:T(2,128)S(1)} %bitcast.13), custom_call_target="tpu_custom_call" | custom-call | tf_op jit(solution)/shard_map/combine/pallas_call | solution.py:401
  (17 shorter events, 0.3 us)
Async XLA Ops:
  2.0 1.7 %collective-permute-start = (bf16[96,1280]{1,0:T(8,128)(2,1)S(1)}, bf16[96,1280]{1,0:T(8,128)(2,1)S(1)}, u32[]{:S(2)}, u32[]{:S(2)}) collective-permute-start(bf16[96,1280]{1,0:T(8,128)(2,1)S(1)} %get-tuple-element.27), channel_id=1, source_target_pairs={{0,1},{1,0},{2,3},{3,2},{4,5},{5,4},{6,7},{7,6},{8,9},{9,8},{10,11... | collective-permute-start | bytes 737288 | tf_op jit(solution)/shard_map/ppermute | solution.py:211
  3.7 9.5 %collective-permute-start.3 = (bf16[48,1280]{1,0:T(8,128)(2,1)S(1)}, bf16[48,1280]{1,0:T(8,128)(2,1)S(1)}, u32[]{:S(2)}, u32[]{:S(2)}) collective-permute-start(bf16[48,1280]{1,0:T(8,128)(2,1)S(1)} %pad_maximum_fusion.5), channel_id=1, source_target_pairs={{0,2},{1,3},{2,0},{3,1},{4,6},{5,7},{6,4},{7,5},{8,10},{9,11},{10,... | collective-permute-start | bytes 368648 | tf_op jit(solution)/shard_map/ppermute | solution.py:211
  6.7 11.2 %collective-permute-start.7 = (bf16[48,1280]{1,0:T(8,128)(2,1)S(1)}, bf16[48,1280]{1,0:T(8,128)(2,1)S(1)}, u32[]{:S(2)}, u32[]{:S(2)}) collective-permute-start(bf16[48,1280]{1,0:T(8,128)(2,1)S(1)} %pad_maximum_fusion.6), channel_id=1, source_target_pairs={{0,4},{1,5},{2,6},{3,7},{4,0},{5,1},{6,2},{7,3},{8,12},{9,13},{10,... | collective-permute-start | bytes 368648 | tf_op jit(solution)/shard_map/ppermute | solution.py:211
  11.3 4.9 %collective-permute-start.1 = (bf16[48,1280]{1,0:T(8,128)(2,1)S(1)}, bf16[48,1280]{1,0:T(8,128)(2,1)S(1)}, u32[]{:S(2)}, u32[]{:S(2)}) collective-permute-start(bf16[48,1280]{1,0:T(8,128)(2,1)S(1)} %join.1.refs_0_), channel_id=1, source_target_pairs={{0,8},{1,17},{2,10},{3,19},{4,12},{5,21},{6,14},{7,23},{8,0},{9,25... | collective-permute-start | bytes 368648 | tf_op jit(solution)/shard_map/ppermute | solution.py:219
  12.9 6.8 %collective-permute-start.10 = (bf16[48,1280]{1,0:T(8,128)(2,1)S(1)}, bf16[48,1280]{1,0:T(8,128)(2,1)S(1)}, u32[]{:S(2)}, u32[]{:S(2)}) collective-permute-start(bf16[48,1280]{1,0:T(8,128)(2,1)S(1)} %pad_maximum_fusion.7), channel_id=1, source_target_pairs={{0,6},{1,7},{2,4},{3,5},{4,2},{5,3},{6,0},{7,1},{8,14},{9,15},{10,... | collective-permute-start | bytes 368648 | tf_op jit(solution)/shard_map/ppermute | solution.py:211
  13.2 7.7 %collective-permute-start.4 = (bf16[48,1280]{1,0:T(8,128)(2,1)S(1)}, bf16[48,1280]{1,0:T(8,128)(2,1)S(1)}, u32[]{:S(2)}, u32[]{:S(2)}) collective-permute-start(bf16[48,1280]{1,0:T(8,128)(2,1)S(1)} %collective-permute-done.3.refs_3_), channel_id=1, source_target_pairs={{0,8},{1,17},{2,10},{3,19},{4,12},{5,21},{6,14},{7,23},{8,0},{9,25... | collective-permute-start | bytes 368648 | tf_op jit(solution)/shard_map/ppermute | solution.py:219
  16.3 11.3 %collective-permute-start.2 = (bf16[96,1280]{1,0:T(8,128)(2,1)S(1)}, bf16[96,1280]{1,0:T(8,128)(2,1)S(1)}, u32[]{:S(2)}, u32[]{:S(2)}) collective-permute-start(bf16[96,1280]{1,0:T(8,128)(2,1)S(1)} %pad_maximum_fusion), channel_id=1, source_target_pairs={{0,16},{1,9},{2,18},{3,11},{4,20},{5,13},{6,22},{7,15},{8,24},{9,1... | collective-permute-start | bytes 737288 | tf_op jit(solution)/shard_map/ppermute | solution.py:219
  17.9 6.2 %collective-permute-start.8 = (bf16[48,1280]{1,0:T(8,128)(2,1)S(1)}, bf16[48,1280]{1,0:T(8,128)(2,1)S(1)}, u32[]{:S(2)}, u32[]{:S(2)}) collective-permute-start(bf16[48,1280]{1,0:T(8,128)(2,1)S(1)} %collective-permute-done.7.refs_0_), channel_id=1, source_target_pairs={{0,8},{1,17},{2,10},{3,19},{4,12},{5,21},{6,14},{7,23},{8,0},{9,25... | collective-permute-start | bytes 368648 | tf_op jit(solution)/shard_map/ppermute | solution.py:219
  19.7 7.0 %collective-permute-start.11 = (bf16[48,1280]{1,0:T(8,128)(2,1)S(1)}, bf16[48,1280]{1,0:T(8,128)(2,1)S(1)}, u32[]{:S(2)}, u32[]{:S(2)}) collective-permute-start(bf16[48,1280]{1,0:T(8,128)(2,1)S(1)} %collective-permute-done.10.refs_3_), channel_id=1, source_target_pairs={{0,8},{1,17},{2,10},{3,19},{4,12},{5,21},{6,14},{7,23},{8,0},{9,25... | collective-permute-start | bytes 368648 | tf_op jit(solution)/shard_map/ppermute | solution.py:219
  20.9 6.7 %collective-permute-start.5 = (bf16[96,1280]{1,0:T(8,128)(2,1)S(1)}, bf16[96,1280]{1,0:T(8,128)(2,1)S(1)}, u32[]{:S(2)}, u32[]{:S(2)}) collective-permute-start(bf16[96,1280]{1,0:T(8,128)(2,1)S(1)} %pad_maximum_fusion.1), channel_id=1, source_target_pairs={{0,16},{1,9},{2,18},{3,11},{4,20},{5,13},{6,22},{7,15},{8,24},{9,1... | collective-permute-start | bytes 737288 | tf_op jit(solution)/shard_map/ppermute | solution.py:219
  24.1 7.5 %collective-permute-start.9 = (bf16[96,1280]{1,0:T(8,128)(2,1)S(1)}, bf16[96,1280]{1,0:T(8,128)(2,1)S(1)}, u32[]{:S(2)}, u32[]{:S(2)}) collective-permute-start(bf16[96,1280]{1,0:T(8,128)(2,1)S(1)} %pad_maximum_fusion.2), channel_id=1, source_target_pairs={{0,16},{1,9},{2,18},{3,11},{4,20},{5,13},{6,22},{7,15},{8,24},{9,1... | collective-permute-start | bytes 737288 | tf_op jit(solution)/shard_map/ppermute | solution.py:219
  26.7 6.3 %collective-permute-start.12 = (bf16[96,1280]{1,0:T(8,128)(2,1)S(1)}, bf16[96,1280]{1,0:T(8,128)(2,1)S(1)}, u32[]{:S(2)}, u32[]{:S(2)}) collective-permute-start(bf16[96,1280]{1,0:T(8,128)(2,1)S(1)} %pad_maximum_fusion.3), channel_id=1, source_target_pairs={{0,16},{1,9},{2,18},{3,11},{4,20},{5,13},{6,22},{7,15},{8,24},{9,1... | collective-permute-start | bytes 737288 | tf_op jit(solution)/shard_map/ppermute | solution.py:219
  30.4 14.1 %collective-permute-start.6 = (bf16[192,640]{1,0:T(8,128)(2,1)S(1)}, bf16[192,640]{1,0:T(8,128)(2,1)S(1)}, u32[]{:S(2)}, u32[]{:S(2)}) collective-permute-start(bf16[192,640]{1,0:T(8,128)(2,1)S(1)} %get-tuple-element.31), channel_id=1, source_target_pairs={{0,16},{1,9},{2,18},{3,11},{4,20},{5,13},{6,22},{7,15},{8,24},{9,1... | collective-permute-start | bytes 737288 | tf_op jit(solution)/shard_map/ppermute | solution.py:219
  35.7 6.2 %collective-permute-start.13 = (bf16[96,640]{1,0:T(8,128)(2,1)S(1)}, bf16[96,640]{1,0:T(8,128)(2,1)S(1)}, u32[]{:S(2)}, u32[]{:S(2)}) collective-permute-start(bf16[96,640]{1,0:T(8,128)(2,1)S(1)} %get-tuple-element.33), channel_id=1, source_target_pairs={{0,8},{1,17},{2,10},{3,19},{4,12},{5,21},{6,14},{7,23},{8,0},{9,25... | collective-permute-start | bytes 368648 | tf_op jit(solution)/shard_map/ppermute | solution.py:219
  37.2 7.1 %collective-permute-start.16 = (bf16[96,640]{1,0:T(8,128)(2,1)S(1)}, bf16[96,640]{1,0:T(8,128)(2,1)S(1)}, u32[]{:S(2)}, u32[]{:S(2)}) collective-permute-start(bf16[96,640]{1,0:T(8,128)(2,1)S(1)} %get-tuple-element.35), channel_id=1, source_target_pairs={{0,16},{1,9},{2,18},{3,11},{4,20},{5,13},{6,22},{7,15},{8,24},{9,1... | collective-permute-start | bytes 368648 | tf_op jit(solution)/shard_map/ppermute | solution.py:219
  37.6 6.7 %collective-permute-start.17 = (bf16[96,640]{1,0:T(8,128)(2,1)S(1)}, bf16[96,640]{1,0:T(8,128)(2,1)S(1)}, u32[]{:S(2)}, u32[]{:S(2)}) collective-permute-start(bf16[96,640]{1,0:T(8,128)(2,1)S(1)} %get-tuple-element.36), channel_id=1, source_target_pairs={{0,24},{1,25},{2,26},{3,27},{4,28},{5,29},{6,30},{7,31},{8,16},{9,... | collective-permute-start | bytes 368648 | tf_op jit(solution)/shard_map/ppermute | solution.py:219
  44.5 4.9 %collective-permute-start.14 = (bf16[96,640]{1,0:T(8,128)(2,1)S(1)}, bf16[96,640]{1,0:T(8,128)(2,1)S(1)}, u32[]{:S(2)}, u32[]{:S(2)}) collective-permute-start(bf16[96,640]{1,0:T(8,128)(2,1)S(1)} %sum.2), channel_id=1, source_target_pairs={{0,8},{1,17},{2,10},{3,19},{4,12},{5,21},{6,14},{7,23},{8,0},{9,25... | collective-permute-start | bytes 368648 | tf_op jit(solution)/shard_map/ppermute | solution.py:219
  45.7 8.5 %collective-permute-start.19 = (bf16[48,640]{1,0:T(8,128)(2,1)S(1)}, bf16[48,640]{1,0:T(8,128)(2,1)S(1)}, u32[]{:S(2)}, u32[]{:S(2)}) collective-permute-start(bf16[48,640]{1,0:T(8,128)(2,1)S(1)} %get-tuple-element.57), channel_id=1, source_target_pairs={{0,6},{1,7},{2,4},{3,5},{4,2},{5,3},{6,0},{7,1},{8,14},{9,15},{10,... | collective-permute-start | bytes 184328 | tf_op jit(solution)/shard_map/ppermute | solution.py:211
  48.8 5.4 %collective-permute-start.18 = (bf16[48,640]{1,0:T(8,128)(2,1)S(1)}, bf16[48,640]{1,0:T(8,128)(2,1)S(1)}, u32[]{:S(2)}, u32[]{:S(2)}) collective-permute-start(bf16[48,640]{1,0:T(8,128)(2,1)S(1)} %get-tuple-element.58), channel_id=1, source_target_pairs={{0,4},{1,5},{2,6},{3,7},{4,0},{5,1},{6,2},{7,3},{8,12},{9,13},{10,... | collective-permute-start | bytes 184328 | tf_op jit(solution)/shard_map/ppermute | solution.py:211
  49.5 4.9 %collective-permute-start.15 = (bf16[48,640]{1,0:T(8,128)(2,1)S(1)}, bf16[48,640]{1,0:T(8,128)(2,1)S(1)}, u32[]{:S(2)}, u32[]{:S(2)}) collective-permute-start(bf16[48,640]{1,0:T(8,128)(2,1)S(1)} %get-tuple-element.59), channel_id=1, source_target_pairs={{0,2},{1,3},{2,0},{3,1},{4,6},{5,7},{6,4},{7,5},{8,10},{9,11},{10,... | collective-permute-start | bytes 184328 | tf_op jit(solution)/shard_map/ppermute | solution.py:211
  51.2 4.7 %copy-start = (s32[128,2]{0,1:T(2,128)S(1)}, s32[128,2]{0,1:T(2,128)}, u32[]{:S(2)}) copy-start(s32[128,2]{0,1:T(2,128)} %param.11) | copy-start | bytes 3076
  51.2 4.7 %copy-start.1 = (s32[128,2]{0,1:T(2,128)S(1)}, s32[128,2]{0,1:T(2,128)}, u32[]{:S(2)}) copy-start(s32[128,2]{0,1:T(2,128)} %param.12) | copy-start | bytes 3076
  51.2 4.7 %copy-start.2 = (s32[128,2]{0,1:T(2,128)S(1)}, s32[128,2]{0,1:T(2,128)}, u32[]{:S(2)}) copy-start(s32[128,2]{0,1:T(2,128)} %param.13) | copy-start | bytes 3076
  54.5 1.4 %collective-permute-start.20 = (bf16[96,640]{1,0:T(8,128)(2,1)S(1)}, bf16[96,640]{1,0:T(8,128)(2,1)S(1)}, u32[]{:S(2)}, u32[]{:S(2)}) collective-permute-start(bf16[96,640]{1,0:T(8,128)(2,1)S(1)} %get-tuple-element.46), channel_id=1, source_target_pairs={{0,1},{1,0},{2,3},{3,2},{4,5},{5,4},{6,7},{7,6},{8,9},{9,8},{10,11... | collective-permute-start | bytes 368648 | tf_op jit(solution)/shard_map/ppermute | solution.py:211

commit v5 on v4

--- a/solution.py
+++ b/solution.py
@@ -16,8 +16,8 @@
 DIRECT = (False, True)
 TILE = 1280
 C_CHUNK = 1.0
-C_LOAD = 1.0
-C_W = 1.0
+C_LOAD = 0.01
+C_W = 0.01
 LOAD = None
 WAIT_Z = False
 DEFER = 3
@@ -26,6 +26,7 @@
 Z1LAST = False
 W_AFTER = -1
 IN_TURN = True
+UP = False
 FIRST_SEND = True
 FIRST_LOAD = True
 HOLD2 = 0
@@ -329,7 +330,7 @@
         count = len(inside) * block
         total = groups * count
         if DIRECT[number]:
-            levels = [(p, p + 1) for p in range(1, groups)]
+            levels = [(p, p + 1) for p in (range(1, groups) if UP else reversed(range(1, groups)))]
         else:
             levels = [(1 << step, 2 << step) for step in reversed(range(steps))]
         outs = pl.pallas_call(

time: 57 us -> 56.3 us (0.988)
  waiting for transfers between devices: 14.6 us -> 13.1 us
  starting transfers between devices: 25.9 us -> 26.8 us
    ppermute x13, waiting for transfers between devices: 11.5 us -> 10.3 us  [swap_groups(): return lax.ppermute(value, ('dp', 'expert'), pairs)]
where the time goes in v5:
time: 56.3 us; the launch traced here: 56.2 us
  starting transfers between devices  26.8 us (48%)
  Pallas kernels  15.2 us (27%)
  waiting for transfers between devices  13.1 us (23%)
  between operations  0.79 us (1%)
    ppermute x13, starting transfers between devices, swap_groups(): return lax.ppermute(value, ('dp', 'expert'), pairs)  14.8 us
    ppermute x8, starting transfers between devices, swap(): return lax.ppermute(value, axis, [(i, i ^ offset) for i in range(size)])  12 us
    ppermute x13, waiting for transfers between devices, swap_groups(): return lax.ppermute(value, ('dp', 'expert'), pairs)  10.3 us
    pallas_call x2, Pallas kernels, body(): pl.pallas_call(functools.partial(chunk_kernel, TILE, groups, levels, plac...  5.26 us
    pallas_call x1, Pallas kernels, weight_out_call(): pl.pallas_call(functools.partial(weight_out_kernel, chunk_count, width),...  2.91 us
    ppermute x8, waiting for transfers between devices, swap(): return lax.ppermute(value, axis, [(i, i ^ offset) for i in range(size)])  2.77 us
    pallas_call x1, Pallas kernels, weight_in_call(): pl.pallas_call(functools.partial(weight_in_kernel, chunk_count, width), o...  2.65 us
    pallas_call x1, Pallas kernels, body(): pl.pallas_call(load_kernel, out_shape=(vmem_out(win.shape), vmem_out(wout...  1.94 us
  transfers between devices with their start and end apart: 21, of which 10 were waited for; matrix products, arithmetic and copies ran while one was open for 0% of the time, Pallas kernels for 23%

profile of v5, /device:TPU:0, one launch (start us, length us, event | category | flops | bytes accessed | tf_op | source)
XLA Modules:
  0.0 56.2 jit_solution(16792584599052261813)
XLA Ops:
  0.6 1.3 %dispatch.1 = (bf16[96,1280]{1,0:T(8,128)(2,1)S(1)}, bf16[96,1280]{1,0:T(8,128)(2,1)S(1)}) custom-call(bf16[128,640]{1,0:T(8,128)(2,1)} %refs_0_.1, bf16[128,640]{1,0:T(8,128)(2,1)} %refs_1_.1, f32[2,128]{1,0:T(2,128)} %bitcast.16, s32[2,128]{1,0:T(2,128)} %bitcast.8, s32[2,128]{1,0:T(2,128)} %bitcast.10, s32[2,128]{1,0:T(2,128)} %bitcast.12), custom_call_target="tpu_custom_call" | custom-call | tf_op jit(solution)/shard_map/dispatch/pallas_call | solution.py:245
  2.0 0.5 collective-permute-start
  2.5 1.1 %collective-permute-done.refs_2_ = bf16[96,1280]{1,0:T(8,128)(2,1)S(1)} collective-permute-done((bf16[96,1280]{1,0:T(8,128)(2,1)S(1)}, bf16[96,1280]{1,0:T(8,128)(2,1)S(1)}, u32[]{:S(2)}, u32[]{:S(2)}) %collective-permute-start) | collective-permute-done | bytes 245792 | tf_op jit(solution)/shard_map/ppermute | solution.py:212
  3.7 3.0 %collective-permute-start.3 = (bf16[48,1280]{1,0:T(8,128)(2,1)S(1)}, bf16[48,1280]{1,0:T(8,128)(2,1)S(1)}, u32[]{:S(2)}, u32[]{:S(2)}) collective-permute-start(bf16[48,1280]{1,0:T(8,128)(2,1)S(1)} %pad_maximum_fusion.5), channel_id=1, source_target_pairs={{0,2},{1,3},{2,0},{3,1},{4,6},{5,7},{6,4},{7,5},{8,10},{9,11},{10,... | collective-permute-start | bytes 368648 | tf_op jit(solution)/shard_map/ppermute | solution.py:212
  6.7 2.7 %collective-permute-start.7 = (bf16[48,1280]{1,0:T(8,128)(2,1)S(1)}, bf16[48,1280]{1,0:T(8,128)(2,1)S(1)}, u32[]{:S(2)}, u32[]{:S(2)}) collective-permute-start(bf16[48,1280]{1,0:T(8,128)(2,1)S(1)} %pad_maximum_fusion.6), channel_id=1, source_target_pairs={{0,4},{1,5},{2,6},{3,7},{4,0},{5,1},{6,2},{7,3},{8,12},{9,13},{10,... | collective-permute-start | bytes 368648 | tf_op jit(solution)/shard_map/ppermute | solution.py:212
  9.4 1.9 %load.1 = (bf16[640,1280]{1,0:T(8,128)(2,1)S(1)}, bf16[1280,640]{1,0:T(8,128)(2,1)S(1)}) custom-call(bf16[640,1280]{1,0:T(8,128)(2,1)} %bitcast.14, bf16[1280,640]{1,0:T(8,128)(2,1)} %bitcast.15, bf16[96,1280]{1,0:T(8,128)(2,1)S(1)} %collective-permute-done.refs_2_), custom_call_target="tpu_custom_call" | custom-call | bytes 65536 | tf_op jit(solution)/shard_map/load/pallas_call | solution.py:270
  11.3 1.6 %collective-permute-start.1 = (bf16[48,1280]{1,0:T(8,128)(2,1)S(1)}, bf16[48,1280]{1,0:T(8,128)(2,1)S(1)}, u32[]{:S(2)}, u32[]{:S(2)}) collective-permute-start(bf16[48,1280]{1,0:T(8,128)(2,1)S(1)} %join.1.refs_0_), channel_id=1, source_target_pairs={{0,8},{1,17},{2,10},{3,19},{4,12},{5,21},{6,14},{7,23},{8,0},{9,25... | collective-permute-start | bytes 368648 | tf_op jit(solution)/shard_map/ppermute | solution.py:220
  12.9 0.3 collective-permute-start.10
  13.2 0.0 collective-permute-done.3.refs_3_
  13.2 0.6 %collective-permute-start.4 = (bf16[48,1280]{1,0:T(8,128)(2,1)S(1)}, bf16[48,1280]{1,0:T(8,128)(2,1)S(1)}, u32[]{:S(2)}, u32[]{:S(2)}) collective-permute-start(bf16[48,1280]{1,0:T(8,128)(2,1)S(1)} %collective-permute-done.3.refs_3_), channel_id=1, source_target_pairs={{0,8},{1,17},{2,10},{3,19},{4,12},{5,21},{6,14},{7,23},{8,0},{9,25... | collective-permute-start | bytes 368648 | tf_op jit(solution)/shard_map/ppermute | solution.py:220
  13.8 2.5 %collective-permute-done.1.refs_1_ = bf16[48,1280]{1,0:T(8,128)(2,1)S(1)} collective-permute-done((bf16[48,1280]{1,0:T(8,128)(2,1)S(1)}, bf16[48,1280]{1,0:T(8,128)(2,1)S(1)}, u32[]{:S(2)}, u32[]{:S(2)}) %collective-permute-start.1) | collective-permute-done | bytes 122912 | tf_op jit(solution)/shard_map/ppermute | solution.py:220
  16.3 1.6 %collective-permute-start.2 = (bf16[96,1280]{1,0:T(8,128)(2,1)S(1)}, bf16[96,1280]{1,0:T(8,128)(2,1)S(1)}, u32[]{:S(2)}, u32[]{:S(2)}) collective-permute-start(bf16[96,1280]{1,0:T(8,128)(2,1)S(1)} %pad_maximum_fusion), channel_id=1, source_target_pairs={{0,16},{1,9},{2,18},{3,11},{4,20},{5,13},{6,22},{7,15},{8,24},{9,1... | collective-permute-start | bytes 737288 | tf_op jit(solution)/shard_map/ppermute | solution.py:220
  17.9 0.0 collective-permute-done.7.refs_0_
  17.9 1.5 %collective-permute-start.8 = (bf16[48,1280]{1,0:T(8,128)(2,1)S(1)}, bf16[48,1280]{1,0:T(8,128)(2,1)S(1)}, u32[]{:S(2)}, u32[]{:S(2)}) collective-permute-start(bf16[48,1280]{1,0:T(8,128)(2,1)S(1)} %collective-permute-done.7.refs_0_), channel_id=1, source_target_pairs={{0,8},{1,17},{2,10},{3,19},{4,12},{5,21},{6,14},{7,23},{8,0},{9,25... | collective-permute-start | bytes 368648 | tf_op jit(solution)/shard_map/ppermute | solution.py:220
  19.4 0.3 collective-permute-done.10.refs_3_
  19.7 1.2 %collective-permute-start.11 = (bf16[48,1280]{1,0:T(8,128)(2,1)S(1)}, bf16[48,1280]{1,0:T(8,128)(2,1)S(1)}, u32[]{:S(2)}, u32[]{:S(2)}) collective-permute-start(bf16[48,1280]{1,0:T(8,128)(2,1)S(1)} %collective-permute-done.10.refs_3_), channel_id=1, source_target_pairs={{0,8},{1,17},{2,10},{3,19},{4,12},{5,21},{6,14},{7,23},{8,0},{9,25... | collective-permute-start | bytes 368648 | tf_op jit(solution)/shard_map/ppermute | solution.py:220
  20.9 0.0 collective-permute-done.4.refs_4_
  21.0 0.9 %collective-permute-start.5 = (bf16[96,1280]{1,0:T(8,128)(2,1)S(1)}, bf16[96,1280]{1,0:T(8,128)(2,1)S(1)}, u32[]{:S(2)}, u32[]{:S(2)}) collective-permute-start(bf16[96,1280]{1,0:T(8,128)(2,1)S(1)} %pad_maximum_fusion.1), channel_id=1, source_target_pairs={{0,16},{1,9},{2,18},{3,11},{4,20},{5,13},{6,22},{7,15},{8,24},{9,1... | collective-permute-start | bytes 737288 | tf_op jit(solution)/shard_map/ppermute | solution.py:220
  21.9 2.2 %collective-permute-done.8.refs_1_ = bf16[48,1280]{1,0:T(8,128)(2,1)S(1)} collective-permute-done((bf16[48,1280]{1,0:T(8,128)(2,1)S(1)}, bf16[48,1280]{1,0:T(8,128)(2,1)S(1)}, u32[]{:S(2)}, u32[]{:S(2)}) %collective-permute-start.8) | collective-permute-done | bytes 122912 | tf_op jit(solution)/shard_map/ppermute | solution.py:220
  24.1 0.1 collective-permute-start.9
  24.2 2.5 %collective-permute-done.11.refs_4_ = bf16[48,1280]{1,0:T(8,128)(2,1)S(1)} collective-permute-done((bf16[48,1280]{1,0:T(8,128)(2,1)S(1)}, bf16[48,1280]{1,0:T(8,128)(2,1)S(1)}, u32[]{:S(2)}, u32[]{:S(2)}) %collective-permute-start.11) | collective-permute-done | bytes 122912 | tf_op jit(solution)/shard_map/ppermute | solution.py:220
  26.7 0.9 %collective-permute-start.12 = (bf16[96,1280]{1,0:T(8,128)(2,1)S(1)}, bf16[96,1280]{1,0:T(8,128)(2,1)S(1)}, u32[]{:S(2)}, u32[]{:S(2)}) collective-permute-start(bf16[96,1280]{1,0:T(8,128)(2,1)S(1)} %pad_maximum_fusion.3), channel_id=1, source_target_pairs={{0,16},{1,9},{2,18},{3,11},{4,20},{5,13},{6,22},{7,15},{8,24},{9,1... | collective-permute-start | bytes 737288 | tf_op jit(solution)/shard_map/ppermute | solution.py:220
  27.6 0.0 collective-permute-done.2.refs_2_
  27.6 0.0 collective-permute-done.5.refs_5_
  27.6 2.7 %chunk.2 = (bf16[192,640]{1,0:T(8,128)(2,1)S(1)}, bf16[96,640]{1,0:T(8,128)(2,1)S(1)}, bf16[96,640]{1,0:T(8,128)(2,1)S(1)}, bf16[384,1280]{1,0:T(8,128)(2,1)S(1)...) custom-call(bf16[48,1280]{1,0:T(8,128)(2,1)S(1)} %join.1.refs_0_, ...), custom_call_target="tpu_custom_call" | custom-call | flops 1887436800 | bytes 3276800 | tf_op jit(solution)/shard_map/chunk/pallas_call | solution.py:336
  30.3 1.3 %collective-permute-start.6 = (bf16[192,640]{1,0:T(8,128)(2,1)S(1)}, bf16[192,640]{1,0:T(8,128)(2,1)S(1)}, u32[]{:S(2)}, u32[]{:S(2)}) collective-permute-start(bf16[192,640]{1,0:T(8,128)(2,1)S(1)} %get-tuple-element.31), channel_id=1, source_target_pairs={{0,16},{1,9},{2,18},{3,11},{4,20},{5,13},{6,22},{7,15},{8,24},{9,1... | collective-permute-start | bytes 737288 | tf_op jit(solution)/shard_map/ppermute | solution.py:220
  31.6 0.0 collective-permute-done.9.refs_2_
  31.6 1.4 %collective-permute-done.12.refs_5_ = bf16[96,1280]{1,0:T(8,128)(2,1)S(1)} collective-permute-done((bf16[96,1280]{1,0:T(8,128)(2,1)S(1)}, bf16[96,1280]{1,0:T(8,128)(2,1)S(1)}, u32[]{:S(2)}, u32[]{:S(2)}) %collective-permute-start.12) | collective-permute-done | bytes 245792 | tf_op jit(solution)/shard_map/ppermute | solution.py:220
  33.0 2.6 %chunk.3 = (bf16[96,640]{1,0:T(8,128)(2,1)S(1)}, bf16[96,640]{1,0:T(8,128)(2,1)S(1)}, bf16[96,640]{1,0:T(8,128)(2,1)S(1)}, bf16[96,640]{1,0:T(8,128)(2,1)S(1)}, ...) custom-call(bf16[48,1280]{1,0:T(8,128)(2,1)S(1)} %collective-permute-done.7.refs_0_, ...), custom_call_target="tpu_custom_call" | custom-call | flops 1887436800 | bytes 3276800 | tf_op jit(solution)/shard_map/chunk/pallas_call | solution.py:336
  35.6 1.4 %collective-permute-start.13 = (bf16[96,640]{1,0:T(8,128)(2,1)S(1)}, bf16[96,640]{1,0:T(8,128)(2,1)S(1)}, u32[]{:S(2)}, u32[]{:S(2)}) collective-permute-start(bf16[96,640]{1,0:T(8,128)(2,1)S(1)} %get-tuple-element.33), channel_id=1, source_target_pairs={{0,24},{1,25},{2,26},{3,27},{4,28},{5,29},{6,30},{7,31},{8,16},{9,... | collective-permute-start | bytes 368648 | tf_op jit(solution)/shard_map/ppermute | solution.py:220
  37.0 1.6 %collective-permute-start.16 = (bf16[96,640]{1,0:T(8,128)(2,1)S(1)}, bf16[96,640]{1,0:T(8,128)(2,1)S(1)}, u32[]{:S(2)}, u32[]{:S(2)}) collective-permute-start(bf16[96,640]{1,0:T(8,128)(2,1)S(1)} %get-tuple-element.35), channel_id=1, source_target_pairs={{0,16},{1,9},{2,18},{3,11},{4,20},{5,13},{6,22},{7,15},{8,24},{9,1... | collective-permute-start | bytes 368648 | tf_op jit(solution)/shard_map/ppermute | solution.py:220
  38.6 0.6 %collective-permute-start.17 = (bf16[96,640]{1,0:T(8,128)(2,1)S(1)}, bf16[96,640]{1,0:T(8,128)(2,1)S(1)}, u32[]{:S(2)}, u32[]{:S(2)}) collective-permute-start(bf16[96,640]{1,0:T(8,128)(2,1)S(1)} %get-tuple-element.36), channel_id=1, source_target_pairs={{0,8},{1,17},{2,10},{3,19},{4,12},{5,21},{6,14},{7,23},{8,0},{9,25... | collective-permute-start | bytes 368648 | tf_op jit(solution)/shard_map/ppermute | solution.py:220
  39.2 2.7 %weight_in_grad.1 = (bf16[640,1280]{1,0:T(8,128)(2,1)}, bf16[16,128]{1,0:T(8,128)(2,1)S(1)}) custom-call(bf16[384,1280]{1,0:T(8,128)(2,1)S(1)} %get-tuple-element.37.refs_0_, bf16[384,1280]{1,0:T(8,128)(2,1)S(1)} %get-tuple-element.38.refs_1_, bf16[384,1280]{1,0:T(8,128)(2,1)S(1)} %get-tuple-element.39.refs_2_, ...), custom_call_target="tpu_custom_call" | custom-call | flops 12582912 | bytes 16384 | tf_op jit(solution)/shard_map/weight_in_grad/pallas_call | solution.py:290
  41.8 0.4 collective-permute-done.13.refs_2_.refs_1_
  42.2 1.2 %collective-permute-done.16.refs_2_ = bf16[96,640]{1,0:T(8,128)(2,1)S(1)} collective-permute-done((bf16[96,640]{1,0:T(8,128)(2,1)S(1)}, bf16[96,640]{1,0:T(8,128)(2,1)S(1)}, u32[]{:S(2)}, u32[]{:S(2)}) %collective-permute-start.16) | collective-permute-done | bytes 122912 | tf_op jit(solution)/shard_map/ppermute | solution.py:220
  43.4 0.1 collective-permute-done.17.refs_3_
  43.5 0.1 sum.3.refs_4_
  43.5 0.0 collective-permute-done.6
  43.6 1.7 %collective-permute-start.14 = (bf16[96,640]{1,0:T(8,128)(2,1)S(1)}, bf16[96,640]{1,0:T(8,128)(2,1)S(1)}, u32[]{:S(2)}, u32[]{:S(2)}) collective-permute-start(bf16[96,640]{1,0:T(8,128)(2,1)S(1)} %sum.2), channel_id=1, source_target_pairs={{0,8},{1,17},{2,10},{3,19},{4,12},{5,21},{6,14},{7,23},{8,0},{9,25... | collective-permute-start | bytes 368648 | tf_op jit(solution)/shard_map/ppermute | solution.py:220
  45.3 3.0 %collective-permute-start.19 = (bf16[48,640]{1,0:T(8,128)(2,1)S(1)}, bf16[48,640]{1,0:T(8,128)(2,1)S(1)}, u32[]{:S(2)}, u32[]{:S(2)}) collective-permute-start(bf16[48,640]{1,0:T(8,128)(2,1)S(1)} %get-tuple-element.57), channel_id=1, source_target_pairs={{0,6},{1,7},{2,4},{3,5},{4,2},{5,3},{6,0},{7,1},{8,14},{9,15},{10,... | collective-permute-start | bytes 184328 | tf_op jit(solution)/shard_map/ppermute | solution.py:212
  48.3 0.3 collective-permute-start.18
  48.6 0.0 collective-permute-done.14
  48.6 0.1 add_convert_fusion
  48.6 2.2 %collective-permute-start.15 = (bf16[48,640]{1,0:T(8,128)(2,1)S(1)}, bf16[48,640]{1,0:T(8,128)(2,1)S(1)}, u32[]{:S(2)}, u32[]{:S(2)}) collective-permute-start(bf16[48,640]{1,0:T(8,128)(2,1)S(1)} %get-tuple-element.59), channel_id=1, source_target_pairs={{0,2},{1,3},{2,0},{3,1},{4,6},{5,7},{6,4},{7,5},{8,10},{9,11},{10,... | collective-permute-start | bytes 184328 | tf_op jit(solution)/shard_map/ppermute | solution.py:212
  50.8 0.0 copy-start
  50.8 0.0 copy-start.1
  50.8 0.0 copy-start.2
  50.8 2.9 %weight_out_grad.1 = (bf16[1280,640]{1,0:T(8,128)(2,1)}, bf16[16,128]{1,0:T(8,128)(2,1)S(1)}) custom-call(bf16[384,1280]{1,0:T(8,128)(2,1)S(1)} %get-tuple-element.37.refs_0_, bf16[384,1280]{1,0:T(8,128)(2,1)S(1)} %get-tuple-element.38.refs_1_, bf16[384,1280]{1,0:T(8,128)(2,1)S(1)} %get-tuple-element.42.refs_2_, ...), custom_call_target="tpu_custom_call" | custom-call | flops 12582912 | bytes 16384 | tf_op jit(solution)/shard_map/weight_out_grad/pallas_call | solution.py:298
  53.7 0.0 collective-permute-done.19.refs_3_
  53.8 0.0 collective-permute-done.18.refs_2_
  53.8 0.0 collective-permute-done.15.refs_1_
  53.8 0.1 collective-permute-start.20
  53.9 1.3 %collective-permute-done.20.other_ref = bf16[96,640]{1,0:T(8,128)(2,1)S(1)} collective-permute-done((bf16[96,640]{1,0:T(8,128)(2,1)S(1)}, bf16[96,640]{1,0:T(8,128)(2,1)S(1)}, u32[]{:S(2)}, u32[]{:S(2)}) %collective-permute-start.20) | collective-permute-done | bytes 122912 | tf_op jit(solution)/shard_map/ppermute | solution.py:212
  55.2 0.0 copy-done
  55.2 0.0 copy-done.1
  55.2 0.0 copy-done.2
  55.2 1.0 %combine.1 = bf16[128,640]{1,0:T(8,128)(2,1)} custom-call(bf16[96,640]{1,0:T(8,128)(2,1)S(1)} %get-tuple-element.45.own_ref, bf16[96,640]{1,0:T(8,128)(2,1)S(1)} %collective-permute-done.20.other_ref, s32[2,128]{1,0:T(2,128)S(1)} %bitcast.9, s32[2,128]{1,0:T(2,128)S(1)} %bitcast.11, s32[2,128]{1,0:T(2,128)S(1)} %bitcast.13), custom_call_target="tpu_custom_call" | custom-call | tf_op jit(solution)/shard_map/combine/pallas_call | solution.py:402
  (16 shorter events, 0.3 us)
Async XLA Ops:
  2.0 1.7 %collective-permute-start = (bf16[96,1280]{1,0:T(8,128)(2,1)S(1)}, bf16[96,1280]{1,0:T(8,128)(2,1)S(1)}, u32[]{:S(2)}, u32[]{:S(2)}) collective-permute-start(bf16[96,1280]{1,0:T(8,128)(2,1)S(1)} %get-tuple-element.27), channel_id=1, source_target_pairs={{0,1},{1,0},{2,3},{3,2},{4,5},{5,4},{6,7},{7,6},{8,9},{9,8},{10,11... | collective-permute-start | bytes 737288 | tf_op jit(solution)/shard_map/ppermute | solution.py:212
  3.7 9.5 %collective-permute-start.3 = (bf16[48,1280]{1,0:T(8,128)(2,1)S(1)}, bf16[48,1280]{1,0:T(8,128)(2,1)S(1)}, u32[]{:S(2)}, u32[]{:S(2)}) collective-permute-start(bf16[48,1280]{1,0:T(8,128)(2,1)S(1)} %pad_maximum_fusion.5), channel_id=1, source_target_pairs={{0,2},{1,3},{2,0},{3,1},{4,6},{5,7},{6,4},{7,5},{8,10},{9,11},{10,... | collective-permute-start | bytes 368648 | tf_op jit(solution)/shard_map/ppermute | solution.py:212
  6.7 11.2 %collective-permute-start.7 = (bf16[48,1280]{1,0:T(8,128)(2,1)S(1)}, bf16[48,1280]{1,0:T(8,128)(2,1)S(1)}, u32[]{:S(2)}, u32[]{:S(2)}) collective-permute-start(bf16[48,1280]{1,0:T(8,128)(2,1)S(1)} %pad_maximum_fusion.6), channel_id=1, source_target_pairs={{0,4},{1,5},{2,6},{3,7},{4,0},{5,1},{6,2},{7,3},{8,12},{9,13},{10,... | collective-permute-start | bytes 368648 | tf_op jit(solution)/shard_map/ppermute | solution.py:212
  11.3 4.9 %collective-permute-start.1 = (bf16[48,1280]{1,0:T(8,128)(2,1)S(1)}, bf16[48,1280]{1,0:T(8,128)(2,1)S(1)}, u32[]{:S(2)}, u32[]{:S(2)}) collective-permute-start(bf16[48,1280]{1,0:T(8,128)(2,1)S(1)} %join.1.refs_0_), channel_id=1, source_target_pairs={{0,8},{1,17},{2,10},{3,19},{4,12},{5,21},{6,14},{7,23},{8,0},{9,25... | collective-permute-start | bytes 368648 | tf_op jit(solution)/shard_map/ppermute | solution.py:220
  12.9 6.8 %collective-permute-start.10 = (bf16[48,1280]{1,0:T(8,128)(2,1)S(1)}, bf16[48,1280]{1,0:T(8,128)(2,1)S(1)}, u32[]{:S(2)}, u32[]{:S(2)}) collective-permute-start(bf16[48,1280]{1,0:T(8,128)(2,1)S(1)} %pad_maximum_fusion.7), channel_id=1, source_target_pairs={{0,6},{1,7},{2,4},{3,5},{4,2},{5,3},{6,0},{7,1},{8,14},{9,15},{10,... | collective-permute-start | bytes 368648 | tf_op jit(solution)/shard_map/ppermute | solution.py:212
  13.2 7.7 %collective-permute-start.4 = (bf16[48,1280]{1,0:T(8,128)(2,1)S(1)}, bf16[48,1280]{1,0:T(8,128)(2,1)S(1)}, u32[]{:S(2)}, u32[]{:S(2)}) collective-permute-start(bf16[48,1280]{1,0:T(8,128)(2,1)S(1)} %collective-permute-done.3.refs_3_), channel_id=1, source_target_pairs={{0,8},{1,17},{2,10},{3,19},{4,12},{5,21},{6,14},{7,23},{8,0},{9,25... | collective-permute-start | bytes 368648 | tf_op jit(solution)/shard_map/ppermute | solution.py:220
  16.3 11.3 %collective-permute-start.2 = (bf16[96,1280]{1,0:T(8,128)(2,1)S(1)}, bf16[96,1280]{1,0:T(8,128)(2,1)S(1)}, u32[]{:S(2)}, u32[]{:S(2)}) collective-permute-start(bf16[96,1280]{1,0:T(8,128)(2,1)S(1)} %pad_maximum_fusion), channel_id=1, source_target_pairs={{0,16},{1,9},{2,18},{3,11},{4,20},{5,13},{6,22},{7,15},{8,24},{9,1... | collective-permute-start | bytes 737288 | tf_op jit(solution)/shard_map/ppermute | solution.py:220
  17.9 6.2 %collective-permute-start.8 = (bf16[48,1280]{1,0:T(8,128)(2,1)S(1)}, bf16[48,1280]{1,0:T(8,128)(2,1)S(1)}, u32[]{:S(2)}, u32[]{:S(2)}) collective-permute-start(bf16[48,1280]{1,0:T(8,128)(2,1)S(1)} %collective-permute-done.7.refs_0_), channel_id=1, source_target_pairs={{0,8},{1,17},{2,10},{3,19},{4,12},{5,21},{6,14},{7,23},{8,0},{9,25... | collective-permute-start | bytes 368648 | tf_op jit(solution)/shard_map/ppermute | solution.py:220
  19.7 7.0 %collective-permute-start.11 = (bf16[48,1280]{1,0:T(8,128)(2,1)S(1)}, bf16[48,1280]{1,0:T(8,128)(2,1)S(1)}, u32[]{:S(2)}, u32[]{:S(2)}) collective-permute-start(bf16[48,1280]{1,0:T(8,128)(2,1)S(1)} %collective-permute-done.10.refs_3_), channel_id=1, source_target_pairs={{0,8},{1,17},{2,10},{3,19},{4,12},{5,21},{6,14},{7,23},{8,0},{9,25... | collective-permute-start | bytes 368648 | tf_op jit(solution)/shard_map/ppermute | solution.py:220
  21.0 6.7 %collective-permute-start.5 = (bf16[96,1280]{1,0:T(8,128)(2,1)S(1)}, bf16[96,1280]{1,0:T(8,128)(2,1)S(1)}, u32[]{:S(2)}, u32[]{:S(2)}) collective-permute-start(bf16[96,1280]{1,0:T(8,128)(2,1)S(1)} %pad_maximum_fusion.1), channel_id=1, source_target_pairs={{0,16},{1,9},{2,18},{3,11},{4,20},{5,13},{6,22},{7,15},{8,24},{9,1... | collective-permute-start | bytes 737288 | tf_op jit(solution)/shard_map/ppermute | solution.py:220
  24.1 7.5 %collective-permute-start.9 = (bf16[96,1280]{1,0:T(8,128)(2,1)S(1)}, bf16[96,1280]{1,0:T(8,128)(2,1)S(1)}, u32[]{:S(2)}, u32[]{:S(2)}) collective-permute-start(bf16[96,1280]{1,0:T(8,128)(2,1)S(1)} %pad_maximum_fusion.2), channel_id=1, source_target_pairs={{0,16},{1,9},{2,18},{3,11},{4,20},{5,13},{6,22},{7,15},{8,24},{9,1... | collective-permute-start | bytes 737288 | tf_op jit(solution)/shard_map/ppermute | solution.py:220
  26.7 6.3 %collective-permute-start.12 = (bf16[96,1280]{1,0:T(8,128)(2,1)S(1)}, bf16[96,1280]{1,0:T(8,128)(2,1)S(1)}, u32[]{:S(2)}, u32[]{:S(2)}) collective-permute-start(bf16[96,1280]{1,0:T(8,128)(2,1)S(1)} %pad_maximum_fusion.3), channel_id=1, source_target_pairs={{0,16},{1,9},{2,18},{3,11},{4,20},{5,13},{6,22},{7,15},{8,24},{9,1... | collective-permute-start | bytes 737288 | tf_op jit(solution)/shard_map/ppermute | solution.py:220
  30.3 13.2 %collective-permute-start.6 = (bf16[192,640]{1,0:T(8,128)(2,1)S(1)}, bf16[192,640]{1,0:T(8,128)(2,1)S(1)}, u32[]{:S(2)}, u32[]{:S(2)}) collective-permute-start(bf16[192,640]{1,0:T(8,128)(2,1)S(1)} %get-tuple-element.31), channel_id=1, source_target_pairs={{0,16},{1,9},{2,18},{3,11},{4,20},{5,13},{6,22},{7,15},{8,24},{9,1... | collective-permute-start | bytes 737288 | tf_op jit(solution)/shard_map/ppermute | solution.py:220
  35.6 6.6 %collective-permute-start.13 = (bf16[96,640]{1,0:T(8,128)(2,1)S(1)}, bf16[96,640]{1,0:T(8,128)(2,1)S(1)}, u32[]{:S(2)}, u32[]{:S(2)}) collective-permute-start(bf16[96,640]{1,0:T(8,128)(2,1)S(1)} %get-tuple-element.33), channel_id=1, source_target_pairs={{0,24},{1,25},{2,26},{3,27},{4,28},{5,29},{6,30},{7,31},{8,16},{9,... | collective-permute-start | bytes 368648 | tf_op jit(solution)/shard_map/ppermute | solution.py:220
  37.0 6.4 %collective-permute-start.16 = (bf16[96,640]{1,0:T(8,128)(2,1)S(1)}, bf16[96,640]{1,0:T(8,128)(2,1)S(1)}, u32[]{:S(2)}, u32[]{:S(2)}) collective-permute-start(bf16[96,640]{1,0:T(8,128)(2,1)S(1)} %get-tuple-element.35), channel_id=1, source_target_pairs={{0,16},{1,9},{2,18},{3,11},{4,20},{5,13},{6,22},{7,15},{8,24},{9,1... | collective-permute-start | bytes 368648 | tf_op jit(solution)/shard_map/ppermute | solution.py:220
  38.6 4.9 %collective-permute-start.17 = (bf16[96,640]{1,0:T(8,128)(2,1)S(1)}, bf16[96,640]{1,0:T(8,128)(2,1)S(1)}, u32[]{:S(2)}, u32[]{:S(2)}) collective-permute-start(bf16[96,640]{1,0:T(8,128)(2,1)S(1)} %get-tuple-element.36), channel_id=1, source_target_pairs={{0,8},{1,17},{2,10},{3,19},{4,12},{5,21},{6,14},{7,23},{8,0},{9,25... | collective-permute-start | bytes 368648 | tf_op jit(solution)/shard_map/ppermute | solution.py:220
  43.6 5.0 %collective-permute-start.14 = (bf16[96,640]{1,0:T(8,128)(2,1)S(1)}, bf16[96,640]{1,0:T(8,128)(2,1)S(1)}, u32[]{:S(2)}, u32[]{:S(2)}) collective-permute-start(bf16[96,640]{1,0:T(8,128)(2,1)S(1)} %sum.2), channel_id=1, source_target_pairs={{0,8},{1,17},{2,10},{3,19},{4,12},{5,21},{6,14},{7,23},{8,0},{9,25... | collective-permute-start | bytes 368648 | tf_op jit(solution)/shard_map/ppermute | solution.py:220
  45.3 8.5 %collective-permute-start.19 = (bf16[48,640]{1,0:T(8,128)(2,1)S(1)}, bf16[48,640]{1,0:T(8,128)(2,1)S(1)}, u32[]{:S(2)}, u32[]{:S(2)}) collective-permute-start(bf16[48,640]{1,0:T(8,128)(2,1)S(1)} %get-tuple-element.57), channel_id=1, source_target_pairs={{0,6},{1,7},{2,4},{3,5},{4,2},{5,3},{6,0},{7,1},{8,14},{9,15},{10,... | collective-permute-start | bytes 184328 | tf_op jit(solution)/shard_map/ppermute | solution.py:212
  48.3 5.5 %collective-permute-start.18 = (bf16[48,640]{1,0:T(8,128)(2,1)S(1)}, bf16[48,640]{1,0:T(8,128)(2,1)S(1)}, u32[]{:S(2)}, u32[]{:S(2)}) collective-permute-start(bf16[48,640]{1,0:T(8,128)(2,1)S(1)} %get-tuple-element.58), channel_id=1, source_target_pairs={{0,4},{1,5},{2,6},{3,7},{4,0},{5,1},{6,2},{7,3},{8,12},{9,13},{10,... | collective-permute-start | bytes 184328 | tf_op jit(solution)/shard_map/ppermute | solution.py:212
  48.6 5.1 %collective-permute-start.15 = (bf16[48,640]{1,0:T(8,128)(2,1)S(1)}, bf16[48,640]{1,0:T(8,128)(2,1)S(1)}, u32[]{:S(2)}, u32[]{:S(2)}) collective-permute-start(bf16[48,640]{1,0:T(8,128)(2,1)S(1)} %get-tuple-element.59), channel_id=1, source_target_pairs={{0,2},{1,3},{2,0},{3,1},{4,6},{5,7},{6,4},{7,5},{8,10},{9,11},{10,... | collective-permute-start | bytes 184328 | tf_op jit(solution)/shard_map/ppermute | solution.py:212
  50.8 4.4 %copy-start = (s32[128,2]{0,1:T(2,128)S(1)}, s32[128,2]{0,1:T(2,128)}, u32[]{:S(2)}) copy-start(s32[128,2]{0,1:T(2,128)} %param.11) | copy-start | bytes 3076
  50.8 4.4 %copy-start.1 = (s32[128,2]{0,1:T(2,128)S(1)}, s32[128,2]{0,1:T(2,128)}, u32[]{:S(2)}) copy-start(s32[128,2]{0,1:T(2,128)} %param.12) | copy-start | bytes 3076
  50.8 4.4 %copy-start.2 = (s32[128,2]{0,1:T(2,128)S(1)}, s32[128,2]{0,1:T(2,128)}, u32[]{:S(2)}) copy-start(s32[128,2]{0,1:T(2,128)} %param.13) | copy-start | bytes 3076
  53.8 1.4 %collective-permute-start.20 = (bf16[96,640]{1,0:T(8,128)(2,1)S(1)}, bf16[96,640]{1,0:T(8,128)(2,1)S(1)}, u32[]{:S(2)}, u32[]{:S(2)}) collective-permute-start(bf16[96,640]{1,0:T(8,128)(2,1)S(1)} %get-tuple-element.46), channel_id=1, source_target_pairs={{0,1},{1,0},{2,3},{3,2},{4,5},{5,4},{6,7},{7,6},{8,9},{9,8},{10,11... | collective-permute-start | bytes 368648 | tf_op jit(solution)/shard_map/ppermute | solution.py:212

commit v6 on v5

--- a/solution.py
+++ b/solution.py
@@ -153,13 +153,18 @@
     done_ref[...] = jnp.zeros(done_ref.shape, bf16)
 
 
-def weight_out_kernel(count, width, *refs):
+def weight_out_kernel(count, width, part, *refs):
+    out_ref, done_ref, held_ref, sem = refs[-4:]
+    size = held_ref.shape[0]
+    span = slice(part * size, (part + 1) * size)
     cot = stacked(refs[:count], slice(width, 2 * width))
-    hidden = stacked(refs[count : 2 * count], slice(None))
-    out_ref, done_ref = refs[-2:]
+    hidden = stacked(refs[count : 2 * count], span)
     total = lax.dot_general(hidden, cot, (((0,), (0,)), ((), ())), preferred_element_type=f32)
-    out_ref[...] = total.astype(bf16)
+    held_ref[...] = total.astype(bf16)
+    copy = pltpu.make_async_copy(held_ref, out_ref.at[span], sem)
+    copy.start()
     done_ref[...] = jnp.zeros(done_ref.shape, bf16)
+    copy.wait()
 
 
 def join_kernel(count, *refs):
@@ -294,13 +299,20 @@
             **weight_call,
         )(*all_rows, *all_pre, after)
 
-    def weight_out_call(after):
+    def weight_out_call(part, after, prior=()):
+        in_hbm_spec = pl.BlockSpec(memory_space=pltpu.HBM)
+        operands = (*all_rows, *all_hidden, after, *prior)
         return pl.pallas_call(
-            functools.partial(weight_out_kernel, chunk_count, width),
+            functools.partial(weight_out_kernel, chunk_count, width, part),
             out_shape=(jax.ShapeDtypeStruct((hidden_total, width), bf16), vmem_out((16, 128))),
+            in_specs=[vmem_whole] * (2 * chunk_count) + [anywhere] + [in_hbm_spec] * len(prior),
+            out_specs=(in_hbm_spec, vmem_whole),
+            scratch_shapes=[pltpu.VMEM((hidden_total // 2, width), bf16), pltpu.SemaphoreType.DMA],
+            input_output_aliases={len(operands) - 1: 0} if prior else {},
+            compiler_params=params(40),
+            cost_estimate=cost(int(C_W * all_count * width * hidden_total), int(C_W * width * hidden_total)),
             name="weight_out_grad",
-            **weight_call,
-        )(*all_rows, *all_hidden, after)
+        )(*operands)
 
     deferred = []
     for number, chunk in enumerate(chunks):
@@ -381,6 +393,7 @@
     if DEFER != 4:
         terms = rest(last, firsts[last], kept_last)
     grad_in, done = weight_in_call({0: sums_of[0], -1: kept_last}.get(W_AFTER, terms[W_AFTER]))
+    half_out, done = weight_out_call(0, done)
     sums_of.append(add_rows(terms, done))
     for (inside, *_), summed in zip(deferred, sums_of, strict=True):
         if Z1LAST and summed is not sums_of[-1]:
@@ -389,7 +402,7 @@
             piece = summed[i * block : (i + 1) * block]
             returned[m] = piece if m == 0 else swap(piece, "expert", 2 * m)
 
-    grad_out, done = weight_out_call(sums_of[-1])
+    grad_out, done = weight_out_call(1, sums_of[-1], (half_out,))
     back_own, for_partner = pl.pallas_call(
         functools.partial(pack_kernel, slot_cap),
         out_shape=(vmem_out((half, width)),) * 2,

time: 56.3 us -> 56.7 us (level)
  Pallas kernels: 15.2 us -> 16.2 us
    ppermute x13, waiting for transfers between devices: 10.3 us -> 8.62 us  [swap_groups(): return lax.ppermute(value, ('dp', 'expert'), pairs)]
    ppermute x8, waiting for transfers between devices: 2.77 us -> 4.14 us  [swap(): return lax.ppermute(value, axis, [(i, i ^ offset) for i in range(size)])]
    pallas_call x1 -> x2, Pallas kernels: 2.91 us -> 3.74 us  [weight_out_call(): pl.pallas_call(functools.partial(weight_out_kernel, chunk_count, width, p...]
  transfers between devices with their start and end apart: 21 -> 21, of which waited for: 10 -> 8; matrix products, arithmetic and copies ran while one was open for 0% -> 0% of each run, Pallas kernels for 23% -> 24%
where the time goes in v6:
time: 56.7 us; the launch traced here: 56.6 us
  starting transfers between devices  26.5 us (47%)
  Pallas kernels  16.2 us (29%)
  waiting for transfers between devices  12.8 us (23%)
  between operations  0.84 us (1%)
    ppermute x13, starting transfers between devices, swap_groups(): return lax.ppermute(value, ('dp', 'expert'), pairs)  14.7 us
    ppermute x8, starting transfers between devices, swap(): return lax.ppermute(value, axis, [(i, i ^ offset) for i in range(size)])  11.9 us
    ppermute x13, waiting for transfers between devices, swap_groups(): return lax.ppermute(value, ('dp', 'expert'), pairs)  8.62 us
    pallas_call x2, Pallas kernels, body(): pl.pallas_call(functools.partial(chunk_kernel, TILE, groups, levels, plac...  5.38 us
    ppermute x8, waiting for transfers between devices, swap(): return lax.ppermute(value, axis, [(i, i ^ offset) for i in range(size)])  4.14 us
    pallas_call x2, Pallas kernels, weight_out_call(): pl.pallas_call(functools.partial(weight_out_kernel, chunk_count, width, p...  3.74 us
    pallas_call x1, Pallas kernels, weight_in_call(): pl.pallas_call(functools.partial(weight_in_kernel, chunk_count, width), o...  2.66 us
    pallas_call x1, Pallas kernels, body(): pl.pallas_call(load_kernel, out_shape=(vmem_out(win.shape), vmem_out(wout...  1.94 us
  transfers between devices with their start and end apart: 21, of which 8 were waited for; matrix products, arithmetic and copies ran while one was open for 0% of the time, Pallas kernels for 24%

profile of v6, /device:TPU:0, one launch (start us, length us, event | category | flops | bytes accessed | tf_op | source)
XLA Modules:
  0.0 56.6 jit_solution(7046638762108568952)
XLA Ops:
  0.6 1.3 %dispatch.1 = (bf16[96,1280]{1,0:T(8,128)(2,1)S(1)}, bf16[96,1280]{1,0:T(8,128)(2,1)S(1)}) custom-call(bf16[128,640]{1,0:T(8,128)(2,1)} %refs_0_.1, bf16[128,640]{1,0:T(8,128)(2,1)} %refs_1_.1, f32[2,128]{1,0:T(2,128)} %bitcast.17, s32[2,128]{1,0:T(2,128)} %bitcast.8, s32[2,128]{1,0:T(2,128)} %bitcast.10, s32[2,128]{1,0:T(2,128)} %bitcast.12), custom_call_target="tpu_custom_call" | custom-call | tf_op jit(solution)/shard_map/dispatch/pallas_call | solution.py:250
  2.0 0.5 collective-permute-start
  2.5 1.1 %collective-permute-done.refs_2_ = bf16[96,1280]{1,0:T(8,128)(2,1)S(1)} collective-permute-done((bf16[96,1280]{1,0:T(8,128)(2,1)S(1)}, bf16[96,1280]{1,0:T(8,128)(2,1)S(1)}, u32[]{:S(2)}, u32[]{:S(2)}) %collective-permute-start) | collective-permute-done | bytes 245792 | tf_op jit(solution)/shard_map/ppermute | solution.py:217
  3.7 3.0 %collective-permute-start.3 = (bf16[48,1280]{1,0:T(8,128)(2,1)S(1)}, bf16[48,1280]{1,0:T(8,128)(2,1)S(1)}, u32[]{:S(2)}, u32[]{:S(2)}) collective-permute-start(bf16[48,1280]{1,0:T(8,128)(2,1)S(1)} %pad_maximum_fusion.5), channel_id=1, source_target_pairs={{0,2},{1,3},{2,0},{3,1},{4,6},{5,7},{6,4},{7,5},{8,10},{9,11},{10,... | collective-permute-start | bytes 368648 | tf_op jit(solution)/shard_map/ppermute | solution.py:217
  6.7 2.7 %collective-permute-start.7 = (bf16[48,1280]{1,0:T(8,128)(2,1)S(1)}, bf16[48,1280]{1,0:T(8,128)(2,1)S(1)}, u32[]{:S(2)}, u32[]{:S(2)}) collective-permute-start(bf16[48,1280]{1,0:T(8,128)(2,1)S(1)} %pad_maximum_fusion.6), channel_id=1, source_target_pairs={{0,4},{1,5},{2,6},{3,7},{4,0},{5,1},{6,2},{7,3},{8,12},{9,13},{10,... | collective-permute-start | bytes 368648 | tf_op jit(solution)/shard_map/ppermute | solution.py:217
  9.4 1.9 %load.1 = (bf16[640,1280]{1,0:T(8,128)(2,1)S(1)}, bf16[1280,640]{1,0:T(8,128)(2,1)S(1)}) custom-call(bf16[640,1280]{1,0:T(8,128)(2,1)} %bitcast.14, bf16[1280,640]{1,0:T(8,128)(2,1)} %bitcast.15, bf16[96,1280]{1,0:T(8,128)(2,1)S(1)} %collective-permute-done.refs_2_), custom_call_target="tpu_custom_call" | custom-call | bytes 65536 | tf_op jit(solution)/shard_map/load/pallas_call | solution.py:275
  11.3 1.6 %collective-permute-start.1 = (bf16[48,1280]{1,0:T(8,128)(2,1)S(1)}, bf16[48,1280]{1,0:T(8,128)(2,1)S(1)}, u32[]{:S(2)}, u32[]{:S(2)}) collective-permute-start(bf16[48,1280]{1,0:T(8,128)(2,1)S(1)} %join.1.refs_0_), channel_id=1, source_target_pairs={{0,8},{1,17},{2,10},{3,19},{4,12},{5,21},{6,14},{7,23},{8,0},{9,25... | collective-permute-start | bytes 368648 | tf_op jit(solution)/shard_map/ppermute | solution.py:225
  12.9 0.3 collective-permute-start.10
  13.2 0.0 collective-permute-done.3.refs_3_
  13.2 0.6 %collective-permute-start.4 = (bf16[48,1280]{1,0:T(8,128)(2,1)S(1)}, bf16[48,1280]{1,0:T(8,128)(2,1)S(1)}, u32[]{:S(2)}, u32[]{:S(2)}) collective-permute-start(bf16[48,1280]{1,0:T(8,128)(2,1)S(1)} %collective-permute-done.3.refs_3_), channel_id=1, source_target_pairs={{0,8},{1,17},{2,10},{3,19},{4,12},{5,21},{6,14},{7,23},{8,0},{9,25... | collective-permute-start | bytes 368648 | tf_op jit(solution)/shard_map/ppermute | solution.py:225
  13.8 2.5 %collective-permute-done.1.refs_1_ = bf16[48,1280]{1,0:T(8,128)(2,1)S(1)} collective-permute-done((bf16[48,1280]{1,0:T(8,128)(2,1)S(1)}, bf16[48,1280]{1,0:T(8,128)(2,1)S(1)}, u32[]{:S(2)}, u32[]{:S(2)}) %collective-permute-start.1) | collective-permute-done | bytes 122912 | tf_op jit(solution)/shard_map/ppermute | solution.py:225
  16.3 1.6 %collective-permute-start.2 = (bf16[96,1280]{1,0:T(8,128)(2,1)S(1)}, bf16[96,1280]{1,0:T(8,128)(2,1)S(1)}, u32[]{:S(2)}, u32[]{:S(2)}) collective-permute-start(bf16[96,1280]{1,0:T(8,128)(2,1)S(1)} %pad_maximum_fusion), channel_id=1, source_target_pairs={{0,16},{1,9},{2,18},{3,11},{4,20},{5,13},{6,22},{7,15},{8,24},{9,1... | collective-permute-start | bytes 737288 | tf_op jit(solution)/shard_map/ppermute | solution.py:225
  17.9 0.0 collective-permute-done.7.refs_0_
  17.9 1.5 %collective-permute-start.8 = (bf16[48,1280]{1,0:T(8,128)(2,1)S(1)}, bf16[48,1280]{1,0:T(8,128)(2,1)S(1)}, u32[]{:S(2)}, u32[]{:S(2)}) collective-permute-start(bf16[48,1280]{1,0:T(8,128)(2,1)S(1)} %collective-permute-done.7.refs_0_), channel_id=1, source_target_pairs={{0,8},{1,17},{2,10},{3,19},{4,12},{5,21},{6,14},{7,23},{8,0},{9,25... | collective-permute-start | bytes 368648 | tf_op jit(solution)/shard_map/ppermute | solution.py:225
  19.4 0.3 collective-permute-done.10.refs_3_
  19.7 1.2 %collective-permute-start.11 = (bf16[48,1280]{1,0:T(8,128)(2,1)S(1)}, bf16[48,1280]{1,0:T(8,128)(2,1)S(1)}, u32[]{:S(2)}, u32[]{:S(2)}) collective-permute-start(bf16[48,1280]{1,0:T(8,128)(2,1)S(1)} %collective-permute-done.10.refs_3_), channel_id=1, source_target_pairs={{0,8},{1,17},{2,10},{3,19},{4,12},{5,21},{6,14},{7,23},{8,0},{9,25... | collective-permute-start | bytes 368648 | tf_op jit(solution)/shard_map/ppermute | solution.py:225
  20.9 0.0 collective-permute-done.4.refs_4_
  20.9 0.9 %collective-permute-start.5 = (bf16[96,1280]{1,0:T(8,128)(2,1)S(1)}, bf16[96,1280]{1,0:T(8,128)(2,1)S(1)}, u32[]{:S(2)}, u32[]{:S(2)}) collective-permute-start(bf16[96,1280]{1,0:T(8,128)(2,1)S(1)} %pad_maximum_fusion.1), channel_id=1, source_target_pairs={{0,16},{1,9},{2,18},{3,11},{4,20},{5,13},{6,22},{7,15},{8,24},{9,1... | collective-permute-start | bytes 737288 | tf_op jit(solution)/shard_map/ppermute | solution.py:225
  21.9 2.2 %collective-permute-done.8.refs_1_ = bf16[48,1280]{1,0:T(8,128)(2,1)S(1)} collective-permute-done((bf16[48,1280]{1,0:T(8,128)(2,1)S(1)}, bf16[48,1280]{1,0:T(8,128)(2,1)S(1)}, u32[]{:S(2)}, u32[]{:S(2)}) %collective-permute-start.8) | collective-permute-done | bytes 122912 | tf_op jit(solution)/shard_map/ppermute | solution.py:225
  24.1 0.1 collective-permute-start.9
  24.2 2.5 %collective-permute-done.11.refs_4_ = bf16[48,1280]{1,0:T(8,128)(2,1)S(1)} collective-permute-done((bf16[48,1280]{1,0:T(8,128)(2,1)S(1)}, bf16[48,1280]{1,0:T(8,128)(2,1)S(1)}, u32[]{:S(2)}, u32[]{:S(2)}) %collective-permute-start.11) | collective-permute-done | bytes 122912 | tf_op jit(solution)/shard_map/ppermute | solution.py:225
  26.7 0.9 %collective-permute-start.12 = (bf16[96,1280]{1,0:T(8,128)(2,1)S(1)}, bf16[96,1280]{1,0:T(8,128)(2,1)S(1)}, u32[]{:S(2)}, u32[]{:S(2)}) collective-permute-start(bf16[96,1280]{1,0:T(8,128)(2,1)S(1)} %pad_maximum_fusion.3), channel_id=1, source_target_pairs={{0,16},{1,9},{2,18},{3,11},{4,20},{5,13},{6,22},{7,15},{8,24},{9,1... | collective-permute-start | bytes 737288 | tf_op jit(solution)/shard_map/ppermute | solution.py:225
  27.6 0.0 collective-permute-done.2.refs_2_
  27.6 0.0 collective-permute-done.5.refs_5_
  27.6 2.7 %chunk.2 = (bf16[192,640]{1,0:T(8,128)(2,1)S(1)}, bf16[96,640]{1,0:T(8,128)(2,1)S(1)}, bf16[96,640]{1,0:T(8,128)(2,1)S(1)}, bf16[384,1280]{1,0:T(8,128)(2,1)S(1)...) custom-call(bf16[48,1280]{1,0:T(8,128)(2,1)S(1)} %join.1.refs_0_, ...), custom_call_target="tpu_custom_call" | custom-call | flops 1887436800 | bytes 3276800 | tf_op jit(solution)/shard_map/chunk/pallas_call | solution.py:348
  30.4 1.3 %collective-permute-start.6 = (bf16[192,640]{1,0:T(8,128)(2,1)S(1)}, bf16[192,640]{1,0:T(8,128)(2,1)S(1)}, u32[]{:S(2)}, u32[]{:S(2)}) collective-permute-start(bf16[192,640]{1,0:T(8,128)(2,1)S(1)} %get-tuple-element.33), channel_id=1, source_target_pairs={{0,16},{1,9},{2,18},{3,11},{4,20},{5,13},{6,22},{7,15},{8,24},{9,1... | collective-permute-start | bytes 737288 | tf_op jit(solution)/shard_map/ppermute | solution.py:225
  31.6 0.0 collective-permute-done.9.refs_2_
  31.6 1.4 %collective-permute-done.12.refs_5_ = bf16[96,1280]{1,0:T(8,128)(2,1)S(1)} collective-permute-done((bf16[96,1280]{1,0:T(8,128)(2,1)S(1)}, bf16[96,1280]{1,0:T(8,128)(2,1)S(1)}, u32[]{:S(2)}, u32[]{:S(2)}) %collective-permute-start.12) | collective-permute-done | bytes 245792 | tf_op jit(solution)/shard_map/ppermute | solution.py:225
  33.0 2.7 %chunk.3 = (bf16[96,640]{1,0:T(8,128)(2,1)S(1)}, bf16[96,640]{1,0:T(8,128)(2,1)S(1)}, bf16[96,640]{1,0:T(8,128)(2,1)S(1)}, bf16[96,640]{1,0:T(8,128)(2,1)S(1)}, ...) custom-call(bf16[48,1280]{1,0:T(8,128)(2,1)S(1)} %collective-permute-done.7.refs_0_, ...), custom_call_target="tpu_custom_call" | custom-call | flops 1887436800 | bytes 3276800 | tf_op jit(solution)/shard_map/chunk/pallas_call | solution.py:348
  35.7 1.4 %collective-permute-start.13 = (bf16[96,640]{1,0:T(8,128)(2,1)S(1)}, bf16[96,640]{1,0:T(8,128)(2,1)S(1)}, u32[]{:S(2)}, u32[]{:S(2)}) collective-permute-start(bf16[96,640]{1,0:T(8,128)(2,1)S(1)} %get-tuple-element.35), channel_id=1, source_target_pairs={{0,24},{1,25},{2,26},{3,27},{4,28},{5,29},{6,30},{7,31},{8,16},{9,... | collective-permute-start | bytes 368648 | tf_op jit(solution)/shard_map/ppermute | solution.py:225
  37.0 1.6 %collective-permute-start.16 = (bf16[96,640]{1,0:T(8,128)(2,1)S(1)}, bf16[96,640]{1,0:T(8,128)(2,1)S(1)}, u32[]{:S(2)}, u32[]{:S(2)}) collective-permute-start(bf16[96,640]{1,0:T(8,128)(2,1)S(1)} %get-tuple-element.37), channel_id=1, source_target_pairs={{0,16},{1,9},{2,18},{3,11},{4,20},{5,13},{6,22},{7,15},{8,24},{9,1... | collective-permute-start | bytes 368648 | tf_op jit(solution)/shard_map/ppermute | solution.py:225
  38.6 0.6 %collective-permute-start.17 = (bf16[96,640]{1,0:T(8,128)(2,1)S(1)}, bf16[96,640]{1,0:T(8,128)(2,1)S(1)}, u32[]{:S(2)}, u32[]{:S(2)}) collective-permute-start(bf16[96,640]{1,0:T(8,128)(2,1)S(1)} %get-tuple-element.38), channel_id=1, source_target_pairs={{0,8},{1,17},{2,10},{3,19},{4,12},{5,21},{6,14},{7,23},{8,0},{9,25... | collective-permute-start | bytes 368648 | tf_op jit(solution)/shard_map/ppermute | solution.py:225
  39.2 2.7 %weight_in_grad.1 = (bf16[640,1280]{1,0:T(8,128)(2,1)}, bf16[16,128]{1,0:T(8,128)(2,1)S(1)}) custom-call(bf16[384,1280]{1,0:T(8,128)(2,1)S(1)} %get-tuple-element.39.refs_0_, bf16[384,1280]{1,0:T(8,128)(2,1)S(1)} %get-tuple-element.40.refs_1_, bf16[384,1280]{1,0:T(8,128)(2,1)S(1)} %get-tuple-element.43.refs_2_, ...), custom_call_target="tpu_custom_call" | custom-call | flops 12582912 | bytes 16384 | tf_op jit(solution)/shard_map/weight_in_grad/pallas_call | solution.py:295
  41.9 1.9 %weight_out_grad.2 = (bf16[1280,640]{1,0:T(8,128)(2,1)}, bf16[16,128]{1,0:T(8,128)(2,1)S(1)}) custom-call(bf16[384,1280]{1,0:T(8,128)(2,1)S(1)} %get-tuple-element.39.refs_0_, bf16[384,1280]{1,0:T(8,128)(2,1)S(1)} %get-tuple-element.40.refs_1_, bf16[384,1280]{1,0:T(8,128)(2,1)S(1)} %get-tuple-element.41.refs_2_, ...), custom_call_target="tpu_custom_call" | custom-call | flops 6291456 | bytes 8192 | tf_op jit(solution)/shard_map/weight_out_grad/pallas_call | solution.py:305
  43.8 0.0 collective-permute-done.13.refs_2_.refs_1_
  43.8 0.0 collective-permute-done.16.refs_2_
  43.8 0.0 collective-permute-done.17.refs_3_
  43.8 0.1 sum.3.refs_4_
  43.9 0.0 collective-permute-done.6
  44.0 1.5 %collective-permute-start.14 = (bf16[96,640]{1,0:T(8,128)(2,1)S(1)}, bf16[96,640]{1,0:T(8,128)(2,1)S(1)}, u32[]{:S(2)}, u32[]{:S(2)}) collective-permute-start(bf16[96,640]{1,0:T(8,128)(2,1)S(1)} %sum.2), channel_id=1, source_target_pairs={{0,8},{1,17},{2,10},{3,19},{4,12},{5,21},{6,14},{7,23},{8,0},{9,25... | collective-permute-start | bytes 368648 | tf_op jit(solution)/shard_map/ppermute | solution.py:225
  45.5 3.6 %collective-permute-start.19 = (bf16[48,640]{1,0:T(8,128)(2,1)S(1)}, bf16[48,640]{1,0:T(8,128)(2,1)S(1)}, u32[]{:S(2)}, u32[]{:S(2)}) collective-permute-start(bf16[48,640]{1,0:T(8,128)(2,1)S(1)} %get-tuple-element.61), channel_id=1, source_target_pairs={{0,6},{1,7},{2,4},{3,5},{4,2},{5,3},{6,0},{7,1},{8,14},{9,15},{10,... | collective-permute-start | bytes 184328 | tf_op jit(solution)/shard_map/ppermute | solution.py:217
  49.0 0.0 collective-permute-start.18
  49.0 0.0 collective-permute-done.14
  49.1 0.1 add_convert_fusion
  49.1 1.8 %collective-permute-start.15 = (bf16[48,640]{1,0:T(8,128)(2,1)S(1)}, bf16[48,640]{1,0:T(8,128)(2,1)S(1)}, u32[]{:S(2)}, u32[]{:S(2)}) collective-permute-start(bf16[48,640]{1,0:T(8,128)(2,1)S(1)} %get-tuple-element.63), channel_id=1, source_target_pairs={{0,2},{1,3},{2,0},{3,1},{4,6},{5,7},{6,4},{7,5},{8,10},{9,11},{10,... | collective-permute-start | bytes 184328 | tf_op jit(solution)/shard_map/ppermute | solution.py:217
  50.9 0.0 copy-start
  50.9 0.0 copy-start.1
  50.9 0.0 copy-start.2
  50.9 1.9 %weight_out_grad.3 = (bf16[1280,640]{1,0:T(8,128)(2,1)}, bf16[16,128]{1,0:T(8,128)(2,1)S(1)}) custom-call(bf16[384,1280]{1,0:T(8,128)(2,1)S(1)} %get-tuple-element.39.refs_0_, bf16[384,1280]{1,0:T(8,128)(2,1)S(1)} %get-tuple-element.40.refs_1_, bf16[384,1280]{1,0:T(8,128)(2,1)S(1)} %get-tuple-element.41.refs_2_, ...), custom_call_target="tpu_custom_call", output_to_operand_aliasing={{0}: (5, {})} | custom-call | flops 6291456 | bytes 8192 | tf_op jit(solution)/shard_map/weight_out_grad/pallas_call | solution.py:305
  52.8 0.0 collective-permute-done.19.refs_3_
  52.8 1.4 %collective-permute-done.18.refs_2_ = bf16[48,640]{1,0:T(8,128)(2,1)S(1)} collective-permute-done((bf16[48,640]{1,0:T(8,128)(2,1)S(1)}, bf16[48,640]{1,0:T(8,128)(2,1)S(1)}, u32[]{:S(2)}, u32[]{:S(2)}) %collective-permute-start.18) | collective-permute-done | bytes 61472 | tf_op jit(solution)/shard_map/ppermute | solution.py:217
  54.2 0.0 collective-permute-done.15.refs_1_
  54.2 0.1 collective-permute-start.20
  54.3 1.3 %collective-permute-done.20.other_ref = bf16[96,640]{1,0:T(8,128)(2,1)S(1)} collective-permute-done((bf16[96,640]{1,0:T(8,128)(2,1)S(1)}, bf16[96,640]{1,0:T(8,128)(2,1)S(1)}, u32[]{:S(2)}, u32[]{:S(2)}) %collective-permute-start.20) | collective-permute-done | bytes 122912 | tf_op jit(solution)/shard_map/ppermute | solution.py:217
  55.6 0.0 copy-done
  55.6 0.0 copy-done.1
  55.6 0.0 copy-done.2
  55.6 1.0 %combine.1 = bf16[128,640]{1,0:T(8,128)(2,1)} custom-call(bf16[96,640]{1,0:T(8,128)(2,1)S(1)} %get-tuple-element.49.own_ref, bf16[96,640]{1,0:T(8,128)(2,1)S(1)} %collective-permute-done.20.other_ref, s32[2,128]{1,0:T(2,128)S(1)} %bitcast.9, s32[2,128]{1,0:T(2,128)S(1)} %bitcast.11, s32[2,128]{1,0:T(2,128)S(1)} %bitcast.13), custom_call_target="tpu_custom_call" | custom-call | tf_op jit(solution)/shard_map/combine/pallas_call | solution.py:415
  (16 shorter events, 0.2 us)
Async XLA Ops:
  2.0 1.7 %collective-permute-start = (bf16[96,1280]{1,0:T(8,128)(2,1)S(1)}, bf16[96,1280]{1,0:T(8,128)(2,1)S(1)}, u32[]{:S(2)}, u32[]{:S(2)}) collective-permute-start(bf16[96,1280]{1,0:T(8,128)(2,1)S(1)} %get-tuple-element.29), channel_id=1, source_target_pairs={{0,1},{1,0},{2,3},{3,2},{4,5},{5,4},{6,7},{7,6},{8,9},{9,8},{10,11... | collective-permute-start | bytes 737288 | tf_op jit(solution)/shard_map/ppermute | solution.py:217
  3.7 9.5 %collective-permute-start.3 = (bf16[48,1280]{1,0:T(8,128)(2,1)S(1)}, bf16[48,1280]{1,0:T(8,128)(2,1)S(1)}, u32[]{:S(2)}, u32[]{:S(2)}) collective-permute-start(bf16[48,1280]{1,0:T(8,128)(2,1)S(1)} %pad_maximum_fusion.5), channel_id=1, source_target_pairs={{0,2},{1,3},{2,0},{3,1},{4,6},{5,7},{6,4},{7,5},{8,10},{9,11},{10,... | collective-permute-start | bytes 368648 | tf_op jit(solution)/shard_map/ppermute | solution.py:217
  6.7 11.2 %collective-permute-start.7 = (bf16[48,1280]{1,0:T(8,128)(2,1)S(1)}, bf16[48,1280]{1,0:T(8,128)(2,1)S(1)}, u32[]{:S(2)}, u32[]{:S(2)}) collective-permute-start(bf16[48,1280]{1,0:T(8,128)(2,1)S(1)} %pad_maximum_fusion.6), channel_id=1, source_target_pairs={{0,4},{1,5},{2,6},{3,7},{4,0},{5,1},{6,2},{7,3},{8,12},{9,13},{10,... | collective-permute-start | bytes 368648 | tf_op jit(solution)/shard_map/ppermute | solution.py:217
  11.3 4.9 %collective-permute-start.1 = (bf16[48,1280]{1,0:T(8,128)(2,1)S(1)}, bf16[48,1280]{1,0:T(8,128)(2,1)S(1)}, u32[]{:S(2)}, u32[]{:S(2)}) collective-permute-start(bf16[48,1280]{1,0:T(8,128)(2,1)S(1)} %join.1.refs_0_), channel_id=1, source_target_pairs={{0,8},{1,17},{2,10},{3,19},{4,12},{5,21},{6,14},{7,23},{8,0},{9,25... | collective-permute-start | bytes 368648 | tf_op jit(solution)/shard_map/ppermute | solution.py:225
  12.9 6.8 %collective-permute-start.10 = (bf16[48,1280]{1,0:T(8,128)(2,1)S(1)}, bf16[48,1280]{1,0:T(8,128)(2,1)S(1)}, u32[]{:S(2)}, u32[]{:S(2)}) collective-permute-start(bf16[48,1280]{1,0:T(8,128)(2,1)S(1)} %pad_maximum_fusion.7), channel_id=1, source_target_pairs={{0,6},{1,7},{2,4},{3,5},{4,2},{5,3},{6,0},{7,1},{8,14},{9,15},{10,... | collective-permute-start | bytes 368648 | tf_op jit(solution)/shard_map/ppermute | solution.py:217
  13.2 7.7 %collective-permute-start.4 = (bf16[48,1280]{1,0:T(8,128)(2,1)S(1)}, bf16[48,1280]{1,0:T(8,128)(2,1)S(1)}, u32[]{:S(2)}, u32[]{:S(2)}) collective-permute-start(bf16[48,1280]{1,0:T(8,128)(2,1)S(1)} %collective-permute-done.3.refs_3_), channel_id=1, source_target_pairs={{0,8},{1,17},{2,10},{3,19},{4,12},{5,21},{6,14},{7,23},{8,0},{9,25... | collective-permute-start | bytes 368648 | tf_op jit(solution)/shard_map/ppermute | solution.py:225
  16.3 11.3 %collective-permute-start.2 = (bf16[96,1280]{1,0:T(8,128)(2,1)S(1)}, bf16[96,1280]{1,0:T(8,128)(2,1)S(1)}, u32[]{:S(2)}, u32[]{:S(2)}) collective-permute-start(bf16[96,1280]{1,0:T(8,128)(2,1)S(1)} %pad_maximum_fusion), channel_id=1, source_target_pairs={{0,16},{1,9},{2,18},{3,11},{4,20},{5,13},{6,22},{7,15},{8,24},{9,1... | collective-permute-start | bytes 737288 | tf_op jit(solution)/shard_map/ppermute | solution.py:225
  17.9 6.2 %collective-permute-start.8 = (bf16[48,1280]{1,0:T(8,128)(2,1)S(1)}, bf16[48,1280]{1,0:T(8,128)(2,1)S(1)}, u32[]{:S(2)}, u32[]{:S(2)}) collective-permute-start(bf16[48,1280]{1,0:T(8,128)(2,1)S(1)} %collective-permute-done.7.refs_0_), channel_id=1, source_target_pairs={{0,8},{1,17},{2,10},{3,19},{4,12},{5,21},{6,14},{7,23},{8,0},{9,25... | collective-permute-start | bytes 368648 | tf_op jit(solution)/shard_map/ppermute | solution.py:225
  19.7 7.0 %collective-permute-start.11 = (bf16[48,1280]{1,0:T(8,128)(2,1)S(1)}, bf16[48,1280]{1,0:T(8,128)(2,1)S(1)}, u32[]{:S(2)}, u32[]{:S(2)}) collective-permute-start(bf16[48,1280]{1,0:T(8,128)(2,1)S(1)} %collective-permute-done.10.refs_3_), channel_id=1, source_target_pairs={{0,8},{1,17},{2,10},{3,19},{4,12},{5,21},{6,14},{7,23},{8,0},{9,25... | collective-permute-start | bytes 368648 | tf_op jit(solution)/shard_map/ppermute | solution.py:225
  20.9 6.7 %collective-permute-start.5 = (bf16[96,1280]{1,0:T(8,128)(2,1)S(1)}, bf16[96,1280]{1,0:T(8,128)(2,1)S(1)}, u32[]{:S(2)}, u32[]{:S(2)}) collective-permute-start(bf16[96,1280]{1,0:T(8,128)(2,1)S(1)} %pad_maximum_fusion.1), channel_id=1, source_target_pairs={{0,16},{1,9},{2,18},{3,11},{4,20},{5,13},{6,22},{7,15},{8,24},{9,1... | collective-permute-start | bytes 737288 | tf_op jit(solution)/shard_map/ppermute | solution.py:225
  24.1 7.5 %collective-permute-start.9 = (bf16[96,1280]{1,0:T(8,128)(2,1)S(1)}, bf16[96,1280]{1,0:T(8,128)(2,1)S(1)}, u32[]{:S(2)}, u32[]{:S(2)}) collective-permute-start(bf16[96,1280]{1,0:T(8,128)(2,1)S(1)} %pad_maximum_fusion.2), channel_id=1, source_target_pairs={{0,16},{1,9},{2,18},{3,11},{4,20},{5,13},{6,22},{7,15},{8,24},{9,1... | collective-permute-start | bytes 737288 | tf_op jit(solution)/shard_map/ppermute | solution.py:225
  26.7 6.3 %collective-permute-start.12 = (bf16[96,1280]{1,0:T(8,128)(2,1)S(1)}, bf16[96,1280]{1,0:T(8,128)(2,1)S(1)}, u32[]{:S(2)}, u32[]{:S(2)}) collective-permute-start(bf16[96,1280]{1,0:T(8,128)(2,1)S(1)} %pad_maximum_fusion.3), channel_id=1, source_target_pairs={{0,16},{1,9},{2,18},{3,11},{4,20},{5,13},{6,22},{7,15},{8,24},{9,1... | collective-permute-start | bytes 737288 | tf_op jit(solution)/shard_map/ppermute | solution.py:225
  30.4 13.5 %collective-permute-start.6 = (bf16[192,640]{1,0:T(8,128)(2,1)S(1)}, bf16[192,640]{1,0:T(8,128)(2,1)S(1)}, u32[]{:S(2)}, u32[]{:S(2)}) collective-permute-start(bf16[192,640]{1,0:T(8,128)(2,1)S(1)} %get-tuple-element.33), channel_id=1, source_target_pairs={{0,16},{1,9},{2,18},{3,11},{4,20},{5,13},{6,22},{7,15},{8,24},{9,1... | collective-permute-start | bytes 737288 | tf_op jit(solution)/shard_map/ppermute | solution.py:225
  35.7 8.1 %collective-permute-start.13 = (bf16[96,640]{1,0:T(8,128)(2,1)S(1)}, bf16[96,640]{1,0:T(8,128)(2,1)S(1)}, u32[]{:S(2)}, u32[]{:S(2)}) collective-permute-start(bf16[96,640]{1,0:T(8,128)(2,1)S(1)} %get-tuple-element.35), channel_id=1, source_target_pairs={{0,24},{1,25},{2,26},{3,27},{4,28},{5,29},{6,30},{7,31},{8,16},{9,... | collective-permute-start | bytes 368648 | tf_op jit(solution)/shard_map/ppermute | solution.py:225
  37.0 6.7 %collective-permute-start.16 = (bf16[96,640]{1,0:T(8,128)(2,1)S(1)}, bf16[96,640]{1,0:T(8,128)(2,1)S(1)}, u32[]{:S(2)}, u32[]{:S(2)}) collective-permute-start(bf16[96,640]{1,0:T(8,128)(2,1)S(1)} %get-tuple-element.37), channel_id=1, source_target_pairs={{0,16},{1,9},{2,18},{3,11},{4,20},{5,13},{6,22},{7,15},{8,24},{9,1... | collective-permute-start | bytes 368648 | tf_op jit(solution)/shard_map/ppermute | solution.py:225
  38.6 5.2 %collective-permute-start.17 = (bf16[96,640]{1,0:T(8,128)(2,1)S(1)}, bf16[96,640]{1,0:T(8,128)(2,1)S(1)}, u32[]{:S(2)}, u32[]{:S(2)}) collective-permute-start(bf16[96,640]{1,0:T(8,128)(2,1)S(1)} %get-tuple-element.38), channel_id=1, source_target_pairs={{0,8},{1,17},{2,10},{3,19},{4,12},{5,21},{6,14},{7,23},{8,0},{9,25... | collective-permute-start | bytes 368648 | tf_op jit(solution)/shard_map/ppermute | solution.py:225
  44.0 5.1 %collective-permute-start.14 = (bf16[96,640]{1,0:T(8,128)(2,1)S(1)}, bf16[96,640]{1,0:T(8,128)(2,1)S(1)}, u32[]{:S(2)}, u32[]{:S(2)}) collective-permute-start(bf16[96,640]{1,0:T(8,128)(2,1)S(1)} %sum.2), channel_id=1, source_target_pairs={{0,8},{1,17},{2,10},{3,19},{4,12},{5,21},{6,14},{7,23},{8,0},{9,25... | collective-permute-start | bytes 368648 | tf_op jit(solution)/shard_map/ppermute | solution.py:225
  45.5 7.3 %collective-permute-start.19 = (bf16[48,640]{1,0:T(8,128)(2,1)S(1)}, bf16[48,640]{1,0:T(8,128)(2,1)S(1)}, u32[]{:S(2)}, u32[]{:S(2)}) collective-permute-start(bf16[48,640]{1,0:T(8,128)(2,1)S(1)} %get-tuple-element.61), channel_id=1, source_target_pairs={{0,6},{1,7},{2,4},{3,5},{4,2},{5,3},{6,0},{7,1},{8,14},{9,15},{10,... | collective-permute-start | bytes 184328 | tf_op jit(solution)/shard_map/ppermute | solution.py:217
  49.0 5.1 %collective-permute-start.18 = (bf16[48,640]{1,0:T(8,128)(2,1)S(1)}, bf16[48,640]{1,0:T(8,128)(2,1)S(1)}, u32[]{:S(2)}, u32[]{:S(2)}) collective-permute-start(bf16[48,640]{1,0:T(8,128)(2,1)S(1)} %get-tuple-element.62), channel_id=1, source_target_pairs={{0,4},{1,5},{2,6},{3,7},{4,0},{5,1},{6,2},{7,3},{8,12},{9,13},{10,... | collective-permute-start | bytes 184328 | tf_op jit(solution)/shard_map/ppermute | solution.py:217
  49.1 5.0 %collective-permute-start.15 = (bf16[48,640]{1,0:T(8,128)(2,1)S(1)}, bf16[48,640]{1,0:T(8,128)(2,1)S(1)}, u32[]{:S(2)}, u32[]{:S(2)}) collective-permute-start(bf16[48,640]{1,0:T(8,128)(2,1)S(1)} %get-tuple-element.63), channel_id=1, source_target_pairs={{0,2},{1,3},{2,0},{3,1},{4,6},{5,7},{6,4},{7,5},{8,10},{9,11},{10,... | collective-permute-start | bytes 184328 | tf_op jit(solution)/shard_map/ppermute | solution.py:217
  50.9 4.7 %copy-start = (s32[128,2]{0,1:T(2,128)S(1)}, s32[128,2]{0,1:T(2,128)}, u32[]{:S(2)}) copy-start(s32[128,2]{0,1:T(2,128)} %param.11) | copy-start | bytes 3076
  50.9 4.7 %copy-start.1 = (s32[128,2]{0,1:T(2,128)S(1)}, s32[128,2]{0,1:T(2,128)}, u32[]{:S(2)}) copy-start(s32[128,2]{0,1:T(2,128)} %param.12) | copy-start | bytes 3076
  50.9 4.7 %copy-start.2 = (s32[128,2]{0,1:T(2,128)S(1)}, s32[128,2]{0,1:T(2,128)}, u32[]{:S(2)}) copy-start(s32[128,2]{0,1:T(2,128)} %param.13) | copy-start | bytes 3076
  54.2 1.4 %collective-permute-start.20 = (bf16[96,640]{1,0:T(8,128)(2,1)S(1)}, bf16[96,640]{1,0:T(8,128)(2,1)S(1)}, u32[]{:S(2)}, u32[]{:S(2)}) collective-permute-start(bf16[96,640]{1,0:T(8,128)(2,1)S(1)} %get-tuple-element.50), channel_id=1, source_target_pairs={{0,1},{1,0},{2,3},{3,2},{4,5},{5,4},{6,7},{7,6},{8,9},{9,8},{10,11... | collective-permute-start | bytes 368648 | tf_op jit(solution)/shard_map/ppermute | solution.py:217
